TPU v7x, 32 devices: a whole 2x2x4 slice. The times are simulated.
32 devices in a mesh: row: 4 (over z), col: 8 (over y, x, core).
Axes of the slice: x: 2, y: 2, z: 4, core: 2. Of those that a mesh axis runs over, the one named last changes fastest.
Arguments:
- gradient: bfloat16 [4096, 6144], P('row', 'col'), may hold values from -1.5 to 1.5
- left_stat: float32 [4096, 4096], P('col', 'row'), may hold values from -6 to 6
- left_basis: bfloat16 [4096, 4096], P('col', 'row'), may hold values from -0.09375 to 0.09375
- right_basis: bfloat16 [6144, 6144], P('row', 'col'), may hold values from -0.078125 to 0.078125
- first_moment: float32 [4096, 6144], P('row', 'col'), may hold values from -0.625 to 0.625
- second_moment: float32 [4096, 6144], P('row', 'col'), may hold values from 0.01 to 0.1
Outputs:
- left_next: float32 [4096, 4096], P('col', 'row')
- first_next: float32 [4096, 6144], P('row', 'col')
- second_next: float32 [4096, 6144], P('row', 'col')
- direction: bfloat16 [4096, 6144], P('row', 'col')
All inputs are finite; a program needn't handle non-finite values.
Results may differ from a plain program's by a relative error of at most 0.015.
Values may be sent and summed in bfloat16 or wider, within the bound.
No kernel may reach another device: no remote copies, remote signals or barrier semaphores. Data moves between devices by JAX's collectives and lax.ppermute only.
A program may use at most 128 MiB of HBM per device.

v0:
```python
import jax
import jax.numpy as jnp
from jax import lax
from jax.experimental import pallas as pl
from jax.experimental.pallas import tpu as pltpu
from jax.sharding import PartitionSpec as P

BF16 = jnp.bfloat16
F32 = jnp.float32
VMEM = 40 * 2**20
QUICK = pl.CostEstimate(flops=2**20, bytes_accessed=2**16, transcendentals=0)

PAIRS = [(0, 1), (1, 0), (2, 3), (3, 2)]
MIDDLE = [(1, 2), (2, 1)]
OUTWARD = [(1, 0), (2, 3)]
INWARD = [(0, 1), (3, 2)]
MIRROR = [(0, 3), (1, 2), (2, 1), (3, 0)]
RELAY = [(0, 2), (1, 0), (2, 3), (3, 1)]
RELAY_BACK = [(0, 1), (1, 3), (2, 0), (3, 2)]


def contract_last(first, second):
    return lax.dot_general(first, second, (((1,), (1,)), ((), ())), preferred_element_type=F32)


def contract_first(first, second):
    return lax.dot_general(first, second, (((0,), (0,)), ((), ())), preferred_element_type=F32)


def together(operands, *earlier):
    return lax.optimization_barrier(tuple(operands) + earlier)[: len(operands)]


def after(x, *earlier):
    return together([x], *earlier)[0]


def joined(keep_order, first, second):
    return jnp.where(keep_order, jnp.concatenate([first, second]), jnp.concatenate([second, first]))


def halves(keep_order, x):
    n = x.shape[0] // 2
    return jnp.where(keep_order, x[:n], x[n:]), jnp.where(keep_order, x[n:], x[:n])


class Line:
    def __init__(self, axis):
        self.axis = axis
        self.i = lax.axis_index(axis)
        self.even = self.i % 2 == 0
        self.lower = self.i < 2
        self.inner = (self.i == 1) | (self.i == 2)

    def send(self, x, pairs):
        return lax.ppermute(x, self.axis, pairs)

    def near(self, x, got):
        return joined(self.even, x, got)

    def whole(self, near, middle, out):
        return joined(self.lower, near, jnp.where(self.inner, middle, out))

    def placed(self, whole, piece, bits):
        return lax.dynamic_update_slice(whole, piece, ((self.i ^ bits) * piece.shape[0], 0))

    def block(self, x, bits):
        n = x.shape[0] // 4
        return lax.dynamic_slice_in_dim(x, (self.i ^ bits) * n, n, 0)

    def scatter_start(self, x):
        near, far = halves(self.lower, x)
        return near, far, self.send(far, INWARD)

    def scatter_end(self, near, through):
        got = self.send(through, MIDDLE)
        mine, other = halves(self.even, near.astype(F32) + got.astype(F32))
        got = self.send(other.astype(near.dtype), PAIRS)
        return (mine + got.astype(F32)).astype(near.dtype)

    def scatter_fast(self, x):
        relay = self.send(self.block(x, 2), RELAY_BACK)
        near = self.send(self.block(x, 1), PAIRS)
        mirror = add(self.block(x, 3), jnp.where(self.inner, relay, 0))
        mirror = self.send(mirror, MIRROR)
        total = self.block(x, 0).astype(F32) + near.astype(F32) + jnp.where(self.inner, 0, relay).astype(F32)
        return (total + mirror.astype(F32)).astype(x.dtype), relay


def add(first, second):
    return (first.astype(F32) + second.astype(F32)).astype(first.dtype)


def products_kernel(rows_ref, right_ref, out_ref):
    out_ref[...] = contract_last(rows_ref[...], right_ref[...]).astype(out_ref.dtype)


def products(rows, right, start, count):
    height, depth = rows.shape
    width = right.shape[0] // 8
    return pl.pallas_call(
        products_kernel,
        grid=(count,),
        in_specs=[
            pl.BlockSpec((height, depth), lambda b: (0, 0)),
            pl.BlockSpec((width, depth), lambda b: (start + b, 0)),
        ],
        out_specs=pl.BlockSpec((height, width), lambda b: (0, b)),
        out_shape=jax.ShapeDtypeStruct((height, count * width), rows.dtype),
        compiler_params=pltpu.CompilerParams(vmem_limit_bytes=VMEM),
        cost_estimate=QUICK,
    )(rows, right)


def scatter_columns(rows, right_rel, axis):
    def swap(x, bit):
        return lax.ppermute(x, axis, [(j, j ^ bit) for j in range(8)])

    width = right_rel.shape[0] // 8
    height = rows.shape[0] // 2
    low, high = slice(0, height // 2), slice(height // 2, height)

    def pair_sum(part):
        away = products(part, right_rel, 4, 4)
        got = swap(away, 1)
        return add(products(after(part, away), right_rel, 0, 4), got)

    def block(x, b, rows):
        return x[rows, b * width : (b + 1) * width]

    def first_sends(x):
        return [
            jnp.concatenate([block(x, 1, low), block(x, 3, low)], axis=1),
            jnp.concatenate([block(x, 2, high), block(x, 3, high)], axis=1),
        ]

    def second_sends(x, by_x, by_y):
        return [add(block(x, 2, low), by_x[:, width:]), add(block(x, 1, high), by_y[:, width:])]

    def sums(x, by_x, by_y, then_y, then_x):
        total = lambda a, b, c: a.astype(F32) + b[:, :width].astype(F32) + c.astype(F32)
        return [total(block(x, 0, low), by_x, then_y), total(block(x, 0, high), by_y, then_x)]

    sum0 = pair_sum(rows[:height])
    by_x0, by_y0 = together(first_sends(sum0))
    by_x0, by_y0 = swap(by_x0, 2), swap(by_y0, 4)
    sum1 = pair_sum(after(rows[height:], sum0))
    then_y0, then_x0, by_x1, by_y1 = together(second_sends(sum0, by_x0, by_y0) + first_sends(sum1))
    then_y0, then_x0 = swap(then_y0, 4), swap(then_x0, 2)
    by_x1, by_y1 = swap(by_x1, 2), swap(by_y1, 4)
    then_y1, then_x1 = together(second_sends(sum1, by_x1, by_y1))
    then_y1, then_x1 = swap(then_y1, 4), swap(then_x1, 2)
    kept = sums(sum0, by_x0, by_y0, then_y0, then_x0) + sums(sum1, by_x1, by_y1, then_y1, then_x1)
    return jnp.concatenate(kept).astype(rows.dtype)


def moments(rotated, first_moment, second_moment):
    first_next = 0.9 * first_moment + 0.1 * rotated
    second_next = 0.95 * second_moment + 0.05 * rotated * rotated
    scaled_first = first_next / (1.0 - 0.9**10)
    scaled_second = second_next / (1.0 - 0.95**10)
    normalized = (scaled_first / (jnp.sqrt(scaled_second) + 1e-08)).astype(BF16)
    return first_next, second_next, normalized


STEPS = 2


def part_kernel(place, left, near, middle, out, first, second, basis, *rest):
    first_out, second_out, back, total, normalized = rest[-5:]
    step = pl.program_id(0)

    @pl.when(step == 0)
    def _():
        total[...] = jnp.zeros_like(total)

    def accumulate(right):
        depth = left.shape[2]
        for b in range(left.shape[0]):
            total[...] += jnp.dot(left[b], right[b * depth : (b + 1) * depth, :], preferred_element_type=F32)

    @pl.when(step < STEPS)
    def _():
        accumulate(near)

    far = (step >= STEPS) & (step < 2 * STEPS)

    @pl.when(far & (place[2] == 1))
    def _():
        accumulate(middle)

    @pl.when(far & (place[2] == 0))
    def _():
        accumulate(out)

    @pl.when(step == 2 * STEPS - 1)
    def _():
        first_out[...], second_out[...], normalized[...] = moments(total[...], first[...], second[...])

    @pl.when(step >= 2 * STEPS)
    def _():
        back[...] = jnp.dot(basis[...], normalized[...], preferred_element_type=F32).astype(BF16)


def part(number, place, left_rotated, near, middle, out, first_moment, second_moment, left_cols, before):
    height, width = first_moment.shape
    size = near.shape[1]
    deep = near.shape[0] // STEPS
    tall = left_cols.shape[0] // 2
    near_step = lambda s: jnp.minimum(s, STEPS - 1)
    far_step = lambda s: jnp.clip(s - STEPS, 0, STEPS - 1)
    last_step = lambda s: jnp.maximum(s - 2 * STEPS, 0)

    def left_block(s, place):
        return jnp.where(s < STEPS, place[0] + near_step(s), place[1] + far_step(s)), 0, 0

    moment = pl.BlockSpec((height, size), lambda s, place: (0, number))
    before = list(before)
    return pl.pallas_call(
        part_kernel,
        grid_spec=pltpu.PrefetchScalarGridSpec(
            num_scalar_prefetch=1,
            grid=(2 * STEPS + 2,),
            in_specs=[
                pl.BlockSpec((4 // STEPS, height, width), left_block),
                pl.BlockSpec((deep, size), lambda s, place: (near_step(s), 0)),
                pl.BlockSpec((deep, size), lambda s, place: (far_step(s) * place[2], 0)),
                pl.BlockSpec((deep, size), lambda s, place: (far_step(s) * (1 - place[2]), 0)),
                moment,
                moment,
                pl.BlockSpec((tall, height), lambda s, place: (last_step(s), 0)),
            ]
            + [pl.BlockSpec(memory_space=pl.ANY)] * len(before),
            out_specs=[moment, moment, pl.BlockSpec((tall, size), lambda s, place: (last_step(s), 0))],
            scratch_shapes=[pltpu.VMEM((height, size), F32), pltpu.VMEM((height, size), BF16)],
        ),
        out_shape=[
            jax.ShapeDtypeStruct((height, width), F32),
            jax.ShapeDtypeStruct((height, width), F32),
            jax.ShapeDtypeStruct((left_cols.shape[0], size), BF16),
        ],
        input_output_aliases={8: 0, 9: 1} if before else {},
        compiler_params=pltpu.CompilerParams(vmem_limit_bytes=VMEM),
        cost_estimate=QUICK,
    )(place, left_rotated, near, middle, out, first_moment, second_moment, left_cols, *before)


def body_on_line(gradient, left_stat, left_basis, right_basis, first_moment, second_moment):
    line = Line("row")
    send = line.send
    height, width = gradient.shape
    cuts = [slice(p * width // 3, (p + 1) * width // 3) for p in range(3)]
    left_cols = lax.all_gather(left_basis, "col", axis=0, tiled=True)
    own0, own1, own2 = [right_basis[:, cut] for cut in cuts]

    mirror = send(gradient, MIRROR)
    pair = send(gradient, PAIRS)
    relay = send(after(jnp.where(line.inner, mirror, gradient), pair), RELAY)
    turn = lambda x, bits: contract_first(line.block(left_cols, bits), x)
    left_sum = turn(gradient, 0) + turn(pair, 1) + turn(mirror, 3)
    pair0 = send(after(own0, left_sum), PAIRS)

    near0, own1 = together([line.near(own0, pair0), own1])
    middle0 = send(near0, MIDDLE)
    pair1 = send(own1, PAIRS)
    near1 = line.near(own1, pair1)
    pair2 = send(after(own2, near1), PAIRS)

    left_part = (left_sum + turn(after(relay, near0), 2)).astype(BF16)
    left_rotated = lax.all_gather(left_part, "col")

    middle0, near1 = together([middle0, near1], left_part, pair2)
    out0 = send(middle0, OUTWARD)
    middle1 = send(near1, MIDDLE)
    columns = jnp.zeros((4 * height, width), BF16)
    for bits, piece in zip((0, 1, 3, 2), together([gradient, pair, mirror, relay], left_part)):
        columns = line.placed(columns, piece, bits)
    product_here = contract_last(columns, gradient).astype(BF16)
    left_rotated, product = together([left_rotated, product_here])
    product = lax.psum_scatter(product, "col", scatter_dimension=0, tiled=True).astype(F32)
    left_next = 0.95 * left_stat + 0.05 * product

    middle1, near2 = together([middle1, line.near(own2, pair2)], out0, product_here)
    out1 = send(middle1, OUTWARD)
    middle2 = send(near2, MIDDLE)

    steps = jnp.where(line.lower, jnp.array([0, STEPS]), jnp.array([STEPS, 0]))
    place = jnp.concatenate([steps, line.inner[None]]).astype(jnp.int32)

    def next_part(number, near, middle, out, before):
        *before, back = part(
            number, place, left_rotated, near, middle, out, first_moment, second_moment, left_cols, before
        )
        return before, back

    moments0, back0 = next_part(0, near0, middle0, after(out0, near2), ())
    back0, far0, sent0 = line.scatter_start(back0)
    out2 = send(after(middle2, out1, far0), OUTWARD)
    moments1, back1 = next_part(1, near1, middle1, after(out1, far0), moments0)
    back1, far1, sent1 = line.scatter_start(after(back1, sent0))
    through0 = add(far0, sent0)
    moments2, back2 = next_part(2, near2, middle2, after(out2, through0, far1), moments1)
    turned2, relayed = line.scatter_fast(after(back2, sent1))
    turned0 = line.scatter_end(back0, through0)
    turned1 = line.scatter_end(back1, add(far1, sent1))
    first_next, second_next = moments2

    near0, near1, near2, middle0, middle1, middle2, out0, out1, out2 = together(
        [near0, near1, near2, middle0, middle1, middle2, out0, out1, out2], relayed
    )
    right0 = line.whole(near0, middle0, out0)
    right1 = line.whole(near1, middle1, out1)
    right2 = line.whole(near2, middle2, out2)
    i = lax.axis_index("col")
    right_cols = after(jnp.concatenate([right0, right1, right2], axis=1), left_next)
    blocks = [lax.dynamic_slice_in_dim(right_cols, (i ^ r) * width, width, 0) for r in (0, 2, 4, 6, 1, 3, 5, 7)]
    turned = jnp.concatenate([turned0, turned1, turned2], axis=1)
    direction = scatter_columns(turned, jnp.concatenate(blocks), "col")
    return (left_next, first_next, second_next, direction)


def body(gradient, left_stat, left_basis, right_basis, first_moment, second_moment):
    columns = lax.all_gather(gradient, "row", axis=0, tiled=True)
    left_cols = lax.all_gather(left_basis, "col", axis=0, tiled=True)
    right_cols = lax.all_gather(right_basis, "row", axis=0, tiled=True)
    left_rotated = lax.all_gather(contract_first(left_cols, columns).astype(BF16), "col", axis=1, tiled=True)
    product = contract_last(columns, gradient).astype(BF16)
    product = lax.psum_scatter(product, "col", scatter_dimension=0, tiled=True).astype(F32)
    left_next = 0.95 * left_stat + 0.05 * product
    rotated = jnp.dot(left_rotated, right_cols, preferred_element_type=F32)
    first_next, second_next, normalized = moments(rotated, first_moment, second_moment)
    back = jnp.dot(left_cols, normalized, preferred_element_type=F32).astype(BF16)
    back = lax.psum_scatter(back, "row", scatter_dimension=0, tiled=True)
    direction = contract_last(back, right_cols).astype(BF16)
    direction = lax.psum_scatter(direction, "col", scatter_dimension=1, tiled=True)
    return (left_next, first_next, second_next, direction)


def solution(mesh):
    on_line = mesh.shape["row"] == 4 and mesh.shape["col"] == 8
    return jax.shard_map(
        body_on_line if on_line else body,
        mesh=mesh,
        in_specs=(
            P("row", "col"),
            P("col", "row"),
            P("col", "row"),
            P("row", "col"),
            P("row", "col"),
            P("row", "col"),
        ),
        out_specs=(P("col", "row"), P("row", "col"), P("row", "col"), P("row", "col")),
        check_vma=False,
    )
```

profile of v0, /device:TPU:0, one launch (start us, length us, event | category | flops | bytes accessed | tf_op | source)
XLA Modules:
  0.0 479.0 jit_solution(17483755325066591248)
XLA Ops:
  8.0 5.1 %collective-permute-start.1 = (bf16[1024,768]{1,0:T(8,128)(2,1)}, bf16[1024,768]{1,0:T(8,128)(2,1)S(1)}, u32[]{:S(2)}, u32[]{:S(2)}) collective-permute-start(bf16[1024,768]{1,0:T(8,128)(2,1)} %param.8), channel_id=1, source_target_pairs={{0,24},{8,16},{16,8},{24,0},{1,25},{9,17},{17,9},{25,1},{2,26},{10... | collective-permute-start | bytes 4718600 | tf_op jit(solution)/shard_map/ppermute | solution.py:56
  16.2 32.4 %collective-permute-done.1 = bf16[1024,768]{1,0:T(8,128)(2,1)S(1)} collective-permute-done((bf16[1024,768]{1,0:T(8,128)(2,1)}, bf16[1024,768]{1,0:T(8,128)(2,1)S(1)}, u32[]{:S(2)}, u32[]{:S(2)}) %collective-permute-start.1) | collective-permute-done | bytes 1572896 | tf_op jit(solution)/shard_map/ppermute | solution.py:56
  50.0 31.6 %collective-permute-done = bf16[1024,768]{1,0:T(8,128)(2,1)} collective-permute-done((bf16[1024,768]{1,0:T(8,128)(2,1)}, bf16[1024,768]{1,0:T(8,128)(2,1)}, u32[]{:S(2)}, u32[]{:S(2)}) %collective-permute-start) | collective-permute-done | bytes 1572896 | tf_op jit(solution)/shard_map/ppermute | solution.py:56
  93.8 41.2 %collective-permute-done.3 = bf16[1536,256]{1,0:T(8,128)(2,1)} collective-permute-done((bf16[1536,256]{1,0:T(8,128)(2,1)}, bf16[1536,256]{1,0:T(8,128)(2,1)}, u32[]{:S(2)}, u32[]{:S(2)}) %collective-permute-start.3) | collective-permute-done | bytes 786464 | tf_op jit(solution)/shard_map/ppermute | solution.py:56
  137.4 5.7 %add_convert_fusion.2 = bf16[1024,768]{1,0:T(8,128)(2,1)} fusion(f32[1024,768]{1,0:T(8,128)S(1)} %copy-done.22, bf16[1024,768]{1,0:T(8,128)(2,1)} %collective-permute-done.2, bf16[4096,1024]{1,0:T(8,128)(2,1)} %all-gather.4.cloned.1.call-done.basis, s32[]{:T(128)S(6)} %select_n.170), kind=kOutput, calls=%fused_computation.7 | convolution fusion | flops 1612185600 | bytes 8388612 | tf_op jit(solution)/shard_map/dot_general | solution.py:27
  146.1 16.0 %collective-permute-done.5 = bf16[1536,256]{1,0:T(8,128)(2,1)S(1)} collective-permute-done((bf16[1536,256]{1,0:T(8,128)(2,1)}, bf16[1536,256]{1,0:T(8,128)(2,1)S(1)}, u32[]{:S(2)}, u32[]{:S(2)}) %collective-permute-start.5) | collective-permute-done | bytes 786464 | tf_op jit(solution)/shard_map/ppermute | solution.py:56
  169.4 13.5 %collective-permute-done.6 = bf16[1536,256]{1,0:T(8,128)(2,1)S(1)} collective-permute-done((bf16[1536,256]{1,0:T(8,128)(2,1)S(1)}, bf16[1536,256]{1,0:T(8,128)(2,1)S(1)}, u32[]{:S(2)}, u32[]{:S(2)}) %collective-permute-start.6) | collective-permute-done | bytes 786464 | tf_op jit(solution)/shard_map/ppermute | solution.py:56
  187.0 9.1 %convolution_convert_fusion = bf16[4096,1024]{1,0:T(8,128)(2,1)} fusion(bf16[4096,768]{1,0:T(8,128)(2,1)S(1)} %constant_dynamic-update-slice_fusion, bf16[1024,768]{1,0:T(8,128)(2,1)S(1)} %copy-done.16), kind=kOutput, calls=%fused_computation.1 | convolution fusion | flops 6446645248 | bytes 16252928 | tf_op jit(solution)/shard_map/dot_general | solution.py:23
  196.1 18.5 %all-gather.6.cloned.1.call-done = bf16[8192,768]{1,0:T(8,128)(2,1)} async-done(((bf16[1024,768]{1,0:T(8,128)(2,1)}), bf16[8192,768]{1,0:T(8,128)(2,1)}) %all-gather.6.cloned.1.call-update) | async-done | bytes 12582928 | tf_op jit(solution)/shard_map/all_gather | solution.py:270
  229.0 16.9 %shard_map.111 = (f32[1024,768]{1,0:T(8,128)}, f32[1024,768]{1,0:T(8,128)}, bf16[4096,256]{1,0:T(8,128)(2,1)S(1)}) custom-call(s32[3]{0:T(128)S(1)} %pad_add_fusion.place, bf16[8,1024,768]{2,1,0:T(8,128)(2,1)} %bitcast.8, bf16[3072,256]{1,0:T(8,128)(2,1)S(1)} %copy-done.9, bf16[3072,256]{1,0:T(8,128)(2,1)} %collective-permute-done.4.middle, ...), custom_call_target="tpu_custom_call" | custom-call | flops 1048576 | bytes 65536 | tf_op jit(solution)/shard_map/pallas_call | solution.py:219
  246.0 5.5 %collective-permute-start.12 = (bf16[2048,256]{1,0:T(8,128)(2,1)S(1)}, bf16[2048,256]{1,0:T(8,128)(2,1)S(1)}, u32[]{:S(2)}, u32[]{:S(2)}) collective-permute-start(bf16[2048,256]{1,0:T(8,128)(2,1)S(1)} %broadcast_select_fusion.5), channel_id=1, source_target_pairs={{0,8},{24,16},{1,9},{25,17},{2,10},{26,18},{3,11},{27,19},{4,12},{... | collective-permute-start | bytes 3145736 | tf_op jit(solution)/shard_map/ppermute | solution.py:56
  251.6 5.0 %collective-permute-done.10.out = bf16[3072,256]{1,0:T(8,128)(2,1)S(1)} collective-permute-done((bf16[3072,256]{1,0:T(8,128)(2,1)}, bf16[3072,256]{1,0:T(8,128)(2,1)S(1)}, u32[]{:S(2)}, u32[]{:S(2)}) %collective-permute-start.10) | collective-permute-done | bytes 1572896 | tf_op jit(solution)/shard_map/ppermute | solution.py:56
  257.9 14.0 %collective-permute-done.12 = bf16[2048,256]{1,0:T(8,128)(2,1)S(1)} collective-permute-done((bf16[2048,256]{1,0:T(8,128)(2,1)S(1)}, bf16[2048,256]{1,0:T(8,128)(2,1)S(1)}, u32[]{:S(2)}, u32[]{:S(2)}) %collective-permute-start.12) | collective-permute-done | bytes 1048608 | tf_op jit(solution)/shard_map/ppermute | solution.py:56
  275.1 15.4 %shard_map.112 = (f32[1024,768]{1,0:T(8,128)}, f32[1024,768]{1,0:T(8,128)}, bf16[4096,256]{1,0:T(8,128)(2,1)S(1)}) custom-call(s32[3]{0:T(128)S(1)} %pad_add_fusion.place, bf16[8,1024,768]{2,1,0:T(8,128)(2,1)} %bitcast.9, bf16[3072,256]{1,0:T(8,128)(2,1)} %maximum_select_fusion.4.near, ...), custom_call_target="tpu_custom_call", output_to_operand_aliasing={{0}: (8, {}), {1}: (9, {})} | custom-call | flops 1048576 | bytes 65536 | tf_op jit(solution)/shard_map/pallas_call | solution.py:219
  293.0 6.8 %collective-permute-start.15 = (bf16[2048,256]{1,0:T(8,128)(2,1)}, bf16[2048,256]{1,0:T(8,128)(2,1)}, u32[]{:S(2)}, u32[]{:S(2)}) collective-permute-start(bf16[2048,256]{1,0:T(8,128)(2,1)} %broadcast_select_fusion.4), channel_id=1, source_target_pairs={{0,8},{24,16},{1,9},{25,17},{2,10},{26,18},{3,11},{27,19},{4,12},{... | collective-permute-start | bytes 3145736 | tf_op jit(solution)/shard_map/ppermute | solution.py:56
  303.0 15.5 %shard_map.113 = (f32[1024,768]{1,0:T(8,128)}, f32[1024,768]{1,0:T(8,128)}, bf16[4096,256]{1,0:T(8,128)(2,1)S(1)}) custom-call(s32[3]{0:T(128)S(1)} %pad_add_fusion.place, bf16[8,1024,768]{2,1,0:T(8,128)(2,1)} %bitcast.10, bf16[3072,256]{1,0:T(8,128)(2,1)S(1)} %copy-done.12, ...), custom_call_target="tpu_custom_call", output_to_operand_aliasing={{0}: (8, {}), {1}: (9, {})} | custom-call | flops 1048576 | bytes 65536 | tf_op jit(solution)/shard_map/pallas_call | solution.py:219
  325.1 26.7 %collective-permute-done.19 = bf16[1024,256]{1,0:T(8,128)(2,1)S(1)} collective-permute-done((bf16[1024,256]{1,0:T(8,128)(2,1)S(1)}, bf16[1024,256]{1,0:T(8,128)(2,1)S(1)}, u32[]{:S(2)}, u32[]{:S(2)}) %collective-permute-start.19) | collective-permute-done | bytes 524320 | tf_op jit(solution)/shard_map/ppermute | solution.py:56
  352.0 4.3 collective-permute-start.20
  364.3 4.3 pad_maximum_fusion
  371.8 7.0 %collective-permute-done.17 = bf16[1024,256]{1,0:T(8,128)(2,1)S(1)} collective-permute-done((bf16[1024,256]{1,0:T(8,128)(2,1)S(1)}, bf16[1024,256]{1,0:T(8,128)(2,1)S(1)}, u32[]{:S(2)}, u32[]{:S(2)}) %collective-permute-start.17) | collective-permute-done | bytes 524320 | tf_op jit(solution)/shard_map/ppermute | solution.py:56
  415.3 14.6 %collective-permute-done.22 = bf16[256,1536]{1,0:T(8,128)(2,1)S(1)} collective-permute-done((bf16[256,1536]{1,0:T(8,128)(2,1)S(1)}, bf16[256,1536]{1,0:T(8,128)(2,1)S(1)}, u32[]{:S(2)}, u32[]{:S(2)}) %collective-permute-start.22) | collective-permute-done | bytes 786464 | tf_op jit(solution)/shard_map/ppermute | solution.py:117
  438.6 16.4 %collective-permute-done.27 = bf16[256,1536]{1,0:T(8,128)(2,1)S(1)} collective-permute-done((bf16[256,1536]{1,0:T(8,128)(2,1)S(1)}, bf16[256,1536]{1,0:T(8,128)(2,1)S(1)}, u32[]{:S(2)}, u32[]{:S(2)}) %collective-permute-start.27) | collective-permute-done | bytes 786464 | tf_op jit(solution)/shard_map/ppermute | solution.py:117
  457.7 6.4 %collective-permute-done.25 = bf16[256,768]{1,0:T(8,128)(2,1)S(1)} collective-permute-done((bf16[256,768]{1,0:T(8,128)(2,1)S(1)}, bf16[256,768]{1,0:T(8,128)(2,1)S(1)}, u32[]{:S(2)}, u32[]{:S(2)}) %collective-permute-start.25) | collective-permute-done | bytes 393248 | tf_op jit(solution)/shard_map/ppermute | solution.py:117
  464.4 6.1 %collective-permute-done.29 = bf16[256,768]{1,0:T(8,128)(2,1)S(1)} collective-permute-done((bf16[256,768]{1,0:T(8,128)(2,1)S(1)}, bf16[256,768]{1,0:T(8,128)(2,1)S(1)}, u32[]{:S(2)}, u32[]{:S(2)}) %collective-permute-start.29) | collective-permute-done | bytes 393248 | tf_op jit(solution)/shard_map/ppermute | solution.py:117
  (160 shorter events, 126.2 us)
Async XLA Ops:
  7.2 76.4 %all-gather.4.cloned.1.call-start = ((), (), s32[]{:S(2)}) async-start(), calls=%async_computation.1 | async-start | bytes 9437184 | tf_op jit(solution)/shard_map/all_gather | solution.py:253
  7.9 206.7 %all-gather.6.cloned.1.call-start = ((), (), s32[]{:S(2)}) async-start(), calls=%async_computation.3 | async-start | bytes 14155776 | tf_op jit(solution)/shard_map/all_gather | solution.py:270
  8.0 40.6 %collective-permute-start.1 = (bf16[1024,768]{1,0:T(8,128)(2,1)}, bf16[1024,768]{1,0:T(8,128)(2,1)S(1)}, u32[]{:S(2)}, u32[]{:S(2)}) collective-permute-start(bf16[1024,768]{1,0:T(8,128)(2,1)} %param.8), channel_id=1, source_target_pairs={{0,24},{8,16},{16,8},{24,0},{1,25},{9,17},{17,9},{25,1},{2,26},{10... | collective-permute-start | bytes 4718600 | tf_op jit(solution)/shard_map/ppermute | solution.py:56
  13.1 68.5 %collective-permute-start = (bf16[1024,768]{1,0:T(8,128)(2,1)}, bf16[1024,768]{1,0:T(8,128)(2,1)}, u32[]{:S(2)}, u32[]{:S(2)}) collective-permute-start(bf16[1024,768]{1,0:T(8,128)(2,1)} %param.8), channel_id=1, source_target_pairs={{0,8},{8,0},{16,24},{24,16},{1,9},{9,1},{17,25},{25,17},{2,10},{10... | collective-permute-start | bytes 4718600 | tf_op jit(solution)/shard_map/ppermute | solution.py:56
  81.6 55.8 %collective-permute-start.2 = (bf16[1024,768]{1,0:T(8,128)(2,1)}, bf16[1024,768]{1,0:T(8,128)(2,1)}, u32[]{:S(2)}, u32[]{:S(2)}) collective-permute-start(bf16[1024,768]{1,0:T(8,128)(2,1)} %broadcast_select_fusion.3), channel_id=1, source_target_pairs={{0,16},{8,0},{16,24},{24,8},{1,17},{9,1},{17,25},{25,9},{2,18},{10... | collective-permute-start | bytes 4718600 | tf_op jit(solution)/shard_map/ppermute | solution.py:56
  93.8 41.3 %collective-permute-start.3 = (bf16[1536,256]{1,0:T(8,128)(2,1)}, bf16[1536,256]{1,0:T(8,128)(2,1)}, u32[]{:S(2)}, u32[]{:S(2)}) collective-permute-start(bf16[1536,256]{1,0:T(8,128)(2,1)} %get-tuple-element.57), channel_id=1, source_target_pairs={{0,8},{8,0},{16,24},{24,16},{1,9},{9,1},{17,25},{25,17},{2,10},{10... | collective-permute-start | bytes 2359304 | tf_op jit(solution)/shard_map/ppermute | solution.py:56
  143.1 236.1 %reduce-scatter.2.cloned.1.call-start = ((), (), s32[]{:S(2)}) async-start(), calls=%async_computation.2 | async-start | bytes 9437184 | tf_op jit(solution)/shard_map/reduce_scatter | solution.py:280
  144.3 38.6 %collective-permute-start.4 = (bf16[3072,256]{1,0:T(8,128)(2,1)S(1)}, bf16[3072,256]{1,0:T(8,128)(2,1)}, u32[]{:S(2)}, u32[]{:S(2)}) collective-permute-start(bf16[3072,256]{1,0:T(8,128)(2,1)S(1)} %maximum_select_fusion.3.near), channel_id=1, source_target_pairs={{8,16},{16,8},{9,17},{17,9},{10,18},{18,10},{11,19},{19,11},{12,20... | collective-permute-start | bytes 4718600 | tf_op jit(solution)/shard_map/ppermute | solution.py:56
  183.8 34.0 %collective-permute-start.7 = (bf16[3072,256]{1,0:T(8,128)(2,1)}, bf16[3072,256]{1,0:T(8,128)(2,1)}, u32[]{:S(2)}, u32[]{:S(2)}) collective-permute-start(bf16[3072,256]{1,0:T(8,128)(2,1)} %maximum_select_fusion.4.near), channel_id=1, source_target_pairs={{8,16},{16,8},{9,17},{17,9},{10,18},{18,10},{11,19},{19,11},{12,20... | collective-permute-start | bytes 4718600 | tf_op jit(solution)/shard_map/ppermute | solution.py:56
  185.6 36.0 %collective-permute-start.8 = (bf16[3072,256]{1,0:T(8,128)(2,1)}, bf16[3072,256]{1,0:T(8,128)(2,1)}, u32[]{:S(2)}, u32[]{:S(2)}) collective-permute-start(bf16[3072,256]{1,0:T(8,128)(2,1)} %collective-permute-done.4.middle), channel_id=1, source_target_pairs={{8,0},{16,24},{9,1},{17,25},{10,2},{18,26},{11,3},{19,27},{12,4},{... | collective-permute-start | bytes 4718600 | tf_op jit(solution)/shard_map/ppermute | solution.py:56
  221.6 35.0 %collective-permute-start.10 = (bf16[3072,256]{1,0:T(8,128)(2,1)}, bf16[3072,256]{1,0:T(8,128)(2,1)S(1)}, u32[]{:S(2)}, u32[]{:S(2)}) collective-permute-start(bf16[3072,256]{1,0:T(8,128)(2,1)} %collective-permute-done.7.middle), channel_id=1, source_target_pairs={{8,0},{16,24},{9,1},{17,25},{10,2},{18,26},{11,3},{19,27},{12,4},{... | collective-permute-start | bytes 4718600 | tf_op jit(solution)/shard_map/ppermute | solution.py:56
  222.9 33.7 %collective-permute-start.9 = (bf16[3072,256]{1,0:T(8,128)(2,1)S(1)}, bf16[3072,256]{1,0:T(8,128)(2,1)}, u32[]{:S(2)}, u32[]{:S(2)}) collective-permute-start(bf16[3072,256]{1,0:T(8,128)(2,1)S(1)} %maximum_select_fusion.5.near), channel_id=1, source_target_pairs={{8,16},{16,8},{9,17},{17,9},{10,18},{18,10},{11,19},{19,11},{12,20... | collective-permute-start | bytes 4718600 | tf_op jit(solution)/shard_map/ppermute | solution.py:56
  246.0 25.9 %collective-permute-start.12 = (bf16[2048,256]{1,0:T(8,128)(2,1)S(1)}, bf16[2048,256]{1,0:T(8,128)(2,1)S(1)}, u32[]{:S(2)}, u32[]{:S(2)}) collective-permute-start(bf16[2048,256]{1,0:T(8,128)(2,1)S(1)} %broadcast_select_fusion.5), channel_id=1, source_target_pairs={{0,8},{24,16},{1,9},{25,17},{2,10},{26,18},{3,11},{27,19},{4,12},{... | collective-permute-start | bytes 3145736 | tf_op jit(solution)/shard_map/ppermute | solution.py:56
  256.6 43.1 %collective-permute-start.11 = (bf16[3072,256]{1,0:T(8,128)(2,1)}, bf16[3072,256]{1,0:T(8,128)(2,1)}, u32[]{:S(2)}, u32[]{:S(2)}) collective-permute-start(bf16[3072,256]{1,0:T(8,128)(2,1)} %collective-permute-done.9.middle), channel_id=1, source_target_pairs={{8,0},{16,24},{9,1},{17,25},{10,2},{18,26},{11,3},{19,27},{12,4},{... | collective-permute-start | bytes 4718600 | tf_op jit(solution)/shard_map/ppermute | solution.py:56
  273.2 45.3 %collective-permute-start.13 = (bf16[2048,256]{1,0:T(8,128)(2,1)}, bf16[2048,256]{1,0:T(8,128)(2,1)}, u32[]{:S(2)}, u32[]{:S(2)}) collective-permute-start(bf16[2048,256]{1,0:T(8,128)(2,1)} %add_convert_fusion.4), channel_id=1, source_target_pairs={{8,16},{16,8},{9,17},{17,9},{10,18},{18,10},{11,19},{19,11},{12,20... | collective-permute-start | bytes 3145736 | tf_op jit(solution)/shard_map/ppermute | solution.py:56
  293.0 27.4 %collective-permute-start.15 = (bf16[2048,256]{1,0:T(8,128)(2,1)}, bf16[2048,256]{1,0:T(8,128)(2,1)}, u32[]{:S(2)}, u32[]{:S(2)}) collective-permute-start(bf16[2048,256]{1,0:T(8,128)(2,1)} %broadcast_select_fusion.4), channel_id=1, source_target_pairs={{0,8},{24,16},{1,9},{25,17},{2,10},{26,18},{3,11},{27,19},{4,12},{... | collective-permute-start | bytes 3145736 | tf_op jit(solution)/shard_map/ppermute | solution.py:56
  320.3 51.0 %collective-permute-start.14 = (bf16[1024,256]{1,0:T(8,128)(2,1)S(1)}, bf16[1024,256]{1,0:T(8,128)(2,1)S(1)}, u32[]{:S(2)}, u32[]{:S(2)}) collective-permute-start(bf16[1024,256]{1,0:T(8,128)(2,1)S(1)} %select_convert_fusion.1), channel_id=1, source_target_pairs={{0,8},{8,0},{16,24},{24,16},{1,9},{9,1},{17,25},{25,17},{2,10},{10... | collective-permute-start | bytes 1572872 | tf_op jit(solution)/shard_map/ppermute | solution.py:56
  320.4 51.0 %collective-permute-start.18 = (bf16[1024,256]{1,0:T(8,128)(2,1)S(1)}, bf16[1024,256]{1,0:T(8,128)(2,1)S(1)}, u32[]{:S(2)}, u32[]{:S(2)}) collective-permute-start(bf16[1024,256]{1,0:T(8,128)(2,1)S(1)} %get-tuple-element.123), channel_id=1, source_target_pairs={{0,8},{8,0},{16,24},{24,16},{1,9},{9,1},{17,25},{25,17},{2,10},{10... | collective-permute-start | bytes 1572872 | tf_op jit(solution)/shard_map/ppermute | solution.py:56
  322.5 29.3 %collective-permute-start.19 = (bf16[1024,256]{1,0:T(8,128)(2,1)S(1)}, bf16[1024,256]{1,0:T(8,128)(2,1)S(1)}, u32[]{:S(2)}, u32[]{:S(2)}) collective-permute-start(bf16[1024,256]{1,0:T(8,128)(2,1)S(1)} %get-tuple-element.124), channel_id=1, source_target_pairs={{0,8},{8,24},{16,0},{24,16},{1,9},{9,25},{17,1},{25,17},{2,10},{10... | collective-permute-start | bytes 1572872 | tf_op jit(solution)/shard_map/ppermute | solution.py:56
  324.2 44.4 %collective-permute-start.16 = (bf16[2048,256]{1,0:T(8,128)(2,1)S(1)}, bf16[2048,256]{1,0:T(8,128)(2,1)S(1)}, u32[]{:S(2)}, u32[]{:S(2)}) collective-permute-start(bf16[2048,256]{1,0:T(8,128)(2,1)S(1)} %add_convert_fusion.3), channel_id=1, source_target_pairs={{8,16},{16,8},{9,17},{17,9},{10,18},{18,10},{11,19},{19,11},{12,20... | collective-permute-start | bytes 3145736 | tf_op jit(solution)/shard_map/ppermute | solution.py:56
  409.6 21.6 %collective-permute-start.24 = (bf16[512,3072]{1,0:T(8,128)(2,1)S(1)}, bf16[512,3072]{1,0:T(8,128)(2,1)}, u32[]{:S(2)}, u32[]{:S(2)}) collective-permute-start(bf16[512,3072]{1,0:T(8,128)(2,1)S(1)} %shard_map.116), channel_id=1, source_target_pairs={{0,1},{1,0},{2,3},{3,2},{4,5},{5,4},{6,7},{7,6},{8,9},{9,8},{10,11... | collective-permute-start | bytes 9437192 | tf_op jit(solution)/shard_map/ppermute | solution.py:117
  434.5 20.5 %collective-permute-start.27 = (bf16[256,1536]{1,0:T(8,128)(2,1)S(1)}, bf16[256,1536]{1,0:T(8,128)(2,1)S(1)}, u32[]{:S(2)}, u32[]{:S(2)}) collective-permute-start(bf16[256,1536]{1,0:T(8,128)(2,1)S(1)} %pad_maximum_fusion.4), channel_id=1, source_target_pairs={{0,2},{1,3},{2,0},{3,1},{4,6},{5,7},{6,4},{7,5},{8,10},{9,11},{10,... | collective-permute-start | bytes 2359304 | tf_op jit(solution)/shard_map/ppermute | solution.py:117
  435.9 28.2 %collective-permute-start.25 = (bf16[256,768]{1,0:T(8,128)(2,1)S(1)}, bf16[256,768]{1,0:T(8,128)(2,1)S(1)}, u32[]{:S(2)}, u32[]{:S(2)}) collective-permute-start(bf16[256,768]{1,0:T(8,128)(2,1)S(1)} %get-tuple-element.102), channel_id=1, source_target_pairs={{0,4},{1,5},{2,6},{3,7},{4,0},{5,1},{6,2},{7,3},{8,12},{9,13},{10,... | collective-permute-start | bytes 1179656 | tf_op jit(solution)/shard_map/ppermute | solution.py:117
  437.2 26.9 %collective-permute-start.26 = (bf16[256,768]{1,0:T(8,128)(2,1)S(1)}, bf16[256,768]{1,0:T(8,128)(2,1)S(1)}, u32[]{:S(2)}, u32[]{:S(2)}) collective-permute-start(bf16[256,768]{1,0:T(8,128)(2,1)S(1)} %get-tuple-element.103), channel_id=1, source_target_pairs={{0,2},{1,3},{2,0},{3,1},{4,6},{5,7},{6,4},{7,5},{8,10},{9,11},{10,... | collective-permute-start | bytes 1179656 | tf_op jit(solution)/shard_map/ppermute | solution.py:117
  (33 other events, 513.6 us)
Sparse Core Ops, SparseCore 0:
  9.9 57.0 all-gather.3
  143.2 71.3 all-gather.5
  218.1 71.2 reduce-scatter.1
where the time goes:
time: 488 us; the launch traced here: 479 us
  waiting for transfers between devices  258 us (53%)
  Pallas kernels  61.6 us (13%)
  starting transfers between devices  49.9 us (10%)
  other arithmetic  40.8 us (8%)
  local copies, waits for them, and re-layouts  29.4 us (6%)
  matrix products  24.6 us (5%)
  between operations  14.7 us (3%)
    ppermute x21, waiting for transfers between devices, send(): return lax.ppermute(x, self.axis, pairs)  191 us
    pallas_call x3, Pallas kernels, part(): pl.pallas_call(part_kernel, grid_spec=pltpu.PrefetchScalarGridSpec(num_sc...  47.9 us
    ppermute x10, waiting for transfers between devices, swap(): return lax.ppermute(x, axis, [(j, j ^ bit) for j in range(8)])  47.5 us
    ppermute x21, starting transfers between devices, send(): return lax.ppermute(x, self.axis, pairs)  41.7 us
    unnamed x53, local copies, waits for them, and re-layouts  20.5 us
    all_gather x1, waiting for transfers between devices, body_on_line(): left_rotated = lax.all_gather(left_part, 'col')  18.5 us
    dot_general x4, matrix products, contract_first(): lax.dot_general(first, second, (((0,), (0,)), ((), ())), preferred_elemen...  15.5 us
    pallas_call x4, Pallas kernels, products(): pl.pallas_call(products_kernel, grid=(count,), in_specs=[pl.BlockSpec((he...  13.8 us
  transfers between devices with their start and end apart: 34, of which 18 were waited for; matrix products, arithmetic and copies ran while one was open for 12% of the time, Pallas kernels for 11%

commit v1 on v0

--- a/solution.py
+++ b/solution.py
@@ -68,62 +68,48 @@
         n = x.shape[0] // 4
         return lax.dynamic_slice_in_dim(x, (self.i ^ bits) * n, n, 0)
 
-    def scatter_start(self, x):
-        near, far = halves(self.lower, x)
-        return near, far, self.send(far, INWARD)
-
-    def scatter_end(self, near, through):
-        got = self.send(through, MIDDLE)
-        mine, other = halves(self.even, near.astype(F32) + got.astype(F32))
-        got = self.send(other.astype(near.dtype), PAIRS)
-        return (mine + got.astype(F32)).astype(near.dtype)
-
-    def scatter_fast(self, x):
-        relay = self.send(self.block(x, 2), RELAY_BACK)
-        near = self.send(self.block(x, 1), PAIRS)
-        mirror = add(self.block(x, 3), jnp.where(self.inner, relay, 0))
-        mirror = self.send(mirror, MIRROR)
-        total = self.block(x, 0).astype(F32) + near.astype(F32) + jnp.where(self.inner, 0, relay).astype(F32)
-        return (total + mirror.astype(F32)).astype(x.dtype), relay
-
 
 def add(first, second):
     return (first.astype(F32) + second.astype(F32)).astype(first.dtype)
 
 
-def products_kernel(rows_ref, right_ref, out_ref):
-    out_ref[...] = contract_last(rows_ref[...], right_ref[...]).astype(out_ref.dtype)
-
-
-def products(rows, right, start, count):
-    height, depth = rows.shape
-    width = right.shape[0] // 8
+def products_kernel(order, *refs):
+    parts = len(refs) // 2
+    total = sum(contract_last(rows[...], right[...]) for rows, right in zip(refs[:parts], refs[parts:]))
+    refs[-1][...] = total.astype(refs[-1].dtype)
+
+
+def products(rows, half, right, order, start):
+    height, depth = rows[0].shape[0] // 2, rows[0].shape[1]
+    width = right[0].shape[0] // 8
     return pl.pallas_call(
         products_kernel,
-        grid=(count,),
-        in_specs=[
-            pl.BlockSpec((height, depth), lambda b: (0, 0)),
-            pl.BlockSpec((width, depth), lambda b: (start + b, 0)),
-        ],
-        out_specs=pl.BlockSpec((height, width), lambda b: (0, b)),
-        out_shape=jax.ShapeDtypeStruct((height, count * width), rows.dtype),
+        grid_spec=pltpu.PrefetchScalarGridSpec(
+            num_scalar_prefetch=1,
+            grid=(4,),
+            in_specs=[pl.BlockSpec((height, depth), lambda b, order: (half, 0))] * len(rows)
+            + [pl.BlockSpec((width, depth), lambda b, order: (order[start + b], 0))] * len(right),
+            out_specs=pl.BlockSpec((height, width), lambda b, order: (0, b)),
+        ),
+        out_shape=jax.ShapeDtypeStruct((height, 4 * width), rows[0].dtype),
         compiler_params=pltpu.CompilerParams(vmem_limit_bytes=VMEM),
         cost_estimate=QUICK,
-    )(rows, right)
-
-
-def scatter_columns(rows, right_rel, axis):
+    )(order, *rows, *right)
+
+
+def scatter_columns(rows, right, axis):
     def swap(x, bit):
         return lax.ppermute(x, axis, [(j, j ^ bit) for j in range(8)])
 
-    width = right_rel.shape[0] // 8
-    height = rows.shape[0] // 2
+    order = lax.axis_index(axis) ^ jnp.array([0, 2, 4, 6, 1, 3, 5, 7], jnp.int32)
+    width = right[0].shape[0] // 8
+    height = rows[0].shape[0] // 2
     low, high = slice(0, height // 2), slice(height // 2, height)
 
-    def pair_sum(part):
-        away = products(part, right_rel, 4, 4)
+    def pair_sum(half, rows):
+        away = products(rows, half, right, order, 4)
         got = swap(away, 1)
-        return add(products(after(part, away), right_rel, 0, 4), got)
+        return add(products(together(rows, away), half, right, order, 0), got)
 
     def block(x, b, rows):
         return x[rows, b * width : (b + 1) * width]
@@ -141,17 +127,19 @@
         total = lambda a, b, c: a.astype(F32) + b[:, :width].astype(F32) + c.astype(F32)
         return [total(block(x, 0, low), by_x, then_y), total(block(x, 0, high), by_y, then_x)]
 
-    sum0 = pair_sum(rows[:height])
+    sum0 = pair_sum(0, rows)
     by_x0, by_y0 = together(first_sends(sum0))
     by_x0, by_y0 = swap(by_x0, 2), swap(by_y0, 4)
-    sum1 = pair_sum(after(rows[height:], sum0))
-    then_y0, then_x0, by_x1, by_y1 = together(second_sends(sum0, by_x0, by_y0) + first_sends(sum1))
+    sum1 = pair_sum(1, together(rows, sum0))
+    then_y0, then_x0, by_x1, by_y1 = together(
+        second_sends(sum0, *together([by_x0, by_y0], sum1)) + first_sends(sum1)
+    )
     then_y0, then_x0 = swap(then_y0, 4), swap(then_x0, 2)
     by_x1, by_y1 = swap(by_x1, 2), swap(by_y1, 4)
     then_y1, then_x1 = together(second_sends(sum1, by_x1, by_y1))
     then_y1, then_x1 = swap(then_y1, 4), swap(then_x1, 2)
     kept = sums(sum0, by_x0, by_y0, then_y0, then_x0) + sums(sum1, by_x1, by_y1, then_y1, then_x1)
-    return jnp.concatenate(kept).astype(rows.dtype)
+    return jnp.concatenate(kept).astype(sum0.dtype)
 
 
 def moments(rotated, first_moment, second_moment):
@@ -294,28 +282,36 @@
         return before, back
 
     moments0, back0 = next_part(0, near0, middle0, after(out0, near2), ())
-    back0, far0, sent0 = line.scatter_start(back0)
+    stay0, far0 = halves(line.lower, back0)
+    got0 = send(far0, INWARD)
     out2 = send(after(middle2, out1, far0), OUTWARD)
     moments1, back1 = next_part(1, near1, middle1, after(out1, far0), moments0)
-    back1, far1, sent1 = line.scatter_start(after(back1, sent0))
-    through0 = add(far0, sent0)
-    moments2, back2 = next_part(2, near2, middle2, after(out2, through0, far1), moments1)
-    turned2, relayed = line.scatter_fast(after(back2, sent1))
-    turned0 = line.scatter_end(back0, through0)
-    turned1 = line.scatter_end(back1, add(far1, sent1))
+    stay1, far1 = halves(line.lower, after(back1, got0))
+    got1 = send(far1, INWARD)
+    through0 = send(add(far0, after(got0, far1)), MIDDLE)
+    right0 = line.whole(near0, middle0, after(out0, far1))
+    right1 = line.whole(near1, middle1, after(out1, far1))
+    mine0, other0 = halves(line.even, stay0.astype(F32) + through0.astype(F32))
+    other0 = other0.astype(BF16)
+    through1 = add(far1, got1)
+    moments2, back2 = next_part(2, near2, middle2, after(out2, other0, through1, right0, right1), moments1)
+    other0 = send(other0, PAIRS)
+    turned0 = (mine0 + other0.astype(F32)).astype(BF16)
+    through1 = send(through1, MIDDLE)
+    mine1, other1 = halves(line.even, stay1.astype(F32) + through1.astype(F32))
+    turned1 = (mine1 + send(other1.astype(BF16), PAIRS).astype(F32)).astype(BF16)
     first_next, second_next = moments2
 
-    near0, near1, near2, middle0, middle1, middle2, out0, out1, out2 = together(
-        [near0, near1, near2, middle0, middle1, middle2, out0, out1, out2], relayed
-    )
-    right0 = line.whole(near0, middle0, out0)
-    right1 = line.whole(near1, middle1, out1)
-    right2 = line.whole(near2, middle2, out2)
-    i = lax.axis_index("col")
-    right_cols = after(jnp.concatenate([right0, right1, right2], axis=1), left_next)
-    blocks = [lax.dynamic_slice_in_dim(right_cols, (i ^ r) * width, width, 0) for r in (0, 2, 4, 6, 1, 3, 5, 7)]
-    turned = jnp.concatenate([turned0, turned1, turned2], axis=1)
-    direction = scatter_columns(turned, jnp.concatenate(blocks), "col")
+    relay = send(line.block(back2, 2), RELAY_BACK)
+    pair = send(line.block(back2, 1), PAIRS)
+    relay = after(relay, through1, other0)
+    mirror = send(add(line.block(back2, 3), jnp.where(line.inner, relay, 0)), MIRROR)
+    right2 = line.whole(near2, middle2, after(out2, relay))
+    mirror, pair = together([mirror, pair], right2, left_next)
+    turned2 = line.block(back2, 0).astype(F32) + jnp.where(line.inner, 0, relay).astype(F32)
+    turned2 = (turned2 + pair.astype(F32) + mirror.astype(F32)).astype(BF16)
+
+    direction = scatter_columns([turned0, turned1, turned2], [right0, right1, right2], "col")
     return (left_next, first_next, second_next, direction)
 
 

time: 488 us -> 527 us (1.080)
  waiting for transfers between devices: 258 us -> 292 us
  starting transfers between devices: 49.9 us -> 70.3 us
  local copies, waits for them, and re-layouts: 29.4 us -> 11.4 us
    all_gather x1, waiting for transfers between devices: 18.5 us -> 53.8 us  [body_on_line(): left_rotated = lax.all_gather(left_part, 'col')]
    ppermute x21, starting transfers between devices: 41.7 us -> 61.7 us  [send(): return lax.ppermute(x, self.axis, pairs)]
    unnamed x53 -> x44, local copies, waits for them, and re-layouts: 20.5 us -> 1.83 us
    convert_element_type x5, other arithmetic: 0.92 us -> 6.57 us  [the longest x1 2.69 us: body_on_line(): turned0 = (mine0 + other0.astype(F32)).astype(BF16)]
    select_n x6, other arithmetic: 12.2 us -> 17.5 us  [joined(): jnp.where(keep_order, jnp.concatenate([first, second]), jnp.concatenate([...]
  transfers between devices with their start and end apart: 34 -> 34, of which waited for: 18 -> 17; matrix products, arithmetic and copies ran while one was open for 12% -> 13% of each run, Pallas kernels for 11% -> 10%
where the time goes in v1:
time: 527 us; the launch traced here: 520 us
  waiting for transfers between devices  292 us (55%)
  starting transfers between devices  70.3 us (13%)
  Pallas kernels  62.2 us (12%)
  other arithmetic  45 us (9%)
  matrix products  24 us (5%)
  between operations  14.7 us (3%)
  local copies, waits for them, and re-layouts  11.4 us (2%)
    ppermute x21, waiting for transfers between devices, send(): return lax.ppermute(x, self.axis, pairs)  194 us
    ppermute x21, starting transfers between devices, send(): return lax.ppermute(x, self.axis, pairs)  61.7 us
    all_gather x1, waiting for transfers between devices, body_on_line(): left_rotated = lax.all_gather(left_part, 'col')  53.8 us
    pallas_call x3, Pallas kernels, part(): pl.pallas_call(part_kernel, grid_spec=pltpu.PrefetchScalarGridSpec(num_sc...  46.1 us
    ppermute x10, waiting for transfers between devices, swap(): return lax.ppermute(x, axis, [(j, j ^ bit) for j in range(8)])  43.8 us
    select_n x6, other arithmetic, joined(): jnp.where(keep_order, jnp.concatenate([first, second]), jnp.concatenate([...  17.5 us
    pallas_call x4, Pallas kernels, products(): pl.pallas_call(products_kernel, grid_spec=pltpu.PrefetchScalarGridSpec(nu...  16.1 us
    dot_general x4, matrix products, contract_first(): lax.dot_general(first, second, (((0,), (0,)), ((), ())), preferred_elemen...  15 us
  transfers between devices with their start and end apart: 34, of which 17 were waited for; matrix products, arithmetic and copies ran while one was open for 13% of the time, Pallas kernels for 10%

profile of v1, /device:TPU:0, one launch (start us, length us, event | category | flops | bytes accessed | tf_op | source)
XLA Modules:
  0.0 520.1 jit_solution(1060393529438579194)
XLA Ops:
  8.0 5.1 collective-permute-start.1
  16.1 32.4 %collective-permute-done.1 = bf16[1024,768]{1,0:T(8,128)(2,1)S(1)} collective-permute-done((bf16[1024,768]{1,0:T(8,128)(2,1)}, bf16[1024,768]{1,0:T(8,128)(2,1)S(1)}, u32[]{:S(2)}, u32[]{:S(2)}) %collective-permute-start.1) | collective-permute-done | bytes 1572896 | tf_op jit(solution)/shard_map/ppermute | solution.py:56
  49.9 31.7 %collective-permute-done = bf16[1024,768]{1,0:T(8,128)(2,1)} collective-permute-done((bf16[1024,768]{1,0:T(8,128)(2,1)}, bf16[1024,768]{1,0:T(8,128)(2,1)}, u32[]{:S(2)}, u32[]{:S(2)}) %collective-permute-start) | collective-permute-done | bytes 1572896 | tf_op jit(solution)/shard_map/ppermute | solution.py:56
  83.4 4.1 fusion.4
  93.8 41.2 %collective-permute-done.3 = bf16[1536,256]{1,0:T(8,128)(2,1)} collective-permute-done((bf16[1536,256]{1,0:T(8,128)(2,1)}, bf16[1536,256]{1,0:T(8,128)(2,1)}, u32[]{:S(2)}, u32[]{:S(2)}) %collective-permute-start.3) | collective-permute-done | bytes 786464 | tf_op jit(solution)/shard_map/ppermute | solution.py:56
  138.5 5.1 add_convert_fusion.2
  152.3 9.0 %convolution_convert_fusion = bf16[4096,1024]{1,0:T(8,128)(2,1)} fusion(bf16[4096,768]{1,0:T(8,128)(2,1)S(1)} %constant_dynamic-update-slice_fusion, bf16[1024,768]{1,0:T(8,128)(2,1)S(1)} %copy-done.18), kind=kOutput, calls=%fused_computation | convolution fusion | flops 6446645248 | bytes 16252928 | tf_op jit(solution)/shard_map/dot_general | solution.py:23
  161.4 53.8 %all-gather.6.cloned.1.call-done = bf16[8192,768]{1,0:T(8,128)(2,1)} async-done(((bf16[1024,768]{1,0:T(8,128)(2,1)}), bf16[8192,768]{1,0:T(8,128)(2,1)}) %all-gather.6.cloned.1.call-update) | async-done | bytes 12582928 | tf_op jit(solution)/shard_map/all_gather | solution.py:258
  220.2 18.5 %collective-permute-done.6 = bf16[1536,256]{1,0:T(8,128)(2,1)} collective-permute-done((bf16[1536,256]{1,0:T(8,128)(2,1)}, bf16[1536,256]{1,0:T(8,128)(2,1)}, u32[]{:S(2)}, u32[]{:S(2)}) %collective-permute-start.6) | collective-permute-done | bytes 786464 | tf_op jit(solution)/shard_map/ppermute | solution.py:56
  244.4 34.5 %collective-permute-done.8.out = bf16[3072,256]{1,0:T(8,128)(2,1)} collective-permute-done((bf16[3072,256]{1,0:T(8,128)(2,1)}, bf16[3072,256]{1,0:T(8,128)(2,1)}, u32[]{:S(2)}, u32[]{:S(2)}) %collective-permute-start.8) | collective-permute-done | bytes 1572896 | tf_op jit(solution)/shard_map/ppermute | solution.py:56
  281.1 15.9 %shard_map.120 = (f32[1024,768]{1,0:T(8,128)}, f32[1024,768]{1,0:T(8,128)}, bf16[4096,256]{1,0:T(8,128)(2,1)S(1)}) custom-call(s32[3]{0:T(128)S(1)} %pad_add_fusion.place, bf16[8,1024,768]{2,1,0:T(8,128)(2,1)} %bitcast.8, bf16[3072,256]{1,0:T(8,128)(2,1)} %maximum_select_fusion.3.near, bf16[3072,256]{1,0:T(8,128)(2,1)} %collective-permute-done.4.middle, ...), custom_call_target="tpu_custom_call" | custom-call | flops 1048576 | bytes 65536 | tf_op jit(solution)/shard_map/pallas_call | solution.py:207
  297.1 7.8 %collective-permute-start.12 = (bf16[2048,256]{1,0:T(8,128)(2,1)S(1)}, bf16[2048,256]{1,0:T(8,128)(2,1)S(1)}, u32[]{:S(2)}, u32[]{:S(2)}) collective-permute-start(bf16[2048,256]{1,0:T(8,128)(2,1)S(1)} %broadcast_select_fusion.5), channel_id=1, source_target_pairs={{0,8},{24,16},{1,9},{25,17},{2,10},{26,18},{3,11},{27,19},{4,12},{... | collective-permute-start | bytes 3145736 | tf_op jit(solution)/shard_map/ppermute | solution.py:56
  304.9 10.9 %collective-permute-done.10.out = bf16[3072,256]{1,0:T(8,128)(2,1)S(1)} collective-permute-done((bf16[3072,256]{1,0:T(8,128)(2,1)}, bf16[3072,256]{1,0:T(8,128)(2,1)S(1)}, u32[]{:S(2)}, u32[]{:S(2)}) %collective-permute-start.10) | collective-permute-done | bytes 1572896 | tf_op jit(solution)/shard_map/ppermute | solution.py:56
  317.3 15.3 %shard_map.121 = (f32[1024,768]{1,0:T(8,128)}, f32[1024,768]{1,0:T(8,128)}, bf16[4096,256]{1,0:T(8,128)(2,1)S(1)}) custom-call(s32[3]{0:T(128)S(1)} %pad_add_fusion.place, bf16[8,1024,768]{2,1,0:T(8,128)(2,1)} %bitcast.9, bf16[3072,256]{1,0:T(8,128)(2,1)} %maximum_select_fusion.4.near, ...), custom_call_target="tpu_custom_call", output_to_operand_aliasing={{0}: (8, {}), {1}: (9, {})} | custom-call | flops 1048576 | bytes 65536 | tf_op jit(solution)/shard_map/pallas_call | solution.py:207
  332.8 6.0 %collective-permute-start.14 = (bf16[2048,256]{1,0:T(8,128)(2,1)S(1)}, bf16[2048,256]{1,0:T(8,128)(2,1)S(1)}, u32[]{:S(2)}, u32[]{:S(2)}) collective-permute-start(bf16[2048,256]{1,0:T(8,128)(2,1)S(1)} %broadcast_select_fusion.4), channel_id=1, source_target_pairs={{0,8},{24,16},{1,9},{25,17},{2,10},{26,18},{3,11},{27,19},{4,12},{... | collective-permute-start | bytes 3145736 | tf_op jit(solution)/shard_map/ppermute | solution.py:56
  345.6 18.8 %collective-permute-start.15 = (bf16[1024,256]{1,0:T(8,128)(2,1)}, bf16[1024,256]{1,0:T(8,128)(2,1)}, u32[]{:S(2)}, u32[]{:S(2)}) collective-permute-start(bf16[1024,256]{1,0:T(8,128)(2,1)} %select_convert_fusion.1), channel_id=1, source_target_pairs={{0,8},{8,0},{16,24},{24,16},{1,9},{9,1},{17,25},{25,17},{2,10},{10... | collective-permute-start | bytes 1572872 | tf_op jit(solution)/shard_map/ppermute | solution.py:56
  371.2 14.8 %shard_map.122 = (f32[1024,768]{1,0:T(8,128)}, f32[1024,768]{1,0:T(8,128)}, bf16[4096,256]{1,0:T(8,128)(2,1)S(1)}) custom-call(s32[3]{0:T(128)S(1)} %pad_add_fusion.place, bf16[8,1024,768]{2,1,0:T(8,128)(2,1)} %bitcast.10, bf16[3072,256]{1,0:T(8,128)(2,1)S(1)} %maximum_select_fusion.5.near, ...), custom_call_target="tpu_custom_call", output_to_operand_aliasing={{0}: (8, {}), {1}: (9, {})} | custom-call | flops 1048576 | bytes 65536 | tf_op jit(solution)/shard_map/pallas_call | solution.py:207
  394.4 8.8 %collective-permute-done.18 = bf16[1024,256]{1,0:T(8,128)(2,1)} collective-permute-done((bf16[1024,256]{1,0:T(8,128)(2,1)}, bf16[1024,256]{1,0:T(8,128)(2,1)}, u32[]{:S(2)}, u32[]{:S(2)}) %collective-permute-start.18) | collective-permute-done | bytes 524320 | tf_op jit(solution)/shard_map/ppermute | solution.py:56
  413.2 14.0 %collective-permute-done.17 = bf16[1024,256]{1,0:T(8,128)(2,1)S(1)} collective-permute-done((bf16[1024,256]{1,0:T(8,128)(2,1)S(1)}, bf16[1024,256]{1,0:T(8,128)(2,1)S(1)}, u32[]{:S(2)}, u32[]{:S(2)}) %collective-permute-start.17) | collective-permute-done | bytes 524320 | tf_op jit(solution)/shard_map/ppermute | solution.py:56
  455.1 4.0 shard_map.126
  460.4 12.7 %collective-permute-done.22 = bf16[256,1536]{1,0:T(8,128)(2,1)S(1)} collective-permute-done((bf16[256,1536]{1,0:T(8,128)(2,1)}, bf16[256,1536]{1,0:T(8,128)(2,1)S(1)}, u32[]{:S(2)}, u32[]{:S(2)}) %collective-permute-start.22) | collective-permute-done | bytes 786464 | tf_op jit(solution)/shard_map/ppermute | solution.py:102
  479.7 16.4 %collective-permute-done.27 = bf16[256,1536]{1,0:T(8,128)(2,1)S(1)} collective-permute-done((bf16[256,1536]{1,0:T(8,128)(2,1)S(1)}, bf16[256,1536]{1,0:T(8,128)(2,1)S(1)}, u32[]{:S(2)}, u32[]{:S(2)}) %collective-permute-start.27) | collective-permute-done | bytes 786464 | tf_op jit(solution)/shard_map/ppermute | solution.py:102
  499.0 6.1 %collective-permute-done.25 = bf16[256,768]{1,0:T(8,128)(2,1)S(1)} collective-permute-done((bf16[256,768]{1,0:T(8,128)(2,1)S(1)}, bf16[256,768]{1,0:T(8,128)(2,1)S(1)}, u32[]{:S(2)}, u32[]{:S(2)}) %collective-permute-start.25) | collective-permute-done | bytes 393248 | tf_op jit(solution)/shard_map/ppermute | solution.py:102
  506.4 5.1 collective-permute-done.29
  (148 shorter events, 113.0 us)
Async XLA Ops:
  7.2 76.2 %all-gather.4.cloned.1.call-start = ((), (), s32[]{:S(2)}) async-start(), calls=%async_computation.1 | async-start | bytes 9437184 | tf_op jit(solution)/shard_map/all_gather | solution.py:241
  7.9 207.2 %all-gather.6.cloned.1.call-start = ((), (), s32[]{:S(2)}) async-start(), calls=%async_computation.3 | async-start | bytes 14155776 | tf_op jit(solution)/shard_map/all_gather | solution.py:258
  8.0 40.6 %collective-permute-start.1 = (bf16[1024,768]{1,0:T(8,128)(2,1)}, bf16[1024,768]{1,0:T(8,128)(2,1)S(1)}, u32[]{:S(2)}, u32[]{:S(2)}) collective-permute-start(bf16[1024,768]{1,0:T(8,128)(2,1)} %param.9), channel_id=1, source_target_pairs={{0,24},{8,16},{16,8},{24,0},{1,25},{9,17},{17,9},{25,1},{2,26},{10... | collective-permute-start | bytes 4718600 | tf_op jit(solution)/shard_map/ppermute | solution.py:56
  13.1 68.5 %collective-permute-start = (bf16[1024,768]{1,0:T(8,128)(2,1)}, bf16[1024,768]{1,0:T(8,128)(2,1)}, u32[]{:S(2)}, u32[]{:S(2)}) collective-permute-start(bf16[1024,768]{1,0:T(8,128)(2,1)} %param.9), channel_id=1, source_target_pairs={{0,8},{8,0},{16,24},{24,16},{1,9},{9,1},{17,25},{25,17},{2,10},{10... | collective-permute-start | bytes 4718600 | tf_op jit(solution)/shard_map/ppermute | solution.py:56
  81.6 56.9 %collective-permute-start.2 = (bf16[1024,768]{1,0:T(8,128)(2,1)}, bf16[1024,768]{1,0:T(8,128)(2,1)}, u32[]{:S(2)}, u32[]{:S(2)}) collective-permute-start(bf16[1024,768]{1,0:T(8,128)(2,1)} %broadcast_select_fusion.3), channel_id=1, source_target_pairs={{0,16},{8,0},{16,24},{24,8},{1,17},{9,1},{17,25},{25,9},{2,18},{10... | collective-permute-start | bytes 4718600 | tf_op jit(solution)/shard_map/ppermute | solution.py:56
  93.6 41.4 %collective-permute-start.3 = (bf16[1536,256]{1,0:T(8,128)(2,1)}, bf16[1536,256]{1,0:T(8,128)(2,1)}, u32[]{:S(2)}, u32[]{:S(2)}) collective-permute-start(bf16[1536,256]{1,0:T(8,128)(2,1)} %get-tuple-element.61), channel_id=1, source_target_pairs={{0,8},{8,0},{16,24},{24,16},{1,9},{9,1},{17,25},{25,17},{2,10},{10... | collective-permute-start | bytes 2359304 | tf_op jit(solution)/shard_map/ppermute | solution.py:56
  143.6 284.7 %reduce-scatter.2.cloned.1.call-start = ((), (), s32[]{:S(2)}) async-start(), calls=%async_computation.2 | async-start | bytes 9437184 | tf_op jit(solution)/shard_map/reduce_scatter | solution.py:268
  143.7 95.0 %collective-permute-start.4 = (bf16[3072,256]{1,0:T(8,128)(2,1)}, bf16[3072,256]{1,0:T(8,128)(2,1)}, u32[]{:S(2)}, u32[]{:S(2)}) collective-permute-start(bf16[3072,256]{1,0:T(8,128)(2,1)} %maximum_select_fusion.3.near), channel_id=1, source_target_pairs={{8,16},{16,8},{9,17},{17,9},{10,18},{18,10},{11,19},{19,11},{12,20... | collective-permute-start | bytes 4718600 | tf_op jit(solution)/shard_map/ppermute | solution.py:56
  145.6 69.5 %collective-permute-start.5 = (bf16[1536,256]{1,0:T(8,128)(2,1)}, bf16[1536,256]{1,0:T(8,128)(2,1)}, u32[]{:S(2)}, u32[]{:S(2)}) collective-permute-start(bf16[1536,256]{1,0:T(8,128)(2,1)} %get-tuple-element.70), channel_id=1, source_target_pairs={{0,8},{8,0},{16,24},{24,16},{1,9},{9,1},{17,25},{25,17},{2,10},{10... | collective-permute-start | bytes 2359304 | tf_op jit(solution)/shard_map/ppermute | solution.py:56
  240.5 38.4 %collective-permute-start.8 = (bf16[3072,256]{1,0:T(8,128)(2,1)}, bf16[3072,256]{1,0:T(8,128)(2,1)}, u32[]{:S(2)}, u32[]{:S(2)}) collective-permute-start(bf16[3072,256]{1,0:T(8,128)(2,1)} %collective-permute-done.4.middle), channel_id=1, source_target_pairs={{8,0},{16,24},{9,1},{17,25},{10,2},{18,26},{11,3},{19,27},{12,4},{... | collective-permute-start | bytes 4718600 | tf_op jit(solution)/shard_map/ppermute | solution.py:56
  278.9 36.9 %collective-permute-start.10 = (bf16[3072,256]{1,0:T(8,128)(2,1)}, bf16[3072,256]{1,0:T(8,128)(2,1)S(1)}, u32[]{:S(2)}, u32[]{:S(2)}) collective-permute-start(bf16[3072,256]{1,0:T(8,128)(2,1)} %collective-permute-done.7.middle), channel_id=1, source_target_pairs={{8,0},{16,24},{9,1},{17,25},{10,2},{18,26},{11,3},{19,27},{12,4},{... | collective-permute-start | bytes 4718600 | tf_op jit(solution)/shard_map/ppermute | solution.py:56
  280.2 35.6 %collective-permute-start.9 = (bf16[3072,256]{1,0:T(8,128)(2,1)S(1)}, bf16[3072,256]{1,0:T(8,128)(2,1)S(1)}, u32[]{:S(2)}, u32[]{:S(2)}) collective-permute-start(bf16[3072,256]{1,0:T(8,128)(2,1)S(1)} %maximum_select_fusion.5.near), channel_id=1, source_target_pairs={{8,16},{16,8},{9,17},{17,9},{10,18},{18,10},{11,19},{19,11},{12,20... | collective-permute-start | bytes 4718600 | tf_op jit(solution)/shard_map/ppermute | solution.py:56
  297.1 35.6 %collective-permute-start.12 = (bf16[2048,256]{1,0:T(8,128)(2,1)S(1)}, bf16[2048,256]{1,0:T(8,128)(2,1)S(1)}, u32[]{:S(2)}, u32[]{:S(2)}) collective-permute-start(bf16[2048,256]{1,0:T(8,128)(2,1)S(1)} %broadcast_select_fusion.5), channel_id=1, source_target_pairs={{0,8},{24,16},{1,9},{25,17},{2,10},{26,18},{3,11},{27,19},{4,12},{... | collective-permute-start | bytes 3145736 | tf_op jit(solution)/shard_map/ppermute | solution.py:56
  315.8 55.4 %collective-permute-start.11 = (bf16[3072,256]{1,0:T(8,128)(2,1)S(1)}, bf16[3072,256]{1,0:T(8,128)(2,1)S(1)}, u32[]{:S(2)}, u32[]{:S(2)}) collective-permute-start(bf16[3072,256]{1,0:T(8,128)(2,1)S(1)} %collective-permute-done.9.middle), channel_id=1, source_target_pairs={{8,0},{16,24},{9,1},{17,25},{10,2},{18,26},{11,3},{19,27},{12,4},{... | collective-permute-start | bytes 4718600 | tf_op jit(solution)/shard_map/ppermute | solution.py:56
  332.8 31.7 %collective-permute-start.14 = (bf16[2048,256]{1,0:T(8,128)(2,1)S(1)}, bf16[2048,256]{1,0:T(8,128)(2,1)S(1)}, u32[]{:S(2)}, u32[]{:S(2)}) collective-permute-start(bf16[2048,256]{1,0:T(8,128)(2,1)S(1)} %broadcast_select_fusion.4), channel_id=1, source_target_pairs={{0,8},{24,16},{1,9},{25,17},{2,10},{26,18},{3,11},{27,19},{4,12},{... | collective-permute-start | bytes 3145736 | tf_op jit(solution)/shard_map/ppermute | solution.py:56
  345.6 46.0 %collective-permute-start.15 = (bf16[1024,256]{1,0:T(8,128)(2,1)}, bf16[1024,256]{1,0:T(8,128)(2,1)}, u32[]{:S(2)}, u32[]{:S(2)}) collective-permute-start(bf16[1024,256]{1,0:T(8,128)(2,1)} %select_convert_fusion.1), channel_id=1, source_target_pairs={{0,8},{8,0},{16,24},{24,16},{1,9},{9,1},{17,25},{25,17},{2,10},{10... | collective-permute-start | bytes 1572872 | tf_op jit(solution)/shard_map/ppermute | solution.py:56
  365.9 37.3 %collective-permute-start.16 = (bf16[2048,256]{1,0:T(8,128)(2,1)}, bf16[2048,256]{1,0:T(8,128)(2,1)}, u32[]{:S(2)}, u32[]{:S(2)}) collective-permute-start(bf16[2048,256]{1,0:T(8,128)(2,1)} %add_convert_fusion.3), channel_id=1, source_target_pairs={{8,16},{16,8},{9,17},{17,9},{10,18},{18,10},{11,19},{19,11},{12,20... | collective-permute-start | bytes 3145736 | tf_op jit(solution)/shard_map/ppermute | solution.py:56
  390.5 41.7 %collective-permute-start.20 = (bf16[1024,256]{1,0:T(8,128)(2,1)}, bf16[1024,256]{1,0:T(8,128)(2,1)}, u32[]{:S(2)}, u32[]{:S(2)}) collective-permute-start(bf16[1024,256]{1,0:T(8,128)(2,1)} %get-tuple-element.131), channel_id=1, source_target_pairs={{0,8},{8,0},{16,24},{24,16},{1,9},{9,1},{17,25},{25,17},{2,10},{10... | collective-permute-start | bytes 1572872 | tf_op jit(solution)/shard_map/ppermute | solution.py:56
  404.9 22.4 %collective-permute-start.17 = (bf16[1024,256]{1,0:T(8,128)(2,1)S(1)}, bf16[1024,256]{1,0:T(8,128)(2,1)S(1)}, u32[]{:S(2)}, u32[]{:S(2)}) collective-permute-start(bf16[1024,256]{1,0:T(8,128)(2,1)S(1)} %select_convert_fusion), channel_id=1, source_target_pairs={{0,8},{8,0},{16,24},{24,16},{1,9},{9,1},{17,25},{25,17},{2,10},{10... | collective-permute-start | bytes 1572872 | tf_op jit(solution)/shard_map/ppermute | solution.py:56
  409.4 24.7 %collective-permute-start.19 = (bf16[1024,256]{1,0:T(8,128)(2,1)}, bf16[1024,256]{1,0:T(8,128)(2,1)}, u32[]{:S(2)}, u32[]{:S(2)}) collective-permute-start(bf16[1024,256]{1,0:T(8,128)(2,1)} %add_convert_fusion.6), channel_id=1, source_target_pairs={{0,24},{8,16},{16,8},{24,0},{1,25},{9,17},{17,9},{25,1},{2,26},{10... | collective-permute-start | bytes 1572872 | tf_op jit(solution)/shard_map/ppermute | solution.py:56
  475.6 20.5 %collective-permute-start.27 = (bf16[256,1536]{1,0:T(8,128)(2,1)S(1)}, bf16[256,1536]{1,0:T(8,128)(2,1)S(1)}, u32[]{:S(2)}, u32[]{:S(2)}) collective-permute-start(bf16[256,1536]{1,0:T(8,128)(2,1)S(1)} %pad_maximum_fusion.2), channel_id=1, source_target_pairs={{0,2},{1,3},{2,0},{3,1},{4,6},{5,7},{6,4},{7,5},{8,10},{9,11},{10,... | collective-permute-start | bytes 2359304 | tf_op jit(solution)/shard_map/ppermute | solution.py:102
  476.2 20.5 %collective-permute-start.28 = (bf16[256,1536]{1,0:T(8,128)(2,1)S(1)}, bf16[256,1536]{1,0:T(8,128)(2,1)S(1)}, u32[]{:S(2)}, u32[]{:S(2)}) collective-permute-start(bf16[256,1536]{1,0:T(8,128)(2,1)S(1)} %concatenate.74), channel_id=1, source_target_pairs={{0,4},{1,5},{2,6},{3,7},{4,0},{5,1},{6,2},{7,3},{8,12},{9,13},{10,... | collective-permute-start | bytes 2359304 | tf_op jit(solution)/shard_map/ppermute | solution.py:102
  477.2 28.0 %collective-permute-start.25 = (bf16[256,768]{1,0:T(8,128)(2,1)S(1)}, bf16[256,768]{1,0:T(8,128)(2,1)S(1)}, u32[]{:S(2)}, u32[]{:S(2)}) collective-permute-start(bf16[256,768]{1,0:T(8,128)(2,1)S(1)} %get-tuple-element.110), channel_id=1, source_target_pairs={{0,4},{1,5},{2,6},{3,7},{4,0},{5,1},{6,2},{7,3},{8,12},{9,13},{10,... | collective-permute-start | bytes 1179656 | tf_op jit(solution)/shard_map/ppermute | solution.py:102
  478.3 26.9 %collective-permute-start.26 = (bf16[256,768]{1,0:T(8,128)(2,1)S(1)}, bf16[256,768]{1,0:T(8,128)(2,1)S(1)}, u32[]{:S(2)}, u32[]{:S(2)}) collective-permute-start(bf16[256,768]{1,0:T(8,128)(2,1)S(1)} %get-tuple-element.111), channel_id=1, source_target_pairs={{0,2},{1,3},{2,0},{3,1},{4,6},{5,7},{6,4},{7,5},{8,10},{9,11},{10,... | collective-permute-start | bytes 1179656 | tf_op jit(solution)/shard_map/ppermute | solution.py:102
  (32 other events, 712.1 us)
Sparse Core Ops, SparseCore 0:
  9.9 57.0 all-gather.3
  143.7 71.3 all-gather.5
  218.6 71.2 reduce-scatter.1

commit v2 on v1

--- a/solution.py
+++ b/solution.py
@@ -264,8 +264,7 @@
     for bits, piece in zip((0, 1, 3, 2), together([gradient, pair, mirror, relay], left_part)):
         columns = line.placed(columns, piece, bits)
     product_here = contract_last(columns, gradient).astype(BF16)
-    left_rotated, product = together([left_rotated, product_here])
-    product = lax.psum_scatter(product, "col", scatter_dimension=0, tiled=True).astype(F32)
+    product = lax.psum_scatter(after(product_here, out0), "col", scatter_dimension=0, tiled=True).astype(F32)
     left_next = 0.95 * left_stat + 0.05 * product
 
     middle1, near2 = together([middle1, line.near(own2, pair2)], out0, product_here)
@@ -307,11 +306,12 @@
     relay = after(relay, through1, other0)
     mirror = send(add(line.block(back2, 3), jnp.where(line.inner, relay, 0)), MIRROR)
     right2 = line.whole(near2, middle2, after(out2, relay))
-    mirror, pair = together([mirror, pair], right2, left_next)
+    mirror, pair = together([mirror, pair], right2)
     turned2 = line.block(back2, 0).astype(F32) + jnp.where(line.inner, 0, relay).astype(F32)
     turned2 = (turned2 + pair.astype(F32) + mirror.astype(F32)).astype(BF16)
 
-    direction = scatter_columns([turned0, turned1, turned2], [right0, right1, right2], "col")
+    right = together([right0, right1, right2], left_next)
+    direction = scatter_columns([turned0, turned1, turned2], right, "col")
     return (left_next, first_next, second_next, direction)
 
 

time: 527 us -> 502 us (0.953)
  waiting for transfers between devices: 292 us -> 228 us
  starting transfers between devices: 70.3 us -> 96.8 us
  local copies, waits for them, and re-layouts: 11.4 us -> 28.2 us
  other arithmetic: 45 us -> 38.8 us
    all_gather x1, waiting for transfers between devices: 53.8 us -> 0.01 us  [body_on_line(): left_rotated = lax.all_gather(left_part, 'col')]
    ppermute x21, starting transfers between devices: 61.7 us -> 86.4 us  [send(): return lax.ppermute(x, self.axis, pairs)]
    unnamed x44 -> x74, local copies, waits for them, and re-layouts: 1.83 us -> 18.9 us
    ppermute x21, waiting for transfers between devices: 194 us -> 186 us  [send(): return lax.ppermute(x, self.axis, pairs)]
  transfers between devices with their start and end apart: 34 -> 34, of which waited for: 17 -> 17; matrix products, arithmetic and copies ran while one was open for 13% -> 13% of each run, Pallas kernels for 10% -> 11%
where the time goes in v2:
time: 502 us; the launch traced here: 493 us
  waiting for transfers between devices  228 us (45%)
  starting transfers between devices  96.8 us (19%)
  Pallas kernels  61.9 us (12%)
  other arithmetic  38.8 us (8%)
  local copies, waits for them, and re-layouts  28.2 us (6%)
  matrix products  24.6 us (5%)
  between operations  14.7 us (3%)
    ppermute x21, waiting for transfers between devices, send(): return lax.ppermute(x, self.axis, pairs)  186 us
    ppermute x21, starting transfers between devices, send(): return lax.ppermute(x, self.axis, pairs)  86.4 us
    pallas_call x3, Pallas kernels, part(): pl.pallas_call(part_kernel, grid_spec=pltpu.PrefetchScalarGridSpec(num_sc...  45.8 us
    ppermute x10, waiting for transfers between devices, swap(): return lax.ppermute(x, axis, [(j, j ^ bit) for j in range(8)])  42.1 us
    unnamed x74, local copies, waits for them, and re-layouts  18.9 us
    pallas_call x4, Pallas kernels, products(): pl.pallas_call(products_kernel, grid_spec=pltpu.PrefetchScalarGridSpec(nu...  16.1 us
    dot_general x4, matrix products, contract_first(): lax.dot_general(first, second, (((0,), (0,)), ((), ())), preferred_elemen...  15.5 us
    select_n x6, other arithmetic, joined(): jnp.where(keep_order, jnp.concatenate([first, second]), jnp.concatenate([...  13.6 us
  transfers between devices with their start and end apart: 34, of which 17 were waited for; matrix products, arithmetic and copies ran while one was open for 13% of the time, Pallas kernels for 11%

profile of v2, /device:TPU:0, one launch (start us, length us, event | category | flops | bytes accessed | tf_op | source)
XLA Modules:
  0.0 493.4 jit_solution(3546928117067949388)
XLA Ops:
  8.0 5.1 %collective-permute-start.1 = (bf16[1024,768]{1,0:T(8,128)(2,1)}, bf16[1024,768]{1,0:T(8,128)(2,1)S(1)}, u32[]{:S(2)}, u32[]{:S(2)}) collective-permute-start(bf16[1024,768]{1,0:T(8,128)(2,1)} %param.9), channel_id=1, source_target_pairs={{0,24},{8,16},{16,8},{24,0},{1,25},{9,17},{17,9},{25,1},{2,26},{10... | collective-permute-start | bytes 4718600 | tf_op jit(solution)/shard_map/ppermute | solution.py:56
  16.2 32.4 %collective-permute-done.1 = bf16[1024,768]{1,0:T(8,128)(2,1)S(1)} collective-permute-done((bf16[1024,768]{1,0:T(8,128)(2,1)}, bf16[1024,768]{1,0:T(8,128)(2,1)S(1)}, u32[]{:S(2)}, u32[]{:S(2)}) %collective-permute-start.1) | collective-permute-done | bytes 1572896 | tf_op jit(solution)/shard_map/ppermute | solution.py:56
  50.0 31.6 %collective-permute-done = bf16[1024,768]{1,0:T(8,128)(2,1)} collective-permute-done((bf16[1024,768]{1,0:T(8,128)(2,1)}, bf16[1024,768]{1,0:T(8,128)(2,1)}, u32[]{:S(2)}, u32[]{:S(2)}) %collective-permute-start) | collective-permute-done | bytes 1572896 | tf_op jit(solution)/shard_map/ppermute | solution.py:56
  83.5 4.1 fusion.4
  93.9 41.1 %collective-permute-done.3 = bf16[1536,256]{1,0:T(8,128)(2,1)S(1)} collective-permute-done((bf16[1536,256]{1,0:T(8,128)(2,1)S(1)}, bf16[1536,256]{1,0:T(8,128)(2,1)S(1)}, u32[]{:S(2)}, u32[]{:S(2)}) %collective-permute-start.3) | collective-permute-done | bytes 786464 | tf_op jit(solution)/shard_map/ppermute | solution.py:56
  136.7 5.7 %add_convert_fusion.2 = bf16[1024,768]{1,0:T(8,128)(2,1)} fusion(f32[1024,768]{1,0:T(8,128)S(1)} %copy-done.36, bf16[1024,768]{1,0:T(8,128)(2,1)} %collective-permute-done.2, bf16[4096,1024]{1,0:T(8,128)(2,1)} %all-gather.4.cloned.1.call-done.basis, s32[]{:T(128)S(6)} %select_n.148), kind=kOutput, calls=%fused_computation.6 | convolution fusion | flops 1612185600 | bytes 8388612 | tf_op jit(solution)/shard_map/dot_general | solution.py:27
  144.3 17.1 %collective-permute-done.5 = bf16[1536,256]{1,0:T(8,128)(2,1)S(1)} collective-permute-done((bf16[1536,256]{1,0:T(8,128)(2,1)}, bf16[1536,256]{1,0:T(8,128)(2,1)S(1)}, u32[]{:S(2)}, u32[]{:S(2)}) %collective-permute-start.5) | collective-permute-done | bytes 786464 | tf_op jit(solution)/shard_map/ppermute | solution.py:56
  169.5 13.0 %collective-permute-done.6 = bf16[1536,256]{1,0:T(8,128)(2,1)S(1)} collective-permute-done((bf16[1536,256]{1,0:T(8,128)(2,1)}, bf16[1536,256]{1,0:T(8,128)(2,1)S(1)}, u32[]{:S(2)}, u32[]{:S(2)}) %collective-permute-start.6) | collective-permute-done | bytes 786464 | tf_op jit(solution)/shard_map/ppermute | solution.py:56
  184.9 9.0 %convolution_convert_fusion = bf16[4096,1024]{1,0:T(8,128)(2,1)} fusion(bf16[4096,768]{1,0:T(8,128)(2,1)S(1)} %constant_dynamic-update-slice_fusion, bf16[1024,768]{1,0:T(8,128)(2,1)S(1)} %copy-done.28), kind=kOutput, calls=%fused_computation | convolution fusion | flops 6446645248 | bytes 16252928 | tf_op jit(solution)/shard_map/dot_general | solution.py:23
  193.9 25.2 %collective-permute-done.7.out = bf16[3072,256]{1,0:T(8,128)(2,1)S(1)} collective-permute-done((bf16[3072,256]{1,0:T(8,128)(2,1)S(1)}, bf16[3072,256]{1,0:T(8,128)(2,1)S(1)}, u32[]{:S(2)}, u32[]{:S(2)}) %collective-permute-start.7) | collective-permute-done | bytes 1572896 | tf_op jit(solution)/shard_map/ppermute | solution.py:56
  236.2 15.0 %shard_map.120 = (f32[1024,768]{1,0:T(8,128)}, f32[1024,768]{1,0:T(8,128)}, bf16[4096,256]{1,0:T(8,128)(2,1)S(1)}) custom-call(s32[3]{0:T(128)S(1)} %pad_add_fusion.place, bf16[8,1024,768]{2,1,0:T(8,128)(2,1)} %bitcast.8, bf16[3072,256]{1,0:T(8,128)(2,1)S(1)} %copy-done.11, bf16[3072,256]{1,0:T(8,128)(2,1)S(1)} %copy-done.15, ...), custom_call_target="tpu_custom_call" | custom-call | flops 1048576 | bytes 65536 | tf_op jit(solution)/shard_map/pallas_call | solution.py:207
  253.6 33.3 %collective-permute-start.12 = (bf16[2048,256]{1,0:T(8,128)(2,1)}, bf16[2048,256]{1,0:T(8,128)(2,1)}, u32[]{:S(2)}, u32[]{:S(2)}) collective-permute-start(bf16[2048,256]{1,0:T(8,128)(2,1)} %broadcast_select_fusion.5), channel_id=1, source_target_pairs={{0,8},{24,16},{1,9},{25,17},{2,10},{26,18},{3,11},{27,19},{4,12},{... | collective-permute-start | bytes 3145736 | tf_op jit(solution)/shard_map/ppermute | solution.py:56
  292.0 15.5 %shard_map.121 = (f32[1024,768]{1,0:T(8,128)}, f32[1024,768]{1,0:T(8,128)}, bf16[4096,256]{1,0:T(8,128)(2,1)S(1)}) custom-call(s32[3]{0:T(128)S(1)} %pad_add_fusion.place, bf16[8,1024,768]{2,1,0:T(8,128)(2,1)} %bitcast.9, bf16[3072,256]{1,0:T(8,128)(2,1)S(1)} %copy-done.13, ...), custom_call_target="tpu_custom_call", output_to_operand_aliasing={{0}: (8, {}), {1}: (9, {})} | custom-call | flops 1048576 | bytes 65536 | tf_op jit(solution)/shard_map/pallas_call | solution.py:207
  307.6 7.1 %collective-permute-start.14 = (bf16[2048,256]{1,0:T(8,128)(2,1)S(1)}, bf16[2048,256]{1,0:T(8,128)(2,1)S(1)}, u32[]{:S(2)}, u32[]{:S(2)}) collective-permute-start(bf16[2048,256]{1,0:T(8,128)(2,1)S(1)} %broadcast_select_fusion.4), channel_id=1, source_target_pairs={{0,8},{24,16},{1,9},{25,17},{2,10},{26,18},{3,11},{27,19},{4,12},{... | collective-permute-start | bytes 3145736 | tf_op jit(solution)/shard_map/ppermute | solution.py:56
  321.2 18.2 %collective-permute-start.15 = (bf16[1024,256]{1,0:T(8,128)(2,1)}, bf16[1024,256]{1,0:T(8,128)(2,1)}, u32[]{:S(2)}, u32[]{:S(2)}) collective-permute-start(bf16[1024,256]{1,0:T(8,128)(2,1)} %select_convert_fusion.1), channel_id=1, source_target_pairs={{0,8},{8,0},{16,24},{24,16},{1,9},{9,1},{17,25},{25,17},{2,10},{10... | collective-permute-start | bytes 1572872 | tf_op jit(solution)/shard_map/ppermute | solution.py:56
  347.0 15.3 %shard_map.122 = (f32[1024,768]{1,0:T(8,128)}, f32[1024,768]{1,0:T(8,128)}, bf16[4096,256]{1,0:T(8,128)(2,1)S(1)}) custom-call(s32[3]{0:T(128)S(1)} %pad_add_fusion.place, bf16[8,1024,768]{2,1,0:T(8,128)(2,1)} %bitcast.10, bf16[3072,256]{1,0:T(8,128)(2,1)} %maximum_select_fusion.5.near, ...), custom_call_target="tpu_custom_call", output_to_operand_aliasing={{0}: (8, {}), {1}: (9, {})} | custom-call | flops 1048576 | bytes 65536 | tf_op jit(solution)/shard_map/pallas_call | solution.py:207
  372.4 6.6 %collective-permute-done.18 = bf16[1024,256]{1,0:T(8,128)(2,1)} collective-permute-done((bf16[1024,256]{1,0:T(8,128)(2,1)}, bf16[1024,256]{1,0:T(8,128)(2,1)}, u32[]{:S(2)}, u32[]{:S(2)}) %collective-permute-start.18) | collective-permute-done | bytes 524320 | tf_op jit(solution)/shard_map/ppermute | solution.py:56
  390.1 17.6 %collective-permute-done.19 = bf16[1024,256]{1,0:T(8,128)(2,1)S(1)} collective-permute-done((bf16[1024,256]{1,0:T(8,128)(2,1)S(1)}, bf16[1024,256]{1,0:T(8,128)(2,1)S(1)}, u32[]{:S(2)}, u32[]{:S(2)}) %collective-permute-start.19) | collective-permute-done | bytes 524320 | tf_op jit(solution)/shard_map/ppermute | solution.py:56
  409.2 4.0 shard_map.123
  413.4 4.0 shard_map.124
  434.5 11.8 %collective-permute-done.22 = bf16[256,1536]{1,0:T(8,128)(2,1)S(1)} collective-permute-done((bf16[256,1536]{1,0:T(8,128)(2,1)}, bf16[256,1536]{1,0:T(8,128)(2,1)S(1)}, u32[]{:S(2)}, u32[]{:S(2)}) %collective-permute-start.22) | collective-permute-done | bytes 786464 | tf_op jit(solution)/shard_map/ppermute | solution.py:102
  453.1 16.4 %collective-permute-done.27 = bf16[256,1536]{1,0:T(8,128)(2,1)S(1)} collective-permute-done((bf16[256,1536]{1,0:T(8,128)(2,1)S(1)}, bf16[256,1536]{1,0:T(8,128)(2,1)S(1)}, u32[]{:S(2)}, u32[]{:S(2)}) %collective-permute-start.27) | collective-permute-done | bytes 786464 | tf_op jit(solution)/shard_map/ppermute | solution.py:102
  473.2 5.2 %collective-permute-done.25 = bf16[256,768]{1,0:T(8,128)(2,1)S(1)} collective-permute-done((bf16[256,768]{1,0:T(8,128)(2,1)S(1)}, bf16[256,768]{1,0:T(8,128)(2,1)S(1)}, u32[]{:S(2)}, u32[]{:S(2)}) %collective-permute-start.25) | collective-permute-done | bytes 393248 | tf_op jit(solution)/shard_map/ppermute | solution.py:102
  479.7 5.1 %collective-permute-done.29 = bf16[256,768]{1,0:T(8,128)(2,1)S(1)} collective-permute-done((bf16[256,768]{1,0:T(8,128)(2,1)S(1)}, bf16[256,768]{1,0:T(8,128)(2,1)S(1)}, u32[]{:S(2)}, u32[]{:S(2)}) %collective-permute-start.29) | collective-permute-done | bytes 393248 | tf_op jit(solution)/shard_map/ppermute | solution.py:102
  (178 shorter events, 119.3 us)
Async XLA Ops:
  7.2 76.4 %all-gather.4.cloned.1.call-start = ((), (), s32[]{:S(2)}) async-start(), calls=%async_computation.1 | async-start | bytes 9437184 | tf_op jit(solution)/shard_map/all_gather | solution.py:241
  7.9 221.0 %all-gather.6.cloned.1.call-start = ((), (), s32[]{:S(2)}) async-start(), calls=%async_computation.3 | async-start | bytes 14155776 | tf_op jit(solution)/shard_map/all_gather | solution.py:258
  8.0 40.6 %collective-permute-start.1 = (bf16[1024,768]{1,0:T(8,128)(2,1)}, bf16[1024,768]{1,0:T(8,128)(2,1)S(1)}, u32[]{:S(2)}, u32[]{:S(2)}) collective-permute-start(bf16[1024,768]{1,0:T(8,128)(2,1)} %param.9), channel_id=1, source_target_pairs={{0,24},{8,16},{16,8},{24,0},{1,25},{9,17},{17,9},{25,1},{2,26},{10... | collective-permute-start | bytes 4718600 | tf_op jit(solution)/shard_map/ppermute | solution.py:56
  13.1 68.5 %collective-permute-start = (bf16[1024,768]{1,0:T(8,128)(2,1)}, bf16[1024,768]{1,0:T(8,128)(2,1)}, u32[]{:S(2)}, u32[]{:S(2)}) collective-permute-start(bf16[1024,768]{1,0:T(8,128)(2,1)} %param.9), channel_id=1, source_target_pairs={{0,8},{8,0},{16,24},{24,16},{1,9},{9,1},{17,25},{25,17},{2,10},{10... | collective-permute-start | bytes 4718600 | tf_op jit(solution)/shard_map/ppermute | solution.py:56
  81.6 55.1 %collective-permute-start.2 = (bf16[1024,768]{1,0:T(8,128)(2,1)}, bf16[1024,768]{1,0:T(8,128)(2,1)}, u32[]{:S(2)}, u32[]{:S(2)}) collective-permute-start(bf16[1024,768]{1,0:T(8,128)(2,1)} %broadcast_select_fusion.3), channel_id=1, source_target_pairs={{0,16},{8,0},{16,24},{24,8},{1,17},{9,1},{17,25},{25,9},{2,18},{10... | collective-permute-start | bytes 4718600 | tf_op jit(solution)/shard_map/ppermute | solution.py:56
  93.8 41.2 %collective-permute-start.3 = (bf16[1536,256]{1,0:T(8,128)(2,1)S(1)}, bf16[1536,256]{1,0:T(8,128)(2,1)S(1)}, u32[]{:S(2)}, u32[]{:S(2)}) collective-permute-start(bf16[1536,256]{1,0:T(8,128)(2,1)S(1)} %copy-done.31), channel_id=1, source_target_pairs={{0,8},{8,0},{16,24},{24,16},{1,9},{9,1},{17,25},{25,17},{2,10},{10... | collective-permute-start | bytes 2359304 | tf_op jit(solution)/shard_map/ppermute | solution.py:56
  142.5 223.8 %reduce-scatter.2.cloned.1.call-start = ((), (), s32[]{:S(2)}) async-start(), calls=%async_computation.2 | async-start | bytes 9437184 | tf_op jit(solution)/shard_map/reduce_scatter | solution.py:267
  143.6 39.0 %collective-permute-start.4 = (bf16[3072,256]{1,0:T(8,128)(2,1)S(1)}, bf16[3072,256]{1,0:T(8,128)(2,1)S(1)}, u32[]{:S(2)}, u32[]{:S(2)}) collective-permute-start(bf16[3072,256]{1,0:T(8,128)(2,1)S(1)} %maximum_select_fusion.3.near), channel_id=1, source_target_pairs={{8,16},{16,8},{9,17},{17,9},{10,18},{18,10},{11,19},{19,11},{12,20... | collective-permute-start | bytes 4718600 | tf_op jit(solution)/shard_map/ppermute | solution.py:56
  183.4 35.7 %collective-permute-start.7 = (bf16[3072,256]{1,0:T(8,128)(2,1)S(1)}, bf16[3072,256]{1,0:T(8,128)(2,1)S(1)}, u32[]{:S(2)}, u32[]{:S(2)}) collective-permute-start(bf16[3072,256]{1,0:T(8,128)(2,1)S(1)} %collective-permute-done.4.middle), channel_id=1, source_target_pairs={{8,0},{16,24},{9,1},{17,25},{10,2},{18,26},{11,3},{19,27},{12,4},{... | collective-permute-start | bytes 4718600 | tf_op jit(solution)/shard_map/ppermute | solution.py:56
  225.7 61.3 %collective-permute-start.10 = (bf16[3072,256]{1,0:T(8,128)(2,1)}, bf16[3072,256]{1,0:T(8,128)(2,1)}, u32[]{:S(2)}, u32[]{:S(2)}) collective-permute-start(bf16[3072,256]{1,0:T(8,128)(2,1)} %collective-permute-done.8.middle), channel_id=1, source_target_pairs={{8,0},{16,24},{9,1},{17,25},{10,2},{18,26},{11,3},{19,27},{12,4},{... | collective-permute-start | bytes 4718600 | tf_op jit(solution)/shard_map/ppermute | solution.py:56
  227.0 60.0 %collective-permute-start.9 = (bf16[3072,256]{1,0:T(8,128)(2,1)}, bf16[3072,256]{1,0:T(8,128)(2,1)}, u32[]{:S(2)}, u32[]{:S(2)}) collective-permute-start(bf16[3072,256]{1,0:T(8,128)(2,1)} %maximum_select_fusion.5.near), channel_id=1, source_target_pairs={{8,16},{16,8},{9,17},{17,9},{10,18},{18,10},{11,19},{19,11},{12,20... | collective-permute-start | bytes 4718600 | tf_op jit(solution)/shard_map/ppermute | solution.py:56
  253.6 53.8 %collective-permute-start.12 = (bf16[2048,256]{1,0:T(8,128)(2,1)}, bf16[2048,256]{1,0:T(8,128)(2,1)}, u32[]{:S(2)}, u32[]{:S(2)}) collective-permute-start(bf16[2048,256]{1,0:T(8,128)(2,1)} %broadcast_select_fusion.5), channel_id=1, source_target_pairs={{0,8},{24,16},{1,9},{25,17},{2,10},{26,18},{3,11},{27,19},{4,12},{... | collective-permute-start | bytes 3145736 | tf_op jit(solution)/shard_map/ppermute | solution.py:56
  287.1 57.6 %collective-permute-start.11 = (bf16[3072,256]{1,0:T(8,128)(2,1)}, bf16[3072,256]{1,0:T(8,128)(2,1)S(1)}, u32[]{:S(2)}, u32[]{:S(2)}) collective-permute-start(bf16[3072,256]{1,0:T(8,128)(2,1)} %collective-permute-done.9.middle), channel_id=1, source_target_pairs={{8,0},{16,24},{9,1},{17,25},{10,2},{18,26},{11,3},{19,27},{12,4},{... | collective-permute-start | bytes 4718600 | tf_op jit(solution)/shard_map/ppermute | solution.py:56
  307.6 31.8 %collective-permute-start.14 = (bf16[2048,256]{1,0:T(8,128)(2,1)S(1)}, bf16[2048,256]{1,0:T(8,128)(2,1)S(1)}, u32[]{:S(2)}, u32[]{:S(2)}) collective-permute-start(bf16[2048,256]{1,0:T(8,128)(2,1)S(1)} %broadcast_select_fusion.4), channel_id=1, source_target_pairs={{0,8},{24,16},{1,9},{25,17},{2,10},{26,18},{3,11},{27,19},{4,12},{... | collective-permute-start | bytes 3145736 | tf_op jit(solution)/shard_map/ppermute | solution.py:56
  321.2 50.0 %collective-permute-start.15 = (bf16[1024,256]{1,0:T(8,128)(2,1)}, bf16[1024,256]{1,0:T(8,128)(2,1)}, u32[]{:S(2)}, u32[]{:S(2)}) collective-permute-start(bf16[1024,256]{1,0:T(8,128)(2,1)} %select_convert_fusion.1), channel_id=1, source_target_pairs={{0,8},{8,0},{16,24},{24,16},{1,9},{9,1},{17,25},{25,17},{2,10},{10... | collective-permute-start | bytes 1572872 | tf_op jit(solution)/shard_map/ppermute | solution.py:56
  340.8 38.2 %collective-permute-start.16 = (bf16[2048,256]{1,0:T(8,128)(2,1)}, bf16[2048,256]{1,0:T(8,128)(2,1)}, u32[]{:S(2)}, u32[]{:S(2)}) collective-permute-start(bf16[2048,256]{1,0:T(8,128)(2,1)} %add_convert_fusion.3), channel_id=1, source_target_pairs={{8,16},{16,8},{9,17},{17,9},{10,18},{18,10},{11,19},{19,11},{12,20... | collective-permute-start | bytes 3145736 | tf_op jit(solution)/shard_map/ppermute | solution.py:56
  370.2 19.9 %collective-permute-start.20 = (bf16[1024,256]{1,0:T(8,128)(2,1)S(1)}, bf16[1024,256]{1,0:T(8,128)(2,1)S(1)}, u32[]{:S(2)}, u32[]{:S(2)}) collective-permute-start(bf16[1024,256]{1,0:T(8,128)(2,1)S(1)} %copy-done.33), channel_id=1, source_target_pairs={{0,8},{8,0},{16,24},{24,16},{1,9},{9,1},{17,25},{25,17},{2,10},{10... | collective-permute-start | bytes 1572872 | tf_op jit(solution)/shard_map/ppermute | solution.py:56
  381.0 28.1 %collective-permute-start.17 = (bf16[1024,256]{1,0:T(8,128)(2,1)S(1)}, bf16[1024,256]{1,0:T(8,128)(2,1)S(1)}, u32[]{:S(2)}, u32[]{:S(2)}) collective-permute-start(bf16[1024,256]{1,0:T(8,128)(2,1)S(1)} %select_convert_fusion), channel_id=1, source_target_pairs={{0,8},{8,0},{16,24},{24,16},{1,9},{9,1},{17,25},{25,17},{2,10},{10... | collective-permute-start | bytes 1572872 | tf_op jit(solution)/shard_map/ppermute | solution.py:56
  384.6 23.1 %collective-permute-start.19 = (bf16[1024,256]{1,0:T(8,128)(2,1)S(1)}, bf16[1024,256]{1,0:T(8,128)(2,1)S(1)}, u32[]{:S(2)}, u32[]{:S(2)}) collective-permute-start(bf16[1024,256]{1,0:T(8,128)(2,1)S(1)} %add_convert_fusion.6), channel_id=1, source_target_pairs={{0,24},{8,16},{16,8},{24,0},{1,25},{9,17},{17,9},{25,1},{2,26},{10... | collective-permute-start | bytes 1572872 | tf_op jit(solution)/shard_map/ppermute | solution.py:56
  426.3 20.0 %collective-permute-start.22 = (bf16[256,1536]{1,0:T(8,128)(2,1)}, bf16[256,1536]{1,0:T(8,128)(2,1)S(1)}, u32[]{:S(2)}, u32[]{:S(2)}) collective-permute-start(bf16[256,1536]{1,0:T(8,128)(2,1)} %pad_maximum_fusion.1), channel_id=1, source_target_pairs={{0,2},{1,3},{2,0},{3,1},{4,6},{5,7},{6,4},{7,5},{8,10},{9,11},{10,... | collective-permute-start | bytes 2359304 | tf_op jit(solution)/shard_map/ppermute | solution.py:102
  448.9 20.5 %collective-permute-start.27 = (bf16[256,1536]{1,0:T(8,128)(2,1)S(1)}, bf16[256,1536]{1,0:T(8,128)(2,1)S(1)}, u32[]{:S(2)}, u32[]{:S(2)}) collective-permute-start(bf16[256,1536]{1,0:T(8,128)(2,1)S(1)} %pad_maximum_fusion.2), channel_id=1, source_target_pairs={{0,2},{1,3},{2,0},{3,1},{4,6},{5,7},{6,4},{7,5},{8,10},{9,11},{10,... | collective-permute-start | bytes 2359304 | tf_op jit(solution)/shard_map/ppermute | solution.py:102
  449.5 20.5 %collective-permute-start.28 = (bf16[256,1536]{1,0:T(8,128)(2,1)S(1)}, bf16[256,1536]{1,0:T(8,128)(2,1)S(1)}, u32[]{:S(2)}, u32[]{:S(2)}) collective-permute-start(bf16[256,1536]{1,0:T(8,128)(2,1)S(1)} %concatenate.74), channel_id=1, source_target_pairs={{0,4},{1,5},{2,6},{3,7},{4,0},{5,1},{6,2},{7,3},{8,12},{9,13},{10,... | collective-permute-start | bytes 2359304 | tf_op jit(solution)/shard_map/ppermute | solution.py:102
  451.1 27.4 %collective-permute-start.25 = (bf16[256,768]{1,0:T(8,128)(2,1)S(1)}, bf16[256,768]{1,0:T(8,128)(2,1)S(1)}, u32[]{:S(2)}, u32[]{:S(2)}) collective-permute-start(bf16[256,768]{1,0:T(8,128)(2,1)S(1)} %get-tuple-element.114), channel_id=1, source_target_pairs={{0,4},{1,5},{2,6},{3,7},{4,0},{5,1},{6,2},{7,3},{8,12},{9,13},{10,... | collective-permute-start | bytes 1179656 | tf_op jit(solution)/shard_map/ppermute | solution.py:102
  451.5 26.9 %collective-permute-start.26 = (bf16[256,768]{1,0:T(8,128)(2,1)S(1)}, bf16[256,768]{1,0:T(8,128)(2,1)S(1)}, u32[]{:S(2)}, u32[]{:S(2)}) collective-permute-start(bf16[256,768]{1,0:T(8,128)(2,1)S(1)} %get-tuple-element.115), channel_id=1, source_target_pairs={{0,2},{1,3},{2,0},{3,1},{4,6},{5,7},{6,4},{7,5},{8,10},{9,11},{10,... | collective-permute-start | bytes 1179656 | tf_op jit(solution)/shard_map/ppermute | solution.py:102
  (47 other events, 551.4 us)
Sparse Core Ops, SparseCore 0:
  9.9 57.0 all-gather.3
  142.6 71.3 all-gather.5
  220.4 69.4 reduce-scatter.1

commit v3 on v2

--- a/solution.py
+++ b/solution.py
@@ -7,7 +7,7 @@
 
 BF16 = jnp.bfloat16
 F32 = jnp.float32
-VMEM = 40 * 2**20
+VMEM = 60 * 2**20
 QUICK = pl.CostEstimate(flops=2**20, bytes_accessed=2**16, transcendentals=0)
 
 PAIRS = [(0, 1), (1, 0), (2, 3), (3, 2)]
@@ -92,7 +92,7 @@
             out_specs=pl.BlockSpec((height, width), lambda b, order: (0, b)),
         ),
         out_shape=jax.ShapeDtypeStruct((height, 4 * width), rows[0].dtype),
-        compiler_params=pltpu.CompilerParams(vmem_limit_bytes=VMEM),
+        compiler_params=pltpu.CompilerParams(vmem_limit_bytes=VMEM // 2),
         cost_estimate=QUICK,
     )(order, *rows, *right)
 
@@ -261,13 +261,13 @@
     out0 = send(middle0, OUTWARD)
     middle1 = send(near1, MIDDLE)
     columns = jnp.zeros((4 * height, width), BF16)
-    for bits, piece in zip((0, 1, 3, 2), together([gradient, pair, mirror, relay], left_part)):
+    near2 = line.near(own2, pair2)
+    for bits, piece in zip((0, 1, 3, 2), together([gradient, pair, mirror, relay], left_part, near2)):
         columns = line.placed(columns, piece, bits)
     product_here = contract_last(columns, gradient).astype(BF16)
-    product = lax.psum_scatter(after(product_here, out0), "col", scatter_dimension=0, tiled=True).astype(F32)
-    left_next = 0.95 * left_stat + 0.05 * product
-
-    middle1, near2 = together([middle1, line.near(own2, pair2)], out0, product_here)
+    product = lax.psum_scatter(after(product_here, out0, middle1), "col", scatter_dimension=0, tiled=True)
+
+    middle1, near2 = together([middle1, near2], out0, product_here)
     out1 = send(middle1, OUTWARD)
     middle2 = send(near2, MIDDLE)
 
@@ -306,6 +306,7 @@
     relay = after(relay, through1, other0)
     mirror = send(add(line.block(back2, 3), jnp.where(line.inner, relay, 0)), MIRROR)
     right2 = line.whole(near2, middle2, after(out2, relay))
+    left_next = 0.95 * left_stat + 0.05 * after(product, relay).astype(F32)
     mirror, pair = together([mirror, pair], right2)
     turned2 = line.block(back2, 0).astype(F32) + jnp.where(line.inner, 0, relay).astype(F32)
     turned2 = (turned2 + pair.astype(F32) + mirror.astype(F32)).astype(BF16)

time: 502 us -> 463 us (0.922)
  starting transfers between devices: 96.8 us -> 70.6 us
  local copies, waits for them, and re-layouts: 28.2 us -> 11.4 us
  Pallas kernels: 61.9 us -> 70.6 us
    ppermute x21, starting transfers between devices: 86.4 us -> 58.6 us  [send(): return lax.ppermute(x, self.axis, pairs)]
    unnamed x74 -> x54, local copies, waits for them, and re-layouts: 18.9 us -> 1.65 us
    pallas_call x3, Pallas kernels: 45.8 us -> 54.5 us  [part(): pl.pallas_call(part_kernel, grid_spec=pltpu.PrefetchScalarGridSpec(num_sc...]
  transfers between devices with their start and end apart: 34 -> 34, of which waited for: 17 -> 18; matrix products, arithmetic and copies ran while one was open for 13% -> 14% of each run, Pallas kernels for 11% -> 14%
where the time goes in v3:
time: 463 us; the launch traced here: 455 us
  waiting for transfers between devices  224 us (48%)
  starting transfers between devices  70.6 us (15%)
  Pallas kernels  70.6 us (15%)
  other arithmetic  38.7 us (8%)
  matrix products  24.6 us (5%)
  between operations  14.7 us (3%)
  local copies, waits for them, and re-layouts  11.4 us (2%)
    ppermute x21, waiting for transfers between devices, send(): return lax.ppermute(x, self.axis, pairs)  182 us
    ppermute x21, starting transfers between devices, send(): return lax.ppermute(x, self.axis, pairs)  58.6 us
    pallas_call x3, Pallas kernels, part(): pl.pallas_call(part_kernel, grid_spec=pltpu.PrefetchScalarGridSpec(num_sc...  54.5 us
    ppermute x10, waiting for transfers between devices, swap(): return lax.ppermute(x, axis, [(j, j ^ bit) for j in range(8)])  41.9 us
    pallas_call x4, Pallas kernels, products(): pl.pallas_call(products_kernel, grid_spec=pltpu.PrefetchScalarGridSpec(nu...  16.2 us
    dot_general x4, matrix products, contract_first(): lax.dot_general(first, second, (((0,), (0,)), ((), ())), preferred_elemen...  15.6 us
    ppermute x10, starting transfers between devices, swap(): return lax.ppermute(x, axis, [(j, j ^ bit) for j in range(8)])  11.9 us
    select_n x6, other arithmetic, joined(): jnp.where(keep_order, jnp.concatenate([first, second]), jnp.concatenate([...  10.4 us
  transfers between devices with their start and end apart: 34, of which 18 were waited for; matrix products, arithmetic and copies ran while one was open for 14% of the time, Pallas kernels for 14%

profile of v3, /device:TPU:0, one launch (start us, length us, event | category | flops | bytes accessed | tf_op | source)
XLA Modules:
  0.0 455.1 jit_solution(8417940305853595666)
XLA Ops:
  8.0 5.1 %collective-permute-start.1 = (bf16[1024,768]{1,0:T(8,128)(2,1)}, bf16[1024,768]{1,0:T(8,128)(2,1)S(1)}, u32[]{:S(2)}, u32[]{:S(2)}) collective-permute-start(bf16[1024,768]{1,0:T(8,128)(2,1)} %param.9), channel_id=1, source_target_pairs={{0,24},{8,16},{16,8},{24,0},{1,25},{9,17},{17,9},{25,1},{2,26},{10... | collective-permute-start | bytes 4718600 | tf_op jit(solution)/shard_map/ppermute | solution.py:56
  16.2 32.4 %collective-permute-done.1 = bf16[1024,768]{1,0:T(8,128)(2,1)S(1)} collective-permute-done((bf16[1024,768]{1,0:T(8,128)(2,1)}, bf16[1024,768]{1,0:T(8,128)(2,1)S(1)}, u32[]{:S(2)}, u32[]{:S(2)}) %collective-permute-start.1) | collective-permute-done | bytes 1572896 | tf_op jit(solution)/shard_map/ppermute | solution.py:56
  50.0 31.5 %collective-permute-done = bf16[1024,768]{1,0:T(8,128)(2,1)} collective-permute-done((bf16[1024,768]{1,0:T(8,128)(2,1)}, bf16[1024,768]{1,0:T(8,128)(2,1)}, u32[]{:S(2)}, u32[]{:S(2)}) %collective-permute-start) | collective-permute-done | bytes 1572896 | tf_op jit(solution)/shard_map/ppermute | solution.py:56
  83.6 4.1 fusion.4
  93.9 41.1 %collective-permute-done.3 = bf16[1536,256]{1,0:T(8,128)(2,1)S(1)} collective-permute-done((bf16[1536,256]{1,0:T(8,128)(2,1)S(1)}, bf16[1536,256]{1,0:T(8,128)(2,1)S(1)}, u32[]{:S(2)}, u32[]{:S(2)}) %collective-permute-start.3) | collective-permute-done | bytes 786464 | tf_op jit(solution)/shard_map/ppermute | solution.py:56
  135.4 5.7 %add_convert_fusion.2 = bf16[1024,768]{1,0:T(8,128)(2,1)} fusion(f32[1024,768]{1,0:T(8,128)S(1)} %copy-done.26, bf16[1024,768]{1,0:T(8,128)(2,1)} %collective-permute-done.2, bf16[4096,1024]{1,0:T(8,128)(2,1)} %all-gather.4.cloned.1.call-done.basis, s32[]{:T(128)S(6)} %select_n.148), kind=kOutput, calls=%fused_computation.6 | convolution fusion | flops 1612185600 | bytes 8388612 | tf_op jit(solution)/shard_map/dot_general | solution.py:27
  144.1 15.8 %collective-permute-done.4 = bf16[1536,256]{1,0:T(8,128)(2,1)S(1)} collective-permute-done((bf16[1536,256]{1,0:T(8,128)(2,1)S(1)}, bf16[1536,256]{1,0:T(8,128)(2,1)S(1)}, u32[]{:S(2)}, u32[]{:S(2)}) %collective-permute-start.4) | collective-permute-done | bytes 786464 | tf_op jit(solution)/shard_map/ppermute | solution.py:56
  161.7 17.5 %collective-permute-done.5 = bf16[1536,256]{1,0:T(8,128)(2,1)S(1)} collective-permute-done((bf16[1536,256]{1,0:T(8,128)(2,1)S(1)}, bf16[1536,256]{1,0:T(8,128)(2,1)S(1)}, u32[]{:S(2)}, u32[]{:S(2)}) %collective-permute-start.5) | collective-permute-done | bytes 786464 | tf_op jit(solution)/shard_map/ppermute | solution.py:56
  189.0 9.0 %convolution_convert_fusion = bf16[4096,1024]{1,0:T(8,128)(2,1)} fusion(bf16[4096,768]{1,0:T(8,128)(2,1)S(1)} %constant_dynamic-update-slice_fusion, bf16[1024,768]{1,0:T(8,128)(2,1)S(1)} %copy-done.16), kind=kOutput, calls=%fused_computation | convolution fusion | flops 6446645248 | bytes 16252928 | tf_op jit(solution)/shard_map/dot_general | solution.py:23
  198.0 19.2 %collective-permute-done.7.out = bf16[3072,256]{1,0:T(8,128)(2,1)S(1)} collective-permute-done((bf16[3072,256]{1,0:T(8,128)(2,1)}, bf16[3072,256]{1,0:T(8,128)(2,1)S(1)}, u32[]{:S(2)}, u32[]{:S(2)}) %collective-permute-start.7) | collective-permute-done | bytes 1572896 | tf_op jit(solution)/shard_map/ppermute | solution.py:56
  222.1 19.8 %shard_map.120 = (f32[1024,768]{1,0:T(8,128)}, f32[1024,768]{1,0:T(8,128)}, bf16[4096,256]{1,0:T(8,128)(2,1)}) custom-call(s32[3]{0:T(128)} %pad_add_fusion.place, bf16[8,1024,768]{2,1,0:T(8,128)(2,1)} %bitcast.8, bf16[3072,256]{1,0:T(8,128)(2,1)} %copy-done.8, bf16[3072,256]{1,0:T(8,128)(2,1)} %collective-permute-done.6.middle, ...), custom_call_target="tpu_custom_call" | custom-call | flops 1048576 | bytes 65536 | tf_op jit(solution)/shard_map/pallas_call | solution.py:207
  244.6 6.1 %collective-permute-start.12 = (bf16[2048,256]{1,0:T(8,128)(2,1)}, bf16[2048,256]{1,0:T(8,128)(2,1)}, u32[]{:S(2)}, u32[]{:S(2)}) collective-permute-start(bf16[2048,256]{1,0:T(8,128)(2,1)} %broadcast_select_fusion.5), channel_id=1, source_target_pairs={{0,8},{24,16},{1,9},{25,17},{2,10},{26,18},{3,11},{27,19},{4,12},{... | collective-permute-start | bytes 3145736 | tf_op jit(solution)/shard_map/ppermute | solution.py:56
  254.9 17.5 %shard_map.121 = (f32[1024,768]{1,0:T(8,128)}, f32[1024,768]{1,0:T(8,128)}, bf16[4096,256]{1,0:T(8,128)(2,1)}) custom-call(s32[3]{0:T(128)} %pad_add_fusion.place, bf16[8,1024,768]{2,1,0:T(8,128)(2,1)} %bitcast.9, bf16[3072,256]{1,0:T(8,128)(2,1)} %maximum_select_fusion.4.near, ...), custom_call_target="tpu_custom_call", output_to_operand_aliasing={{0}: (8, {}), {1}: (9, {})} | custom-call | flops 1048576 | bytes 65536 | tf_op jit(solution)/shard_map/pallas_call | solution.py:207
  274.3 6.8 %collective-permute-start.14 = (bf16[2048,256]{1,0:T(8,128)(2,1)S(1)}, bf16[2048,256]{1,0:T(8,128)(2,1)S(1)}, u32[]{:S(2)}, u32[]{:S(2)}) collective-permute-start(bf16[2048,256]{1,0:T(8,128)(2,1)S(1)} %broadcast_select_fusion.4), channel_id=1, source_target_pairs={{0,8},{24,16},{1,9},{25,17},{2,10},{26,18},{3,11},{27,19},{4,12},{... | collective-permute-start | bytes 3145736 | tf_op jit(solution)/shard_map/ppermute | solution.py:56
  287.7 18.0 %collective-permute-start.17 = (bf16[1024,256]{1,0:T(8,128)(2,1)}, bf16[1024,256]{1,0:T(8,128)(2,1)}, u32[]{:S(2)}, u32[]{:S(2)}) collective-permute-start(bf16[1024,256]{1,0:T(8,128)(2,1)} %select_convert_fusion.1), channel_id=1, source_target_pairs={{0,8},{8,0},{16,24},{24,16},{1,9},{9,1},{17,25},{25,17},{2,10},{10... | collective-permute-start | bytes 1572872 | tf_op jit(solution)/shard_map/ppermute | solution.py:56
  310.9 17.2 %shard_map.122 = (f32[1024,768]{1,0:T(8,128)}, f32[1024,768]{1,0:T(8,128)}, bf16[4096,256]{1,0:T(8,128)(2,1)}) custom-call(s32[3]{0:T(128)} %pad_add_fusion.place, bf16[8,1024,768]{2,1,0:T(8,128)(2,1)} %bitcast.10, bf16[3072,256]{1,0:T(8,128)(2,1)} %copy-done.6, ...), custom_call_target="tpu_custom_call", output_to_operand_aliasing={{0}: (8, {}), {1}: (9, {})} | custom-call | flops 1048576 | bytes 65536 | tf_op jit(solution)/shard_map/pallas_call | solution.py:207
  335.4 8.2 %collective-permute-done.15 = bf16[1024,256]{1,0:T(8,128)(2,1)} collective-permute-done((bf16[1024,256]{1,0:T(8,128)(2,1)}, bf16[1024,256]{1,0:T(8,128)(2,1)}, u32[]{:S(2)}, u32[]{:S(2)}) %collective-permute-start.15) | collective-permute-done | bytes 524320 | tf_op jit(solution)/shard_map/ppermute | solution.py:56
  357.9 10.2 %collective-permute-done.19 = bf16[1024,256]{1,0:T(8,128)(2,1)S(1)} collective-permute-done((bf16[1024,256]{1,0:T(8,128)(2,1)}, bf16[1024,256]{1,0:T(8,128)(2,1)S(1)}, u32[]{:S(2)}, u32[]{:S(2)}) %collective-permute-start.19) | collective-permute-done | bytes 524320 | tf_op jit(solution)/shard_map/ppermute | solution.py:56
  373.0 4.0 shard_map.123
  377.1 4.0 shard_map.124
  397.8 11.0 %collective-permute-done.22 = bf16[256,1536]{1,0:T(8,128)(2,1)S(1)} collective-permute-done((bf16[256,1536]{1,0:T(8,128)(2,1)S(1)}, bf16[256,1536]{1,0:T(8,128)(2,1)S(1)}, u32[]{:S(2)}, u32[]{:S(2)}) %collective-permute-start.22) | collective-permute-done | bytes 786464 | tf_op jit(solution)/shard_map/ppermute | solution.py:102
  414.6 16.4 %collective-permute-done.27 = bf16[256,1536]{1,0:T(8,128)(2,1)S(1)} collective-permute-done((bf16[256,1536]{1,0:T(8,128)(2,1)S(1)}, bf16[256,1536]{1,0:T(8,128)(2,1)S(1)}, u32[]{:S(2)}, u32[]{:S(2)}) %collective-permute-start.27) | collective-permute-done | bytes 786464 | tf_op jit(solution)/shard_map/ppermute | solution.py:102
  435.1 4.8 %collective-permute-done.25 = bf16[256,768]{1,0:T(8,128)(2,1)S(1)} collective-permute-done((bf16[256,768]{1,0:T(8,128)(2,1)S(1)}, bf16[256,768]{1,0:T(8,128)(2,1)S(1)}, u32[]{:S(2)}, u32[]{:S(2)}) %collective-permute-start.25) | collective-permute-done | bytes 393248 | tf_op jit(solution)/shard_map/ppermute | solution.py:102
  440.2 6.3 %collective-permute-done.29 = bf16[256,768]{1,0:T(8,128)(2,1)S(1)} collective-permute-done((bf16[256,768]{1,0:T(8,128)(2,1)S(1)}, bf16[256,768]{1,0:T(8,128)(2,1)S(1)}, u32[]{:S(2)}, u32[]{:S(2)}) %collective-permute-start.29) | collective-permute-done | bytes 393248 | tf_op jit(solution)/shard_map/ppermute | solution.py:102
  (158 shorter events, 108.4 us)
Async XLA Ops:
  7.2 76.4 %all-gather.4.cloned.1.call-start = ((), (), s32[]{:S(2)}) async-start(), calls=%async_computation.1 | async-start | bytes 9437184 | tf_op jit(solution)/shard_map/all_gather | solution.py:241
  7.9 214.2 %all-gather.6.cloned.1.call-start = ((), (), s32[]{:S(2)}) async-start(), calls=%async_computation.3 | async-start | bytes 14155776 | tf_op jit(solution)/shard_map/all_gather | solution.py:258
  8.0 40.6 %collective-permute-start.1 = (bf16[1024,768]{1,0:T(8,128)(2,1)}, bf16[1024,768]{1,0:T(8,128)(2,1)S(1)}, u32[]{:S(2)}, u32[]{:S(2)}) collective-permute-start(bf16[1024,768]{1,0:T(8,128)(2,1)} %param.9), channel_id=1, source_target_pairs={{0,24},{8,16},{16,8},{24,0},{1,25},{9,17},{17,9},{25,1},{2,26},{10... | collective-permute-start | bytes 4718600 | tf_op jit(solution)/shard_map/ppermute | solution.py:56
  13.1 68.5 %collective-permute-start = (bf16[1024,768]{1,0:T(8,128)(2,1)}, bf16[1024,768]{1,0:T(8,128)(2,1)}, u32[]{:S(2)}, u32[]{:S(2)}) collective-permute-start(bf16[1024,768]{1,0:T(8,128)(2,1)} %param.9), channel_id=1, source_target_pairs={{0,8},{8,0},{16,24},{24,16},{1,9},{9,1},{17,25},{25,17},{2,10},{10... | collective-permute-start | bytes 4718600 | tf_op jit(solution)/shard_map/ppermute | solution.py:56
  81.6 53.8 %collective-permute-start.2 = (bf16[1024,768]{1,0:T(8,128)(2,1)}, bf16[1024,768]{1,0:T(8,128)(2,1)}, u32[]{:S(2)}, u32[]{:S(2)}) collective-permute-start(bf16[1024,768]{1,0:T(8,128)(2,1)} %broadcast_select_fusion.3), channel_id=1, source_target_pairs={{0,16},{8,0},{16,24},{24,8},{1,17},{9,1},{17,25},{25,9},{2,18},{10... | collective-permute-start | bytes 4718600 | tf_op jit(solution)/shard_map/ppermute | solution.py:56
  93.8 41.2 %collective-permute-start.3 = (bf16[1536,256]{1,0:T(8,128)(2,1)S(1)}, bf16[1536,256]{1,0:T(8,128)(2,1)S(1)}, u32[]{:S(2)}, u32[]{:S(2)}) collective-permute-start(bf16[1536,256]{1,0:T(8,128)(2,1)S(1)} %copy-done.21), channel_id=1, source_target_pairs={{0,8},{8,0},{16,24},{24,16},{1,9},{9,1},{17,25},{25,17},{2,10},{10... | collective-permute-start | bytes 2359304 | tf_op jit(solution)/shard_map/ppermute | solution.py:56
  141.1 208.2 %reduce-scatter.2.cloned.1.call-start = ((), (), s32[]{:S(2)}) async-start(), calls=%async_computation.2 | async-start | bytes 9437184 | tf_op jit(solution)/shard_map/reduce_scatter | solution.py:268
  142.3 38.8 %collective-permute-start.6 = (bf16[3072,256]{1,0:T(8,128)(2,1)S(1)}, bf16[3072,256]{1,0:T(8,128)(2,1)}, u32[]{:S(2)}, u32[]{:S(2)}) collective-permute-start(bf16[3072,256]{1,0:T(8,128)(2,1)S(1)} %maximum_select_fusion.3.near), channel_id=1, source_target_pairs={{8,16},{16,8},{9,17},{17,9},{10,18},{18,10},{11,19},{19,11},{12,20... | collective-permute-start | bytes 4718600 | tf_op jit(solution)/shard_map/ppermute | solution.py:56
  181.1 36.1 %collective-permute-start.7 = (bf16[3072,256]{1,0:T(8,128)(2,1)}, bf16[3072,256]{1,0:T(8,128)(2,1)S(1)}, u32[]{:S(2)}, u32[]{:S(2)}) collective-permute-start(bf16[3072,256]{1,0:T(8,128)(2,1)} %collective-permute-done.6.middle), channel_id=1, source_target_pairs={{8,0},{16,24},{9,1},{17,25},{10,2},{18,26},{11,3},{19,27},{12,4},{... | collective-permute-start | bytes 4718600 | tf_op jit(solution)/shard_map/ppermute | solution.py:56
  182.7 34.5 %collective-permute-start.8 = (bf16[3072,256]{1,0:T(8,128)(2,1)}, bf16[3072,256]{1,0:T(8,128)(2,1)}, u32[]{:S(2)}, u32[]{:S(2)}) collective-permute-start(bf16[3072,256]{1,0:T(8,128)(2,1)} %maximum_select_fusion.4.near), channel_id=1, source_target_pairs={{8,16},{16,8},{9,17},{17,9},{10,18},{18,10},{11,19},{19,11},{12,20... | collective-permute-start | bytes 4718600 | tf_op jit(solution)/shard_map/ppermute | solution.py:56
  218.4 35.0 %collective-permute-start.10 = (bf16[3072,256]{1,0:T(8,128)(2,1)}, bf16[3072,256]{1,0:T(8,128)(2,1)S(1)}, u32[]{:S(2)}, u32[]{:S(2)}) collective-permute-start(bf16[3072,256]{1,0:T(8,128)(2,1)} %collective-permute-done.8.middle), channel_id=1, source_target_pairs={{8,0},{16,24},{9,1},{17,25},{10,2},{18,26},{11,3},{19,27},{12,4},{... | collective-permute-start | bytes 4718600 | tf_op jit(solution)/shard_map/ppermute | solution.py:56
  219.7 33.7 %collective-permute-start.9 = (bf16[3072,256]{1,0:T(8,128)(2,1)S(1)}, bf16[3072,256]{1,0:T(8,128)(2,1)}, u32[]{:S(2)}, u32[]{:S(2)}) collective-permute-start(bf16[3072,256]{1,0:T(8,128)(2,1)S(1)} %maximum_select_fusion.5.near), channel_id=1, source_target_pairs={{8,16},{16,8},{9,17},{17,9},{10,18},{18,10},{11,19},{19,11},{12,20... | collective-permute-start | bytes 4718600 | tf_op jit(solution)/shard_map/ppermute | solution.py:56
  244.6 27.9 %collective-permute-start.12 = (bf16[2048,256]{1,0:T(8,128)(2,1)}, bf16[2048,256]{1,0:T(8,128)(2,1)}, u32[]{:S(2)}, u32[]{:S(2)}) collective-permute-start(bf16[2048,256]{1,0:T(8,128)(2,1)} %broadcast_select_fusion.5), channel_id=1, source_target_pairs={{0,8},{24,16},{1,9},{25,17},{2,10},{26,18},{3,11},{27,19},{4,12},{... | collective-permute-start | bytes 3145736 | tf_op jit(solution)/shard_map/ppermute | solution.py:56
  253.4 57.4 %collective-permute-start.11 = (bf16[3072,256]{1,0:T(8,128)(2,1)}, bf16[3072,256]{1,0:T(8,128)(2,1)}, u32[]{:S(2)}, u32[]{:S(2)}) collective-permute-start(bf16[3072,256]{1,0:T(8,128)(2,1)} %collective-permute-done.9.middle), channel_id=1, source_target_pairs={{8,0},{16,24},{9,1},{17,25},{10,2},{18,26},{11,3},{19,27},{12,4},{... | collective-permute-start | bytes 4718600 | tf_op jit(solution)/shard_map/ppermute | solution.py:56
  274.3 31.4 %collective-permute-start.14 = (bf16[2048,256]{1,0:T(8,128)(2,1)S(1)}, bf16[2048,256]{1,0:T(8,128)(2,1)S(1)}, u32[]{:S(2)}, u32[]{:S(2)}) collective-permute-start(bf16[2048,256]{1,0:T(8,128)(2,1)S(1)} %broadcast_select_fusion.4), channel_id=1, source_target_pairs={{0,8},{24,16},{1,9},{25,17},{2,10},{26,18},{3,11},{27,19},{4,12},{... | collective-permute-start | bytes 3145736 | tf_op jit(solution)/shard_map/ppermute | solution.py:56
  287.7 45.0 %collective-permute-start.17 = (bf16[1024,256]{1,0:T(8,128)(2,1)}, bf16[1024,256]{1,0:T(8,128)(2,1)}, u32[]{:S(2)}, u32[]{:S(2)}) collective-permute-start(bf16[1024,256]{1,0:T(8,128)(2,1)} %select_convert_fusion.1), channel_id=1, source_target_pairs={{0,8},{8,0},{16,24},{24,16},{1,9},{9,1},{17,25},{25,17},{2,10},{10... | collective-permute-start | bytes 1572872 | tf_op jit(solution)/shard_map/ppermute | solution.py:56
  307.2 36.4 %collective-permute-start.16 = (bf16[2048,256]{1,0:T(8,128)(2,1)}, bf16[2048,256]{1,0:T(8,128)(2,1)}, u32[]{:S(2)}, u32[]{:S(2)}) collective-permute-start(bf16[2048,256]{1,0:T(8,128)(2,1)} %add_convert_fusion.3), channel_id=1, source_target_pairs={{8,16},{16,8},{9,17},{17,9},{10,18},{18,10},{11,19},{19,11},{12,20... | collective-permute-start | bytes 3145736 | tf_op jit(solution)/shard_map/ppermute | solution.py:56
  331.5 26.4 %collective-permute-start.20 = (bf16[1024,256]{1,0:T(8,128)(2,1)}, bf16[1024,256]{1,0:T(8,128)(2,1)}, u32[]{:S(2)}, u32[]{:S(2)}) collective-permute-start(bf16[1024,256]{1,0:T(8,128)(2,1)} %get-tuple-element.137), channel_id=1, source_target_pairs={{0,8},{8,0},{16,24},{24,16},{1,9},{9,1},{17,25},{25,17},{2,10},{10... | collective-permute-start | bytes 1572872 | tf_op jit(solution)/shard_map/ppermute | solution.py:56
  388.4 20.4 %collective-permute-start.22 = (bf16[256,1536]{1,0:T(8,128)(2,1)S(1)}, bf16[256,1536]{1,0:T(8,128)(2,1)S(1)}, u32[]{:S(2)}, u32[]{:S(2)}) collective-permute-start(bf16[256,1536]{1,0:T(8,128)(2,1)S(1)} %pad_maximum_fusion.1), channel_id=1, source_target_pairs={{0,2},{1,3},{2,0},{3,1},{4,6},{5,7},{6,4},{7,5},{8,10},{9,11},{10,... | collective-permute-start | bytes 2359304 | tf_op jit(solution)/shard_map/ppermute | solution.py:102
  390.7 19.5 %collective-permute-start.23 = (bf16[256,1536]{1,0:T(8,128)(2,1)S(1)}, bf16[256,1536]{1,0:T(8,128)(2,1)S(1)}, u32[]{:S(2)}, u32[]{:S(2)}) collective-permute-start(bf16[256,1536]{1,0:T(8,128)(2,1)S(1)} %concatenate.73), channel_id=1, source_target_pairs={{0,4},{1,5},{2,6},{3,7},{4,0},{5,1},{6,2},{7,3},{8,12},{9,13},{10,... | collective-permute-start | bytes 2359304 | tf_op jit(solution)/shard_map/ppermute | solution.py:102
  410.5 20.5 %collective-permute-start.27 = (bf16[256,1536]{1,0:T(8,128)(2,1)S(1)}, bf16[256,1536]{1,0:T(8,128)(2,1)S(1)}, u32[]{:S(2)}, u32[]{:S(2)}) collective-permute-start(bf16[256,1536]{1,0:T(8,128)(2,1)S(1)} %pad_maximum_fusion.2), channel_id=1, source_target_pairs={{0,2},{1,3},{2,0},{3,1},{4,6},{5,7},{6,4},{7,5},{8,10},{9,11},{10,... | collective-permute-start | bytes 2359304 | tf_op jit(solution)/shard_map/ppermute | solution.py:102
  410.9 20.5 %collective-permute-start.28 = (bf16[256,1536]{1,0:T(8,128)(2,1)S(1)}, bf16[256,1536]{1,0:T(8,128)(2,1)S(1)}, u32[]{:S(2)}, u32[]{:S(2)}) collective-permute-start(bf16[256,1536]{1,0:T(8,128)(2,1)S(1)} %concatenate.74), channel_id=1, source_target_pairs={{0,4},{1,5},{2,6},{3,7},{4,0},{5,1},{6,2},{7,3},{8,12},{9,13},{10,... | collective-permute-start | bytes 2359304 | tf_op jit(solution)/shard_map/ppermute | solution.py:102
  412.7 27.2 %collective-permute-start.25 = (bf16[256,768]{1,0:T(8,128)(2,1)S(1)}, bf16[256,768]{1,0:T(8,128)(2,1)S(1)}, u32[]{:S(2)}, u32[]{:S(2)}) collective-permute-start(bf16[256,768]{1,0:T(8,128)(2,1)S(1)} %get-tuple-element.116), channel_id=1, source_target_pairs={{0,4},{1,5},{2,6},{3,7},{4,0},{5,1},{6,2},{7,3},{8,12},{9,13},{10,... | collective-permute-start | bytes 1179656 | tf_op jit(solution)/shard_map/ppermute | solution.py:102
  413.0 26.9 %collective-permute-start.26 = (bf16[256,768]{1,0:T(8,128)(2,1)S(1)}, bf16[256,768]{1,0:T(8,128)(2,1)S(1)}, u32[]{:S(2)}, u32[]{:S(2)}) collective-permute-start(bf16[256,768]{1,0:T(8,128)(2,1)S(1)} %get-tuple-element.117), channel_id=1, source_target_pairs={{0,2},{1,3},{2,0},{3,1},{4,6},{5,7},{6,4},{7,5},{8,10},{9,11},{10,... | collective-permute-start | bytes 1179656 | tf_op jit(solution)/shard_map/ppermute | solution.py:102
  (37 other events, 551.9 us)
Sparse Core Ops, SparseCore 0:
  9.9 57.0 all-gather.3
  141.3 71.3 all-gather.5
  217.4 72.8 reduce-scatter.1

commit v4 on v3

--- a/solution.py
+++ b/solution.py
@@ -154,66 +154,85 @@
 STEPS = 2
 
 
-def part_kernel(place, left, near, middle, out, first, second, basis, *rest):
+def accumulate(total, left, right):
+    depth = left.shape[2]
+    for b in range(left.shape[0]):
+        total[...] += jnp.dot(left[b], right[b * depth : (b + 1) * depth, :], preferred_element_type=F32)
+
+
+def near_kernel(place, left, near, total):
+    @pl.when(pl.program_id(0) == 0)
+    def _():
+        total[...] = jnp.zeros_like(total)
+
+    accumulate(total, left, near)
+
+
+def near_product(place, left_rotated, near):
+    blocks, height, width = left_rotated.shape
+    size = near.shape[1]
+    deep = near.shape[0] // STEPS
+    return pl.pallas_call(
+        near_kernel,
+        grid_spec=pltpu.PrefetchScalarGridSpec(
+            num_scalar_prefetch=1,
+            grid=(STEPS,),
+            in_specs=[
+                pl.BlockSpec((blocks // 2 // STEPS, height, width), lambda s, place: (place[0] + s, 0, 0)),
+                pl.BlockSpec((deep, size), lambda s, place: (s, 0)),
+            ],
+            out_specs=pl.BlockSpec((height, size), lambda s, place: (0, 0)),
+        ),
+        out_shape=jax.ShapeDtypeStruct((height, size), F32),
+        compiler_params=pltpu.CompilerParams(vmem_limit_bytes=VMEM),
+        cost_estimate=QUICK,
+    )(place, left_rotated, near)
+
+
+def part_kernel(place, left, middle, out, near, first, second, basis, *rest):
     first_out, second_out, back, total, normalized = rest[-5:]
     step = pl.program_id(0)
 
     @pl.when(step == 0)
     def _():
-        total[...] = jnp.zeros_like(total)
-
-    def accumulate(right):
-        depth = left.shape[2]
-        for b in range(left.shape[0]):
-            total[...] += jnp.dot(left[b], right[b * depth : (b + 1) * depth, :], preferred_element_type=F32)
-
-    @pl.when(step < STEPS)
-    def _():
-        accumulate(near)
-
-    far = (step >= STEPS) & (step < 2 * STEPS)
-
-    @pl.when(far & (place[2] == 1))
-    def _():
-        accumulate(middle)
-
-    @pl.when(far & (place[2] == 0))
-    def _():
-        accumulate(out)
-
-    @pl.when(step == 2 * STEPS - 1)
+        total[...] = near[...]
+
+    @pl.when((step < STEPS) & (place[2] == 1))
+    def _():
+        accumulate(total, left, middle)
+
+    @pl.when((step < STEPS) & (place[2] == 0))
+    def _():
+        accumulate(total, left, out)
+
+    @pl.when(step == STEPS - 1)
     def _():
         first_out[...], second_out[...], normalized[...] = moments(total[...], first[...], second[...])
 
-    @pl.when(step >= 2 * STEPS)
+    @pl.when(step >= STEPS)
     def _():
         back[...] = jnp.dot(basis[...], normalized[...], preferred_element_type=F32).astype(BF16)
 
 
 def part(number, place, left_rotated, near, middle, out, first_moment, second_moment, left_cols, before):
     height, width = first_moment.shape
-    size = near.shape[1]
-    deep = near.shape[0] // STEPS
+    size = middle.shape[1]
+    deep = middle.shape[0] // STEPS
     tall = left_cols.shape[0] // 2
-    near_step = lambda s: jnp.minimum(s, STEPS - 1)
-    far_step = lambda s: jnp.clip(s - STEPS, 0, STEPS - 1)
-    last_step = lambda s: jnp.maximum(s - 2 * STEPS, 0)
-
-    def left_block(s, place):
-        return jnp.where(s < STEPS, place[0] + near_step(s), place[1] + far_step(s)), 0, 0
-
+    step = lambda s: jnp.minimum(s, STEPS - 1)
+    last_step = lambda s: jnp.maximum(s - STEPS, 0)
     moment = pl.BlockSpec((height, size), lambda s, place: (0, number))
     before = list(before)
     return pl.pallas_call(
         part_kernel,
         grid_spec=pltpu.PrefetchScalarGridSpec(
             num_scalar_prefetch=1,
-            grid=(2 * STEPS + 2,),
+            grid=(STEPS + 2,),
             in_specs=[
-                pl.BlockSpec((4 // STEPS, height, width), left_block),
-                pl.BlockSpec((deep, size), lambda s, place: (near_step(s), 0)),
-                pl.BlockSpec((deep, size), lambda s, place: (far_step(s) * place[2], 0)),
-                pl.BlockSpec((deep, size), lambda s, place: (far_step(s) * (1 - place[2]), 0)),
+                pl.BlockSpec((4 // STEPS, height, width), lambda s, place: (place[1] + step(s), 0, 0)),
+                pl.BlockSpec((deep, size), lambda s, place: (step(s) * place[2], 0)),
+                pl.BlockSpec((deep, size), lambda s, place: (step(s) * (1 - place[2]), 0)),
+                pl.BlockSpec((height, size), lambda s, place: (0, 0)),
                 moment,
                 moment,
                 pl.BlockSpec((tall, height), lambda s, place: (last_step(s), 0)),
@@ -230,7 +249,7 @@
         input_output_aliases={8: 0, 9: 1} if before else {},
         compiler_params=pltpu.CompilerParams(vmem_limit_bytes=VMEM),
         cost_estimate=QUICK,
-    )(place, left_rotated, near, middle, out, first_moment, second_moment, left_cols, *before)
+    )(place, left_rotated, middle, out, near, first_moment, second_moment, left_cols, *before)
 
 
 def body_on_line(gradient, left_stat, left_basis, right_basis, first_moment, second_moment):
@@ -280,38 +299,40 @@
         )
         return before, back
 
-    moments0, back0 = next_part(0, near0, middle0, after(out0, near2), ())
+    half0 = near_product(place, left_rotated, after(near0, near2))
+    moments0, back0 = next_part(0, half0, middle0, out0, ())
     stay0, far0 = halves(line.lower, back0)
     got0 = send(far0, INWARD)
-    out2 = send(after(middle2, out1, far0), OUTWARD)
-    moments1, back1 = next_part(1, near1, middle1, after(out1, far0), moments0)
-    stay1, far1 = halves(line.lower, after(back1, got0))
+    half1 = near_product(place, left_rotated, after(near1, far0))
+    out1 = after(out1, half1)
+    out2 = send(after(middle2, out1), OUTWARD)
+    moments1, back1 = next_part(1, half1, middle1, out1, moments0)
+    stay1, far1 = halves(line.lower, back1)
     got1 = send(far1, INWARD)
     through0 = send(add(far0, after(got0, far1)), MIDDLE)
-    right0 = line.whole(near0, middle0, after(out0, far1))
-    right1 = line.whole(near1, middle1, after(out1, far1))
+    half2 = near_product(place, left_rotated, after(near2, far1))
+    got1, out2 = together([got1, out2], half2)
+    through1 = add(far1, got1)
+    moments2, back2 = next_part(2, half2, middle2, after(out2, through1), moments1)
+    through1 = send(through1, MIDDLE)
     mine0, other0 = halves(line.even, stay0.astype(F32) + through0.astype(F32))
-    other0 = other0.astype(BF16)
-    through1 = add(far1, got1)
-    moments2, back2 = next_part(2, near2, middle2, after(out2, other0, through1, right0, right1), moments1)
-    other0 = send(other0, PAIRS)
-    turned0 = (mine0 + other0.astype(F32)).astype(BF16)
-    through1 = send(through1, MIDDLE)
+    turned0 = (mine0 + send(other0.astype(BF16), PAIRS).astype(F32)).astype(BF16)
     mine1, other1 = halves(line.even, stay1.astype(F32) + through1.astype(F32))
     turned1 = (mine1 + send(other1.astype(BF16), PAIRS).astype(F32)).astype(BF16)
     first_next, second_next = moments2
 
     relay = send(line.block(back2, 2), RELAY_BACK)
     pair = send(line.block(back2, 1), PAIRS)
-    relay = after(relay, through1, other0)
+    relay = after(relay, through1)
     mirror = send(add(line.block(back2, 3), jnp.where(line.inner, relay, 0)), MIRROR)
-    right2 = line.whole(near2, middle2, after(out2, relay))
-    left_next = 0.95 * left_stat + 0.05 * after(product, relay).astype(F32)
-    mirror, pair = together([mirror, pair], right2)
+    out0, out1, out2, product = together([out0, out1, out2, product], turned1)
+    right = [line.whole(near0, middle0, out0), line.whole(near1, middle1, out1), line.whole(near2, middle2, out2)]
+    left_next = 0.95 * left_stat + 0.05 * product.astype(F32)
+    mirror, pair = together([mirror, pair], *right)
     turned2 = line.block(back2, 0).astype(F32) + jnp.where(line.inner, 0, relay).astype(F32)
     turned2 = (turned2 + pair.astype(F32) + mirror.astype(F32)).astype(BF16)
 
-    right = together([right0, right1, right2], left_next)
+    right = together(right, left_next)
     direction = scatter_columns([turned0, turned1, turned2], right, "col")
     return (left_next, first_next, second_next, direction)
 

time: 463 us -> 478 us (1.032)
  waiting for transfers between devices: 224 us -> 244 us
  starting transfers between devices: 70.6 us -> 56.3 us
  Pallas kernels: 70.6 us -> 77.4 us
    ppermute x21, waiting for transfers between devices: 182 us -> 201 us  [send(): return lax.ppermute(x, self.axis, pairs)]
    pallas_call x0 -> x3, Pallas kernels: none -> 17.8 us  [near_product(): pl.pallas_call(near_kernel, grid_spec=pltpu.PrefetchScalarGridSpec(num_sc...]
    ppermute x21, starting transfers between devices: 58.6 us -> 45.1 us  [send(): return lax.ppermute(x, self.axis, pairs)]
    pallas_call x3, Pallas kernels: 54.5 us -> 43.4 us  [part(): pl.pallas_call(part_kernel, grid_spec=pltpu.PrefetchScalarGridSpec(num_sc...]
  transfers between devices with their start and end apart: 34 -> 34, of which waited for: 18 -> 17; matrix products, arithmetic and copies ran while one was open for 14% -> 13% of each run, Pallas kernels for 14% -> 15%
where the time goes in v4:
time: 478 us; the launch traced here: 470 us
  waiting for transfers between devices  244 us (51%)
  Pallas kernels  77.4 us (16%)
  starting transfers between devices  56.3 us (12%)
  other arithmetic  40.7 us (9%)
  matrix products  24.6 us (5%)
  between operations  14.6 us (3%)
  local copies, waits for them, and re-layouts  11.8 us (2%)
    ppermute x21, waiting for transfers between devices, send(): return lax.ppermute(x, self.axis, pairs)  201 us
    ppermute x21, starting transfers between devices, send(): return lax.ppermute(x, self.axis, pairs)  45.1 us
    pallas_call x3, Pallas kernels, part(): pl.pallas_call(part_kernel, grid_spec=pltpu.PrefetchScalarGridSpec(num_sc...  43.4 us
    ppermute x10, waiting for transfers between devices, swap(): return lax.ppermute(x, axis, [(j, j ^ bit) for j in range(8)])  42 us
    pallas_call x3, Pallas kernels, near_product(): pl.pallas_call(near_kernel, grid_spec=pltpu.PrefetchScalarGridSpec(num_sc...  17.8 us
    pallas_call x4, Pallas kernels, products(): pl.pallas_call(products_kernel, grid_spec=pltpu.PrefetchScalarGridSpec(nu...  16.1 us
    dot_general x4, matrix products, contract_first(): lax.dot_general(first, second, (((0,), (0,)), ((), ())), preferred_elemen...  15.6 us
    ppermute x10, starting transfers between devices, swap(): return lax.ppermute(x, axis, [(j, j ^ bit) for j in range(8)])  11.1 us
  transfers between devices with their start and end apart: 34, of which 17 were waited for; matrix products, arithmetic and copies ran while one was open for 13% of the time, Pallas kernels for 15%

profile of v4, /device:TPU:0, one launch (start us, length us, event | category | flops | bytes accessed | tf_op | source)
XLA Modules:
  0.0 469.7 jit_solution(17142566302705329510)
XLA Ops:
  8.0 5.1 %collective-permute-start.1 = (bf16[1024,768]{1,0:T(8,128)(2,1)}, bf16[1024,768]{1,0:T(8,128)(2,1)S(1)}, u32[]{:S(2)}, u32[]{:S(2)}) collective-permute-start(bf16[1024,768]{1,0:T(8,128)(2,1)} %param.9), channel_id=1, source_target_pairs={{0,24},{8,16},{16,8},{24,0},{1,25},{9,17},{17,9},{25,1},{2,26},{10... | collective-permute-start | bytes 4718600 | tf_op jit(solution)/shard_map/ppermute | solution.py:56
  16.1 32.5 %collective-permute-done.1 = bf16[1024,768]{1,0:T(8,128)(2,1)S(1)} collective-permute-done((bf16[1024,768]{1,0:T(8,128)(2,1)}, bf16[1024,768]{1,0:T(8,128)(2,1)S(1)}, u32[]{:S(2)}, u32[]{:S(2)}) %collective-permute-start.1) | collective-permute-done | bytes 1572896 | tf_op jit(solution)/shard_map/ppermute | solution.py:56
  50.0 31.6 %collective-permute-done = bf16[1024,768]{1,0:T(8,128)(2,1)} collective-permute-done((bf16[1024,768]{1,0:T(8,128)(2,1)}, bf16[1024,768]{1,0:T(8,128)(2,1)}, u32[]{:S(2)}, u32[]{:S(2)}) %collective-permute-start) | collective-permute-done | bytes 1572896 | tf_op jit(solution)/shard_map/ppermute | solution.py:56
  93.9 41.1 %collective-permute-done.2 = bf16[1536,256]{1,0:T(8,128)(2,1)S(1)} collective-permute-done((bf16[1536,256]{1,0:T(8,128)(2,1)S(1)}, bf16[1536,256]{1,0:T(8,128)(2,1)S(1)}, u32[]{:S(2)}, u32[]{:S(2)}) %collective-permute-start.2) | collective-permute-done | bytes 786464 | tf_op jit(solution)/shard_map/ppermute | solution.py:56
  136.8 5.7 %add_convert_fusion.2 = bf16[1024,768]{1,0:T(8,128)(2,1)} fusion(f32[1024,768]{1,0:T(8,128)S(1)} %copy-done.21, bf16[1024,768]{1,0:T(8,128)(2,1)} %collective-permute-done.5, bf16[4096,1024]{1,0:T(8,128)(2,1)} %all-gather.4.cloned.1.call-done.basis, s32[]{:T(128)S(6)} %select_n.150), kind=kOutput, calls=%fused_computation.6 | convolution fusion | flops 1612185600 | bytes 8388612 | tf_op jit(solution)/shard_map/dot_general | solution.py:27
  145.5 15.8 %collective-permute-done.4 = bf16[1536,256]{1,0:T(8,128)(2,1)S(1)} collective-permute-done((bf16[1536,256]{1,0:T(8,128)(2,1)S(1)}, bf16[1536,256]{1,0:T(8,128)(2,1)S(1)}, u32[]{:S(2)}, u32[]{:S(2)}) %collective-permute-start.4) | collective-permute-done | bytes 786464 | tf_op jit(solution)/shard_map/ppermute | solution.py:56
  163.5 17.7 %collective-permute-done.6 = bf16[1536,256]{1,0:T(8,128)(2,1)S(1)} collective-permute-done((bf16[1536,256]{1,0:T(8,128)(2,1)}, bf16[1536,256]{1,0:T(8,128)(2,1)S(1)}, u32[]{:S(2)}, u32[]{:S(2)}) %collective-permute-start.6) | collective-permute-done | bytes 786464 | tf_op jit(solution)/shard_map/ppermute | solution.py:56
  191.8 9.1 %convolution_convert_fusion = bf16[4096,1024]{1,0:T(8,128)(2,1)} fusion(bf16[4096,768]{1,0:T(8,128)(2,1)S(1)} %constant_dynamic-update-slice_fusion, bf16[1024,768]{1,0:T(8,128)(2,1)S(1)} %copy-done.12), kind=kOutput, calls=%fused_computation | convolution fusion | flops 6446645248 | bytes 16252928 | tf_op jit(solution)/shard_map/dot_general | solution.py:23
  200.9 19.6 %collective-permute-done.7.out = bf16[3072,256]{1,0:T(8,128)(2,1)} collective-permute-done((bf16[3072,256]{1,0:T(8,128)(2,1)}, bf16[3072,256]{1,0:T(8,128)(2,1)}, u32[]{:S(2)}, u32[]{:S(2)}) %collective-permute-start.7) | collective-permute-done | bytes 1572896 | tf_op jit(solution)/shard_map/ppermute | solution.py:56
  224.2 5.8 %shard_map.120.near = f32[1024,256]{1,0:T(8,128)} custom-call(s32[3]{0:T(128)} %pad_add_fusion.place, bf16[8,1024,768]{2,1,0:T(8,128)(2,1)} %bitcast.8, bf16[3072,256]{1,0:T(8,128)(2,1)} %copy-done.3), custom_call_target="tpu_custom_call" | custom-call | flops 1048576 | bytes 65536 | tf_op jit(solution)/shard_map/pallas_call | solution.py:175
  230.1 16.1 %shard_map.121 = (f32[1024,768]{1,0:T(8,128)}, f32[1024,768]{1,0:T(8,128)}, bf16[4096,256]{1,0:T(8,128)(2,1)}) custom-call(s32[3]{0:T(128)} %pad_add_fusion.place, bf16[8,1024,768]{2,1,0:T(8,128)(2,1)} %bitcast.9, bf16[3072,256]{1,0:T(8,128)(2,1)} %collective-permute-done.3.middle, bf16[3072,256]{1,0:T(8,128)(2,1)} %collective-permute-done.7.out, ...), custom_call_target="tpu_custom_call" | custom-call | flops 1048576 | bytes 65536 | tf_op jit(solution)/shard_map/pallas_call | solution.py:226
  248.8 7.8 %collective-permute-start.15 = (bf16[2048,256]{1,0:T(8,128)(2,1)}, bf16[2048,256]{1,0:T(8,128)(2,1)}, u32[]{:S(2)}, u32[]{:S(2)}) collective-permute-start(bf16[2048,256]{1,0:T(8,128)(2,1)} %broadcast_select_fusion.5), channel_id=1, source_target_pairs={{0,8},{24,16},{1,9},{25,17},{2,10},{26,18},{3,11},{27,19},{4,12},{... | collective-permute-start | bytes 3145736 | tf_op jit(solution)/shard_map/ppermute | solution.py:56
  256.6 6.0 %shard_map.122.near = f32[1024,256]{1,0:T(8,128)} custom-call(s32[3]{0:T(128)} %pad_add_fusion.place, bf16[8,1024,768]{2,1,0:T(8,128)(2,1)} %bitcast.10, bf16[3072,256]{1,0:T(8,128)(2,1)} %copy-done.5), custom_call_target="tpu_custom_call" | custom-call | flops 1048576 | bytes 65536 | tf_op jit(solution)/shard_map/pallas_call | solution.py:175
  264.2 13.8 %shard_map.123 = (f32[1024,768]{1,0:T(8,128)}, f32[1024,768]{1,0:T(8,128)}, bf16[4096,256]{1,0:T(8,128)(2,1)}) custom-call(s32[3]{0:T(128)} %pad_add_fusion.place, bf16[8,1024,768]{2,1,0:T(8,128)(2,1)} %bitcast.11, bf16[3072,256]{1,0:T(8,128)(2,1)} %collective-permute-done.8.middle, ...), custom_call_target="tpu_custom_call", output_to_operand_aliasing={{0}: (8, {}), {1}: (9, {})} | custom-call | flops 1048576 | bytes 65536 | tf_op jit(solution)/shard_map/pallas_call | solution.py:226
  281.2 5.5 %collective-permute-start.10 = (bf16[2048,256]{1,0:T(8,128)(2,1)}, bf16[2048,256]{1,0:T(8,128)(2,1)S(1)}, u32[]{:S(2)}, u32[]{:S(2)}) collective-permute-start(bf16[2048,256]{1,0:T(8,128)(2,1)} %broadcast_select_fusion.4), channel_id=1, source_target_pairs={{0,8},{24,16},{1,9},{25,17},{2,10},{26,18},{3,11},{27,19},{4,12},{... | collective-permute-start | bytes 3145736 | tf_op jit(solution)/shard_map/ppermute | solution.py:56
  291.0 5.9 %shard_map.124.near = f32[1024,256]{1,0:T(8,128)} custom-call(s32[3]{0:T(128)} %pad_add_fusion.place, bf16[8,1024,768]{2,1,0:T(8,128)(2,1)} %bitcast.12, bf16[3072,256]{1,0:T(8,128)(2,1)} %maximum_select_fusion.5.near), custom_call_target="tpu_custom_call" | custom-call | flops 1048576 | bytes 65536 | tf_op jit(solution)/shard_map/pallas_call | solution.py:175
  296.9 8.7 %collective-permute-done.10 = bf16[2048,256]{1,0:T(8,128)(2,1)S(1)} collective-permute-done((bf16[2048,256]{1,0:T(8,128)(2,1)}, bf16[2048,256]{1,0:T(8,128)(2,1)S(1)}, u32[]{:S(2)}, u32[]{:S(2)}) %collective-permute-start.10) | collective-permute-done | bytes 1048608 | tf_op jit(solution)/shard_map/ppermute | solution.py:56
  310.3 13.5 %shard_map.125 = (f32[1024,768]{1,0:T(8,128)}, f32[1024,768]{1,0:T(8,128)}, bf16[4096,256]{1,0:T(8,128)(2,1)}) custom-call(s32[3]{0:T(128)} %pad_add_fusion.place, bf16[8,1024,768]{2,1,0:T(8,128)(2,1)} %bitcast.13, bf16[3072,256]{1,0:T(8,128)(2,1)} %collective-permute-done.11.middle, ...), custom_call_target="tpu_custom_call", output_to_operand_aliasing={{0}: (8, {}), {1}: (9, {})} | custom-call | flops 1048576 | bytes 65536 | tf_op jit(solution)/shard_map/pallas_call | solution.py:226
  335.6 18.6 %collective-permute-done.18 = bf16[1024,256]{1,0:T(8,128)(2,1)S(1)} collective-permute-done((bf16[1024,256]{1,0:T(8,128)(2,1)S(1)}, bf16[1024,256]{1,0:T(8,128)(2,1)S(1)}, u32[]{:S(2)}, u32[]{:S(2)}) %collective-permute-start.18) | collective-permute-done | bytes 524320 | tf_op jit(solution)/shard_map/ppermute | solution.py:56
  360.1 5.3 %collective-permute-done.17 = bf16[1024,256]{1,0:T(8,128)(2,1)S(1)} collective-permute-done((bf16[1024,256]{1,0:T(8,128)(2,1)S(1)}, bf16[1024,256]{1,0:T(8,128)(2,1)S(1)}, u32[]{:S(2)}, u32[]{:S(2)}) %collective-permute-start.17) | collective-permute-done | bytes 524320 | tf_op jit(solution)/shard_map/ppermute | solution.py:56
  365.6 10.6 %collective-permute-done.14 = bf16[1024,256]{1,0:T(8,128)(2,1)S(1)} collective-permute-done((bf16[1024,256]{1,0:T(8,128)(2,1)S(1)}, bf16[1024,256]{1,0:T(8,128)(2,1)S(1)}, u32[]{:S(2)}, u32[]{:S(2)}) %collective-permute-start.14) | collective-permute-done | bytes 524320 | tf_op jit(solution)/shard_map/ppermute | solution.py:56
  412.4 11.1 %collective-permute-done.22 = bf16[256,1536]{1,0:T(8,128)(2,1)S(1)} collective-permute-done((bf16[256,1536]{1,0:T(8,128)(2,1)S(1)}, bf16[256,1536]{1,0:T(8,128)(2,1)S(1)}, u32[]{:S(2)}, u32[]{:S(2)}) %collective-permute-start.22) | collective-permute-done | bytes 786464 | tf_op jit(solution)/shard_map/ppermute | solution.py:102
  429.3 16.4 %collective-permute-done.27 = bf16[256,1536]{1,0:T(8,128)(2,1)S(1)} collective-permute-done((bf16[256,1536]{1,0:T(8,128)(2,1)S(1)}, bf16[256,1536]{1,0:T(8,128)(2,1)S(1)}, u32[]{:S(2)}, u32[]{:S(2)}) %collective-permute-start.27) | collective-permute-done | bytes 786464 | tf_op jit(solution)/shard_map/ppermute | solution.py:102
  454.9 6.2 %collective-permute-done.29 = bf16[256,768]{1,0:T(8,128)(2,1)S(1)} collective-permute-done((bf16[256,768]{1,0:T(8,128)(2,1)S(1)}, bf16[256,768]{1,0:T(8,128)(2,1)S(1)}, u32[]{:S(2)}, u32[]{:S(2)}) %collective-permute-start.29) | collective-permute-done | bytes 393248 | tf_op jit(solution)/shard_map/ppermute | solution.py:102
  (151 shorter events, 125.4 us)
Async XLA Ops:
  7.2 76.4 %all-gather.4.cloned.1.call-start = ((), (), s32[]{:S(2)}) async-start(), calls=%async_computation.1 | async-start | bytes 9437184 | tf_op jit(solution)/shard_map/all_gather | solution.py:260
  7.9 216.3 %all-gather.6.cloned.1.call-start = ((), (), s32[]{:S(2)}) async-start(), calls=%async_computation.3 | async-start | bytes 14155776 | tf_op jit(solution)/shard_map/all_gather | solution.py:277
  8.0 40.6 %collective-permute-start.1 = (bf16[1024,768]{1,0:T(8,128)(2,1)}, bf16[1024,768]{1,0:T(8,128)(2,1)S(1)}, u32[]{:S(2)}, u32[]{:S(2)}) collective-permute-start(bf16[1024,768]{1,0:T(8,128)(2,1)} %param.9), channel_id=1, source_target_pairs={{0,24},{8,16},{16,8},{24,0},{1,25},{9,17},{17,9},{25,1},{2,26},{10... | collective-permute-start | bytes 4718600 | tf_op jit(solution)/shard_map/ppermute | solution.py:56
  13.1 68.5 %collective-permute-start = (bf16[1024,768]{1,0:T(8,128)(2,1)}, bf16[1024,768]{1,0:T(8,128)(2,1)}, u32[]{:S(2)}, u32[]{:S(2)}) collective-permute-start(bf16[1024,768]{1,0:T(8,128)(2,1)} %param.9), channel_id=1, source_target_pairs={{0,8},{8,0},{16,24},{24,16},{1,9},{9,1},{17,25},{25,17},{2,10},{10... | collective-permute-start | bytes 4718600 | tf_op jit(solution)/shard_map/ppermute | solution.py:56
  81.6 55.2 %collective-permute-start.5 = (bf16[1024,768]{1,0:T(8,128)(2,1)}, bf16[1024,768]{1,0:T(8,128)(2,1)}, u32[]{:S(2)}, u32[]{:S(2)}) collective-permute-start(bf16[1024,768]{1,0:T(8,128)(2,1)} %broadcast_select_fusion.3), channel_id=1, source_target_pairs={{0,16},{8,0},{16,24},{24,8},{1,17},{9,1},{17,25},{25,9},{2,18},{10... | collective-permute-start | bytes 4718600 | tf_op jit(solution)/shard_map/ppermute | solution.py:56
  93.8 41.2 %collective-permute-start.2 = (bf16[1536,256]{1,0:T(8,128)(2,1)S(1)}, bf16[1536,256]{1,0:T(8,128)(2,1)S(1)}, u32[]{:S(2)}, u32[]{:S(2)}) collective-permute-start(bf16[1536,256]{1,0:T(8,128)(2,1)S(1)} %copy-done.16), channel_id=1, source_target_pairs={{0,8},{8,0},{16,24},{24,16},{1,9},{9,1},{17,25},{25,17},{2,10},{10... | collective-permute-start | bytes 2359304 | tf_op jit(solution)/shard_map/ppermute | solution.py:56
  142.6 233.9 %reduce-scatter.2.cloned.1.call-start = ((), (), s32[]{:S(2)}) async-start(), calls=%async_computation.2 | async-start | bytes 9437184 | tf_op jit(solution)/shard_map/reduce_scatter | solution.py:287
  143.7 40.6 %collective-permute-start.3 = (bf16[3072,256]{1,0:T(8,128)(2,1)S(1)}, bf16[3072,256]{1,0:T(8,128)(2,1)}, u32[]{:S(2)}, u32[]{:S(2)}) collective-permute-start(bf16[3072,256]{1,0:T(8,128)(2,1)S(1)} %maximum_select_fusion.3.near), channel_id=1, source_target_pairs={{8,16},{16,8},{9,17},{17,9},{10,18},{18,10},{11,19},{19,11},{12,20... | collective-permute-start | bytes 4718600 | tf_op jit(solution)/shard_map/ppermute | solution.py:56
  184.3 36.2 %collective-permute-start.7 = (bf16[3072,256]{1,0:T(8,128)(2,1)}, bf16[3072,256]{1,0:T(8,128)(2,1)}, u32[]{:S(2)}, u32[]{:S(2)}) collective-permute-start(bf16[3072,256]{1,0:T(8,128)(2,1)} %collective-permute-done.3.middle), channel_id=1, source_target_pairs={{8,0},{16,24},{9,1},{17,25},{10,2},{18,26},{11,3},{19,27},{12,4},{... | collective-permute-start | bytes 4718600 | tf_op jit(solution)/shard_map/ppermute | solution.py:56
  185.7 34.8 %collective-permute-start.8 = (bf16[3072,256]{1,0:T(8,128)(2,1)S(1)}, bf16[3072,256]{1,0:T(8,128)(2,1)}, u32[]{:S(2)}, u32[]{:S(2)}) collective-permute-start(bf16[3072,256]{1,0:T(8,128)(2,1)S(1)} %maximum_select_fusion.4.near), channel_id=1, source_target_pairs={{8,16},{16,8},{9,17},{17,9},{10,18},{18,10},{11,19},{19,11},{12,20... | collective-permute-start | bytes 4718600 | tf_op jit(solution)/shard_map/ppermute | solution.py:56
  220.5 42.2 %collective-permute-start.9 = (bf16[3072,256]{1,0:T(8,128)(2,1)}, bf16[3072,256]{1,0:T(8,128)(2,1)S(1)}, u32[]{:S(2)}, u32[]{:S(2)}) collective-permute-start(bf16[3072,256]{1,0:T(8,128)(2,1)} %collective-permute-done.8.middle), channel_id=1, source_target_pairs={{8,0},{16,24},{9,1},{17,25},{10,2},{18,26},{11,3},{19,27},{12,4},{... | collective-permute-start | bytes 4718600 | tf_op jit(solution)/shard_map/ppermute | solution.py:56
  221.8 40.9 %collective-permute-start.11 = (bf16[3072,256]{1,0:T(8,128)(2,1)S(1)}, bf16[3072,256]{1,0:T(8,128)(2,1)}, u32[]{:S(2)}, u32[]{:S(2)}) collective-permute-start(bf16[3072,256]{1,0:T(8,128)(2,1)S(1)} %copy-done.7), channel_id=1, source_target_pairs={{8,16},{16,8},{9,17},{17,9},{10,18},{18,10},{11,19},{19,11},{12,20... | collective-permute-start | bytes 4718600 | tf_op jit(solution)/shard_map/ppermute | solution.py:56
  248.8 37.8 %collective-permute-start.15 = (bf16[2048,256]{1,0:T(8,128)(2,1)}, bf16[2048,256]{1,0:T(8,128)(2,1)}, u32[]{:S(2)}, u32[]{:S(2)}) collective-permute-start(bf16[2048,256]{1,0:T(8,128)(2,1)} %broadcast_select_fusion.5), channel_id=1, source_target_pairs={{0,8},{24,16},{1,9},{25,17},{2,10},{26,18},{3,11},{27,19},{4,12},{... | collective-permute-start | bytes 3145736 | tf_op jit(solution)/shard_map/ppermute | solution.py:56
  262.7 43.0 %collective-permute-start.12 = (bf16[3072,256]{1,0:T(8,128)(2,1)}, bf16[3072,256]{1,0:T(8,128)(2,1)}, u32[]{:S(2)}, u32[]{:S(2)}) collective-permute-start(bf16[3072,256]{1,0:T(8,128)(2,1)} %collective-permute-done.11.middle), channel_id=1, source_target_pairs={{8,0},{16,24},{9,1},{17,25},{10,2},{18,26},{11,3},{19,27},{12,4},{... | collective-permute-start | bytes 4718600 | tf_op jit(solution)/shard_map/ppermute | solution.py:56
  281.2 24.4 %collective-permute-start.10 = (bf16[2048,256]{1,0:T(8,128)(2,1)}, bf16[2048,256]{1,0:T(8,128)(2,1)S(1)}, u32[]{:S(2)}, u32[]{:S(2)}) collective-permute-start(bf16[2048,256]{1,0:T(8,128)(2,1)} %broadcast_select_fusion.4), channel_id=1, source_target_pairs={{0,8},{24,16},{1,9},{25,17},{2,10},{26,18},{3,11},{27,19},{4,12},{... | collective-permute-start | bytes 3145736 | tf_op jit(solution)/shard_map/ppermute | solution.py:56
  289.4 41.0 %collective-permute-start.16 = (bf16[2048,256]{1,0:T(8,128)(2,1)}, bf16[2048,256]{1,0:T(8,128)(2,1)}, u32[]{:S(2)}, u32[]{:S(2)}) collective-permute-start(bf16[2048,256]{1,0:T(8,128)(2,1)} %add_convert_fusion.3), channel_id=1, source_target_pairs={{8,16},{16,8},{9,17},{17,9},{10,18},{18,10},{11,19},{19,11},{12,20... | collective-permute-start | bytes 3145736 | tf_op jit(solution)/shard_map/ppermute | solution.py:56
  308.7 25.3 %collective-permute-start.13 = (bf16[2048,256]{1,0:T(8,128)(2,1)}, bf16[2048,256]{1,0:T(8,128)(2,1)}, u32[]{:S(2)}, u32[]{:S(2)}) collective-permute-start(bf16[2048,256]{1,0:T(8,128)(2,1)} %add_convert_fusion.4), channel_id=1, source_target_pairs={{8,16},{16,8},{9,17},{17,9},{10,18},{18,10},{11,19},{19,11},{12,20... | collective-permute-start | bytes 3145736 | tf_op jit(solution)/shard_map/ppermute | solution.py:56
  325.8 58.0 %collective-permute-start.20 = (bf16[1024,256]{1,0:T(8,128)(2,1)}, bf16[1024,256]{1,0:T(8,128)(2,1)}, u32[]{:S(2)}, u32[]{:S(2)}) collective-permute-start(bf16[1024,256]{1,0:T(8,128)(2,1)} %get-tuple-element.143), channel_id=1, source_target_pairs={{0,8},{8,0},{16,24},{24,16},{1,9},{9,1},{17,25},{25,17},{2,10},{10... | collective-permute-start | bytes 1572872 | tf_op jit(solution)/shard_map/ppermute | solution.py:56
  330.3 23.8 %collective-permute-start.18 = (bf16[1024,256]{1,0:T(8,128)(2,1)S(1)}, bf16[1024,256]{1,0:T(8,128)(2,1)S(1)}, u32[]{:S(2)}, u32[]{:S(2)}) collective-permute-start(bf16[1024,256]{1,0:T(8,128)(2,1)S(1)} %get-tuple-element.144), channel_id=1, source_target_pairs={{0,8},{8,24},{16,0},{24,16},{1,9},{9,25},{17,1},{25,17},{2,10},{10... | collective-permute-start | bytes 1572872 | tf_op jit(solution)/shard_map/ppermute | solution.py:56
  332.2 33.2 %collective-permute-start.17 = (bf16[1024,256]{1,0:T(8,128)(2,1)S(1)}, bf16[1024,256]{1,0:T(8,128)(2,1)S(1)}, u32[]{:S(2)}, u32[]{:S(2)}) collective-permute-start(bf16[1024,256]{1,0:T(8,128)(2,1)S(1)} %select_convert_fusion), channel_id=1, source_target_pairs={{0,8},{8,0},{16,24},{24,16},{1,9},{9,1},{17,25},{25,17},{2,10},{10... | collective-permute-start | bytes 1572872 | tf_op jit(solution)/shard_map/ppermute | solution.py:56
  354.3 21.9 %collective-permute-start.14 = (bf16[1024,256]{1,0:T(8,128)(2,1)S(1)}, bf16[1024,256]{1,0:T(8,128)(2,1)S(1)}, u32[]{:S(2)}, u32[]{:S(2)}) collective-permute-start(bf16[1024,256]{1,0:T(8,128)(2,1)S(1)} %select_convert_fusion.1), channel_id=1, source_target_pairs={{0,8},{8,0},{16,24},{24,16},{1,9},{9,1},{17,25},{25,17},{2,10},{10... | collective-permute-start | bytes 1572872 | tf_op jit(solution)/shard_map/ppermute | solution.py:56
  358.8 25.1 %collective-permute-start.19 = (bf16[1024,256]{1,0:T(8,128)(2,1)}, bf16[1024,256]{1,0:T(8,128)(2,1)}, u32[]{:S(2)}, u32[]{:S(2)}) collective-permute-start(bf16[1024,256]{1,0:T(8,128)(2,1)} %add_convert_fusion.6), channel_id=1, source_target_pairs={{0,24},{8,16},{16,8},{24,0},{1,25},{9,17},{17,9},{25,1},{2,26},{10... | collective-permute-start | bytes 1572872 | tf_op jit(solution)/shard_map/ppermute | solution.py:56
  427.3 27.3 %collective-permute-start.25 = (bf16[256,768]{1,0:T(8,128)(2,1)S(1)}, bf16[256,768]{1,0:T(8,128)(2,1)S(1)}, u32[]{:S(2)}, u32[]{:S(2)}) collective-permute-start(bf16[256,768]{1,0:T(8,128)(2,1)S(1)} %get-tuple-element.122), channel_id=1, source_target_pairs={{0,4},{1,5},{2,6},{3,7},{4,0},{5,1},{6,2},{7,3},{8,12},{9,13},{10,... | collective-permute-start | bytes 1179656 | tf_op jit(solution)/shard_map/ppermute | solution.py:102
  427.6 26.9 %collective-permute-start.26 = (bf16[256,768]{1,0:T(8,128)(2,1)S(1)}, bf16[256,768]{1,0:T(8,128)(2,1)S(1)}, u32[]{:S(2)}, u32[]{:S(2)}) collective-permute-start(bf16[256,768]{1,0:T(8,128)(2,1)S(1)} %get-tuple-element.123), channel_id=1, source_target_pairs={{0,2},{1,3},{2,0},{3,1},{4,6},{5,7},{6,4},{7,5},{8,10},{9,11},{10,... | collective-permute-start | bytes 1179656 | tf_op jit(solution)/shard_map/ppermute | solution.py:102
  (32 other events, 417.0 us)
Sparse Core Ops, SparseCore 0:
  9.9 57.0 all-gather.3
  142.7 71.3 all-gather.5
  220.6 73.5 reduce-scatter.1

commit v5 on v3

--- a/solution.py
+++ b/solution.py
@@ -80,14 +80,15 @@
 
 
 def products(rows, half, right, order, start):
-    height, depth = rows[0].shape[0] // 2, rows[0].shape[1]
+    height, depth = rows[-1].shape
     width = right[0].shape[0] // 8
     return pl.pallas_call(
         products_kernel,
         grid_spec=pltpu.PrefetchScalarGridSpec(
             num_scalar_prefetch=1,
             grid=(4,),
-            in_specs=[pl.BlockSpec((height, depth), lambda b, order: (half, 0))] * len(rows)
+            in_specs=[pl.BlockSpec((height, depth), lambda b, order: (half, 0))] * (len(rows) - 1)
+            + [pl.BlockSpec((height, depth), lambda b, order: (0, 0))]
             + [pl.BlockSpec((width, depth), lambda b, order: (order[start + b], 0))] * len(right),
             out_specs=pl.BlockSpec((height, width), lambda b, order: (0, b)),
         ),
@@ -97,13 +98,13 @@
     )(order, *rows, *right)
 
 
-def scatter_columns(rows, right, axis):
+def scatter_columns(rows, rows_low, rows_high, right, axis):
     def swap(x, bit):
         return lax.ppermute(x, axis, [(j, j ^ bit) for j in range(8)])
 
     order = lax.axis_index(axis) ^ jnp.array([0, 2, 4, 6, 1, 3, 5, 7], jnp.int32)
     width = right[0].shape[0] // 8
-    height = rows[0].shape[0] // 2
+    height = rows_low.shape[0]
     low, high = slice(0, height // 2), slice(height // 2, height)
 
     def pair_sum(half, rows):
@@ -127,10 +128,10 @@
         total = lambda a, b, c: a.astype(F32) + b[:, :width].astype(F32) + c.astype(F32)
         return [total(block(x, 0, low), by_x, then_y), total(block(x, 0, high), by_y, then_x)]
 
-    sum0 = pair_sum(0, rows)
+    sum0 = pair_sum(0, rows + [rows_low])
     by_x0, by_y0 = together(first_sends(sum0))
     by_x0, by_y0 = swap(by_x0, 2), swap(by_y0, 4)
-    sum1 = pair_sum(1, together(rows, sum0))
+    sum1 = pair_sum(1, rows + [rows_high(sum0)])
     then_y0, then_x0, by_x1, by_y1 = together(
         second_sends(sum0, *together([by_x0, by_y0], sum1)) + first_sends(sum1)
     )
@@ -292,8 +293,8 @@
     right1 = line.whole(near1, middle1, after(out1, far1))
     mine0, other0 = halves(line.even, stay0.astype(F32) + through0.astype(F32))
     other0 = other0.astype(BF16)
-    through1 = add(far1, got1)
-    moments2, back2 = next_part(2, near2, middle2, after(out2, other0, through1, right0, right1), moments1)
+    through1 = add(far1, after(got1, right0, right1))
+    moments2, back2 = next_part(2, near2, middle2, after(out2, through1), moments1)
     other0 = send(other0, PAIRS)
     turned0 = (mine0 + other0.astype(F32)).astype(BF16)
     through1 = send(through1, MIDDLE)
@@ -301,18 +302,35 @@
     turned1 = (mine1 + send(other1.astype(BF16), PAIRS).astype(F32)).astype(BF16)
     first_next, second_next = moments2
 
-    relay = send(line.block(back2, 2), RELAY_BACK)
-    pair = send(line.block(back2, 1), PAIRS)
-    relay = after(relay, through1, other0)
-    mirror = send(add(line.block(back2, 3), jnp.where(line.inner, relay, 0)), MIRROR)
-    right2 = line.whole(near2, middle2, after(out2, relay))
-    left_next = 0.95 * left_stat + 0.05 * after(product, relay).astype(F32)
-    mirror, pair = together([mirror, pair], right2)
-    turned2 = line.block(back2, 0).astype(F32) + jnp.where(line.inner, 0, relay).astype(F32)
-    turned2 = (turned2 + pair.astype(F32) + mirror.astype(F32)).astype(BF16)
-
-    right = together([right0, right1, right2], left_next)
-    direction = scatter_columns([turned0, turned1, turned2], right, "col")
+    low, high = [
+        [line.block(back2, bits)[h * height // 2 : (h + 1) * height // 2] for bits in range(4)] for h in range(2)
+    ]
+
+    def first_step(blocks):
+        return send(blocks[2], RELAY_BACK), send(blocks[1], PAIRS)
+
+    def second_step(blocks, relay):
+        return send(add(blocks[3], jnp.where(line.inner, relay, 0)), MIRROR)
+
+    def summed(blocks, relay, pair, mirror):
+        total = blocks[0].astype(F32) + jnp.where(line.inner, 0, relay).astype(F32)
+        return (total + pair.astype(F32) + mirror.astype(F32)).astype(BF16)
+
+    relay_low, pair_low = first_step(low)
+    relay_low = after(relay_low, through1)
+    mirror_low = second_step(low, relay_low)
+    relay_high, pair_high = first_step(together(high, relay_low))
+    right2 = line.whole(near2, middle2, after(out2, relay_high))
+    left_next = 0.95 * left_stat + 0.05 * after(product, relay_high).astype(F32)
+    to_mirror = add(high[3], jnp.where(line.inner, relay_high, 0))
+    mirror_high = send(to_mirror, MIRROR)
+    turned_low = summed(low, relay_low, pair_low, after(mirror_low, right2, left_next, to_mirror))
+
+    def turned_high(earlier):
+        return summed(high, relay_high, pair_high, after(mirror_high, earlier))
+
+    right = [right0, right1, right2]
+    direction = scatter_columns([turned0, turned1], turned_low, turned_high, right, "col")
     return (left_next, first_next, second_next, direction)
 
 

time: 463 us -> 469 us (1.013)
  other arithmetic: 38.7 us -> 43.5 us
  starting transfers between devices: 70.6 us -> 65.8 us
    ppermute x21 -> x24, waiting for transfers between devices: 182 us -> 184 us  [send(): return lax.ppermute(x, self.axis, pairs)]
    ppermute x21 -> x24, starting transfers between devices: 58.6 us -> 56.3 us  [send(): return lax.ppermute(x, self.axis, pairs)]
  transfers between devices with their start and end apart: 34 -> 37, of which waited for: 18 -> 16; matrix products, arithmetic and copies ran while one was open for 14% -> 15% of each run, Pallas kernels for 14% -> 14%
where the time goes in v5:
time: 469 us; the launch traced here: 461 us
  waiting for transfers between devices  227 us (48%)
  Pallas kernels  70.5 us (15%)
  starting transfers between devices  65.8 us (14%)
  other arithmetic  43.5 us (9%)
  matrix products  24.6 us (5%)
  between operations  14.8 us (3%)
  local copies, waits for them, and re-layouts  14.4 us (3%)
    ppermute x24, waiting for transfers between devices, send(): return lax.ppermute(x, self.axis, pairs)  184 us
    ppermute x24, starting transfers between devices, send(): return lax.ppermute(x, self.axis, pairs)  56.3 us
    pallas_call x3, Pallas kernels, part(): pl.pallas_call(part_kernel, grid_spec=pltpu.PrefetchScalarGridSpec(num_sc...  54.4 us
    ppermute x10, waiting for transfers between devices, swap(): return lax.ppermute(x, axis, [(j, j ^ bit) for j in range(8)])  42.7 us
    pallas_call x4, Pallas kernels, products(): pl.pallas_call(products_kernel, grid_spec=pltpu.PrefetchScalarGridSpec(nu...  16.1 us
    dot_general x4, matrix products, contract_first(): lax.dot_general(first, second, (((0,), (0,)), ((), ())), preferred_elemen...  15.6 us
    select_n x6, other arithmetic, joined(): jnp.where(keep_order, jnp.concatenate([first, second]), jnp.concatenate([...  10.6 us
  transfers between devices with their start and end apart: 37, of which 16 were waited for; matrix products, arithmetic and copies ran while one was open for 15% of the time, Pallas kernels for 14%

profile of v5, /device:TPU:0, one launch (start us, length us, event | category | flops | bytes accessed | tf_op | source)
XLA Modules:
  0.0 461.1 jit_solution(10415777663369843108)
XLA Ops:
  8.0 5.1 %collective-permute-start.1 = (bf16[1024,768]{1,0:T(8,128)(2,1)}, bf16[1024,768]{1,0:T(8,128)(2,1)S(1)}, u32[]{:S(2)}, u32[]{:S(2)}) collective-permute-start(bf16[1024,768]{1,0:T(8,128)(2,1)} %param.9), channel_id=1, source_target_pairs={{0,24},{8,16},{16,8},{24,0},{1,25},{9,17},{17,9},{25,1},{2,26},{10... | collective-permute-start | bytes 4718600 | tf_op jit(solution)/shard_map/ppermute | solution.py:56
  16.2 32.4 %collective-permute-done.1 = bf16[1024,768]{1,0:T(8,128)(2,1)S(1)} collective-permute-done((bf16[1024,768]{1,0:T(8,128)(2,1)}, bf16[1024,768]{1,0:T(8,128)(2,1)S(1)}, u32[]{:S(2)}, u32[]{:S(2)}) %collective-permute-start.1) | collective-permute-done | bytes 1572896 | tf_op jit(solution)/shard_map/ppermute | solution.py:56
  50.0 31.5 %collective-permute-done = bf16[1024,768]{1,0:T(8,128)(2,1)} collective-permute-done((bf16[1024,768]{1,0:T(8,128)(2,1)}, bf16[1024,768]{1,0:T(8,128)(2,1)}, u32[]{:S(2)}, u32[]{:S(2)}) %collective-permute-start) | collective-permute-done | bytes 1572896 | tf_op jit(solution)/shard_map/ppermute | solution.py:56
  83.6 4.1 fusion.4
  93.9 41.1 %collective-permute-done.3 = bf16[1536,256]{1,0:T(8,128)(2,1)S(1)} collective-permute-done((bf16[1536,256]{1,0:T(8,128)(2,1)S(1)}, bf16[1536,256]{1,0:T(8,128)(2,1)S(1)}, u32[]{:S(2)}, u32[]{:S(2)}) %collective-permute-start.3) | collective-permute-done | bytes 786464 | tf_op jit(solution)/shard_map/ppermute | solution.py:56
  135.4 5.7 %add_convert_fusion.2 = bf16[1024,768]{1,0:T(8,128)(2,1)} fusion(f32[1024,768]{1,0:T(8,128)S(1)} %copy-done.31, bf16[1024,768]{1,0:T(8,128)(2,1)} %collective-permute-done.2, bf16[4096,1024]{1,0:T(8,128)(2,1)} %all-gather.4.cloned.1.call-done.basis, s32[]{:T(128)S(6)} %select_n.160), kind=kOutput, calls=%fused_computation.6 | convolution fusion | flops 1612185600 | bytes 8388612 | tf_op jit(solution)/shard_map/dot_general | solution.py:27
  144.1 15.8 %collective-permute-done.4 = bf16[1536,256]{1,0:T(8,128)(2,1)S(1)} collective-permute-done((bf16[1536,256]{1,0:T(8,128)(2,1)S(1)}, bf16[1536,256]{1,0:T(8,128)(2,1)S(1)}, u32[]{:S(2)}, u32[]{:S(2)}) %collective-permute-start.4) | collective-permute-done | bytes 786464 | tf_op jit(solution)/shard_map/ppermute | solution.py:56
  161.7 17.5 %collective-permute-done.5 = bf16[1536,256]{1,0:T(8,128)(2,1)S(1)} collective-permute-done((bf16[1536,256]{1,0:T(8,128)(2,1)S(1)}, bf16[1536,256]{1,0:T(8,128)(2,1)S(1)}, u32[]{:S(2)}, u32[]{:S(2)}) %collective-permute-start.5) | collective-permute-done | bytes 786464 | tf_op jit(solution)/shard_map/ppermute | solution.py:56
  189.0 9.1 %convolution_convert_fusion = bf16[4096,1024]{1,0:T(8,128)(2,1)} fusion(bf16[4096,768]{1,0:T(8,128)(2,1)S(1)} %constant_dynamic-update-slice_fusion, bf16[1024,768]{1,0:T(8,128)(2,1)S(1)} %copy-done.20), kind=kOutput, calls=%fused_computation | convolution fusion | flops 6446645248 | bytes 16252928 | tf_op jit(solution)/shard_map/dot_general | solution.py:23
  198.1 19.2 %collective-permute-done.7.out = bf16[3072,256]{1,0:T(8,128)(2,1)S(1)} collective-permute-done((bf16[3072,256]{1,0:T(8,128)(2,1)}, bf16[3072,256]{1,0:T(8,128)(2,1)S(1)}, u32[]{:S(2)}, u32[]{:S(2)}) %collective-permute-start.7) | collective-permute-done | bytes 1572896 | tf_op jit(solution)/shard_map/ppermute | solution.py:56
  222.2 19.8 %shard_map.120 = (f32[1024,768]{1,0:T(8,128)}, f32[1024,768]{1,0:T(8,128)}, bf16[4096,256]{1,0:T(8,128)(2,1)}) custom-call(s32[3]{0:T(128)} %pad_add_fusion.place, bf16[8,1024,768]{2,1,0:T(8,128)(2,1)} %bitcast.8, bf16[3072,256]{1,0:T(8,128)(2,1)} %copy-done.9, bf16[3072,256]{1,0:T(8,128)(2,1)} %collective-permute-done.6.middle, ...), custom_call_target="tpu_custom_call" | custom-call | flops 1048576 | bytes 65536 | tf_op jit(solution)/shard_map/pallas_call | solution.py:208
  244.6 6.1 %collective-permute-start.12 = (bf16[2048,256]{1,0:T(8,128)(2,1)}, bf16[2048,256]{1,0:T(8,128)(2,1)}, u32[]{:S(2)}, u32[]{:S(2)}) collective-permute-start(bf16[2048,256]{1,0:T(8,128)(2,1)} %broadcast_select_fusion.5), channel_id=1, source_target_pairs={{0,8},{24,16},{1,9},{25,17},{2,10},{26,18},{3,11},{27,19},{4,12},{... | collective-permute-start | bytes 3145736 | tf_op jit(solution)/shard_map/ppermute | solution.py:56
  255.0 17.6 %shard_map.121 = (f32[1024,768]{1,0:T(8,128)}, f32[1024,768]{1,0:T(8,128)}, bf16[4096,256]{1,0:T(8,128)(2,1)}) custom-call(s32[3]{0:T(128)} %pad_add_fusion.place, bf16[8,1024,768]{2,1,0:T(8,128)(2,1)} %bitcast.9, bf16[3072,256]{1,0:T(8,128)(2,1)} %maximum_select_fusion.4.near, ...), custom_call_target="tpu_custom_call", output_to_operand_aliasing={{0}: (8, {}), {1}: (9, {})} | custom-call | flops 1048576 | bytes 65536 | tf_op jit(solution)/shard_map/pallas_call | solution.py:208
  274.3 6.7 %collective-permute-start.13 = (bf16[2048,256]{1,0:T(8,128)(2,1)S(1)}, bf16[2048,256]{1,0:T(8,128)(2,1)S(1)}, u32[]{:S(2)}, u32[]{:S(2)}) collective-permute-start(bf16[2048,256]{1,0:T(8,128)(2,1)S(1)} %broadcast_select_fusion.4), channel_id=1, source_target_pairs={{0,8},{24,16},{1,9},{25,17},{2,10},{26,18},{3,11},{27,19},{4,12},{... | collective-permute-start | bytes 3145736 | tf_op jit(solution)/shard_map/ppermute | solution.py:56
  288.8 10.3 %collective-permute-done.13 = bf16[2048,256]{1,0:T(8,128)(2,1)S(1)} collective-permute-done((bf16[2048,256]{1,0:T(8,128)(2,1)S(1)}, bf16[2048,256]{1,0:T(8,128)(2,1)S(1)}, u32[]{:S(2)}, u32[]{:S(2)}) %collective-permute-start.13) | collective-permute-done | bytes 1048608 | tf_op jit(solution)/shard_map/ppermute | solution.py:56
  304.9 12.8 %collective-permute-start.18 = (bf16[1024,256]{1,0:T(8,128)(2,1)}, bf16[1024,256]{1,0:T(8,128)(2,1)}, u32[]{:S(2)}, u32[]{:S(2)}) collective-permute-start(bf16[1024,256]{1,0:T(8,128)(2,1)} %select_convert_fusion.1), channel_id=1, source_target_pairs={{0,8},{8,0},{16,24},{24,16},{1,9},{9,1},{17,25},{25,17},{2,10},{10... | collective-permute-start | bytes 1572872 | tf_op jit(solution)/shard_map/ppermute | solution.py:56
  317.7 17.0 %shard_map.122 = (f32[1024,768]{1,0:T(8,128)}, f32[1024,768]{1,0:T(8,128)}, bf16[4096,256]{1,0:T(8,128)(2,1)}) custom-call(s32[3]{0:T(128)} %pad_add_fusion.place, bf16[8,1024,768]{2,1,0:T(8,128)(2,1)} %bitcast.10, bf16[3072,256]{1,0:T(8,128)(2,1)} %copy-done.7, ...), custom_call_target="tpu_custom_call", output_to_operand_aliasing={{0}: (8, {}), {1}: (9, {})} | custom-call | flops 1048576 | bytes 65536 | tf_op jit(solution)/shard_map/pallas_call | solution.py:208
  341.5 6.4 %collective-permute-done.14 = bf16[512,256]{1,0:T(8,128)(2,1)S(1)} collective-permute-done((bf16[512,256]{1,0:T(8,128)(2,1)S(1)}, bf16[512,256]{1,0:T(8,128)(2,1)S(1)}, u32[]{:S(2)}, u32[]{:S(2)}) %collective-permute-start.14) | collective-permute-done | bytes 262176 | tf_op jit(solution)/shard_map/ppermute | solution.py:56
  369.4 4.0 shard_map.123
  381.9 7.1 %collective-permute-done.26 = bf16[512,256]{1,0:T(8,128)(2,1)S(1)} collective-permute-done((bf16[512,256]{1,0:T(8,128)(2,1)S(1)}, bf16[512,256]{1,0:T(8,128)(2,1)S(1)}, u32[]{:S(2)}, u32[]{:S(2)}) %collective-permute-start.26) | collective-permute-done | bytes 262176 | tf_op jit(solution)/shard_map/ppermute | solution.py:56
  402.5 12.1 %collective-permute-done.23 = bf16[256,1536]{1,0:T(8,128)(2,1)S(1)} collective-permute-done((bf16[256,1536]{1,0:T(8,128)(2,1)S(1)}, bf16[256,1536]{1,0:T(8,128)(2,1)S(1)}, u32[]{:S(2)}, u32[]{:S(2)}) %collective-permute-start.23) | collective-permute-done | bytes 786464 | tf_op jit(solution)/shard_map/ppermute | solution.py:103
  420.5 16.4 %collective-permute-done.30 = bf16[256,1536]{1,0:T(8,128)(2,1)S(1)} collective-permute-done((bf16[256,1536]{1,0:T(8,128)(2,1)S(1)}, bf16[256,1536]{1,0:T(8,128)(2,1)S(1)}, u32[]{:S(2)}, u32[]{:S(2)}) %collective-permute-start.30) | collective-permute-done | bytes 786464 | tf_op jit(solution)/shard_map/ppermute | solution.py:103
  439.9 5.8 %collective-permute-done.28 = bf16[256,768]{1,0:T(8,128)(2,1)S(1)} collective-permute-done((bf16[256,768]{1,0:T(8,128)(2,1)S(1)}, bf16[256,768]{1,0:T(8,128)(2,1)S(1)}, u32[]{:S(2)}, u32[]{:S(2)}) %collective-permute-start.28) | collective-permute-done | bytes 393248 | tf_op jit(solution)/shard_map/ppermute | solution.py:103
  446.1 6.5 %collective-permute-done.32 = bf16[256,768]{1,0:T(8,128)(2,1)S(1)} collective-permute-done((bf16[256,768]{1,0:T(8,128)(2,1)S(1)}, bf16[256,768]{1,0:T(8,128)(2,1)S(1)}, u32[]{:S(2)}, u32[]{:S(2)}) %collective-permute-start.32) | collective-permute-done | bytes 393248 | tf_op jit(solution)/shard_map/ppermute | solution.py:103
  (176 shorter events, 116.1 us)
Async XLA Ops:
  7.2 76.4 %all-gather.4.cloned.1.call-start = ((), (), s32[]{:S(2)}) async-start(), calls=%async_computation.1 | async-start | bytes 9437184 | tf_op jit(solution)/shard_map/all_gather | solution.py:242
  7.9 214.3 %all-gather.6.cloned.1.call-start = ((), (), s32[]{:S(2)}) async-start(), calls=%async_computation.3 | async-start | bytes 14155776 | tf_op jit(solution)/shard_map/all_gather | solution.py:259
  8.0 40.6 %collective-permute-start.1 = (bf16[1024,768]{1,0:T(8,128)(2,1)}, bf16[1024,768]{1,0:T(8,128)(2,1)S(1)}, u32[]{:S(2)}, u32[]{:S(2)}) collective-permute-start(bf16[1024,768]{1,0:T(8,128)(2,1)} %param.9), channel_id=1, source_target_pairs={{0,24},{8,16},{16,8},{24,0},{1,25},{9,17},{17,9},{25,1},{2,26},{10... | collective-permute-start | bytes 4718600 | tf_op jit(solution)/shard_map/ppermute | solution.py:56
  13.1 68.5 %collective-permute-start = (bf16[1024,768]{1,0:T(8,128)(2,1)}, bf16[1024,768]{1,0:T(8,128)(2,1)}, u32[]{:S(2)}, u32[]{:S(2)}) collective-permute-start(bf16[1024,768]{1,0:T(8,128)(2,1)} %param.9), channel_id=1, source_target_pairs={{0,8},{8,0},{16,24},{24,16},{1,9},{9,1},{17,25},{25,17},{2,10},{10... | collective-permute-start | bytes 4718600 | tf_op jit(solution)/shard_map/ppermute | solution.py:56
  81.6 53.8 %collective-permute-start.2 = (bf16[1024,768]{1,0:T(8,128)(2,1)}, bf16[1024,768]{1,0:T(8,128)(2,1)}, u32[]{:S(2)}, u32[]{:S(2)}) collective-permute-start(bf16[1024,768]{1,0:T(8,128)(2,1)} %broadcast_select_fusion.3), channel_id=1, source_target_pairs={{0,16},{8,0},{16,24},{24,8},{1,17},{9,1},{17,25},{25,9},{2,18},{10... | collective-permute-start | bytes 4718600 | tf_op jit(solution)/shard_map/ppermute | solution.py:56
  93.8 41.2 %collective-permute-start.3 = (bf16[1536,256]{1,0:T(8,128)(2,1)S(1)}, bf16[1536,256]{1,0:T(8,128)(2,1)S(1)}, u32[]{:S(2)}, u32[]{:S(2)}) collective-permute-start(bf16[1536,256]{1,0:T(8,128)(2,1)S(1)} %copy-done.25), channel_id=1, source_target_pairs={{0,8},{8,0},{16,24},{24,16},{1,9},{9,1},{17,25},{25,17},{2,10},{10... | collective-permute-start | bytes 2359304 | tf_op jit(solution)/shard_map/ppermute | solution.py:56
  141.1 220.6 %reduce-scatter.2.cloned.1.call-start = ((), (), s32[]{:S(2)}) async-start(), calls=%async_computation.2 | async-start | bytes 9437184 | tf_op jit(solution)/shard_map/reduce_scatter | solution.py:269
  142.3 38.8 %collective-permute-start.6 = (bf16[3072,256]{1,0:T(8,128)(2,1)S(1)}, bf16[3072,256]{1,0:T(8,128)(2,1)}, u32[]{:S(2)}, u32[]{:S(2)}) collective-permute-start(bf16[3072,256]{1,0:T(8,128)(2,1)S(1)} %maximum_select_fusion.3.near), channel_id=1, source_target_pairs={{8,16},{16,8},{9,17},{17,9},{10,18},{18,10},{11,19},{19,11},{12,20... | collective-permute-start | bytes 4718600 | tf_op jit(solution)/shard_map/ppermute | solution.py:56
  181.1 36.1 %collective-permute-start.7 = (bf16[3072,256]{1,0:T(8,128)(2,1)}, bf16[3072,256]{1,0:T(8,128)(2,1)S(1)}, u32[]{:S(2)}, u32[]{:S(2)}) collective-permute-start(bf16[3072,256]{1,0:T(8,128)(2,1)} %collective-permute-done.6.middle), channel_id=1, source_target_pairs={{8,0},{16,24},{9,1},{17,25},{10,2},{18,26},{11,3},{19,27},{12,4},{... | collective-permute-start | bytes 4718600 | tf_op jit(solution)/shard_map/ppermute | solution.py:56
  182.7 34.5 %collective-permute-start.8 = (bf16[3072,256]{1,0:T(8,128)(2,1)}, bf16[3072,256]{1,0:T(8,128)(2,1)}, u32[]{:S(2)}, u32[]{:S(2)}) collective-permute-start(bf16[3072,256]{1,0:T(8,128)(2,1)} %maximum_select_fusion.4.near), channel_id=1, source_target_pairs={{8,16},{16,8},{9,17},{17,9},{10,18},{18,10},{11,19},{19,11},{12,20... | collective-permute-start | bytes 4718600 | tf_op jit(solution)/shard_map/ppermute | solution.py:56
  218.4 35.0 %collective-permute-start.10 = (bf16[3072,256]{1,0:T(8,128)(2,1)}, bf16[3072,256]{1,0:T(8,128)(2,1)S(1)}, u32[]{:S(2)}, u32[]{:S(2)}) collective-permute-start(bf16[3072,256]{1,0:T(8,128)(2,1)} %collective-permute-done.8.middle), channel_id=1, source_target_pairs={{8,0},{16,24},{9,1},{17,25},{10,2},{18,26},{11,3},{19,27},{12,4},{... | collective-permute-start | bytes 4718600 | tf_op jit(solution)/shard_map/ppermute | solution.py:56
  219.7 33.8 %collective-permute-start.9 = (bf16[3072,256]{1,0:T(8,128)(2,1)S(1)}, bf16[3072,256]{1,0:T(8,128)(2,1)}, u32[]{:S(2)}, u32[]{:S(2)}) collective-permute-start(bf16[3072,256]{1,0:T(8,128)(2,1)S(1)} %maximum_select_fusion.5.near), channel_id=1, source_target_pairs={{8,16},{16,8},{9,17},{17,9},{10,18},{18,10},{11,19},{19,11},{12,20... | collective-permute-start | bytes 4718600 | tf_op jit(solution)/shard_map/ppermute | solution.py:56
  244.6 27.9 %collective-permute-start.12 = (bf16[2048,256]{1,0:T(8,128)(2,1)}, bf16[2048,256]{1,0:T(8,128)(2,1)}, u32[]{:S(2)}, u32[]{:S(2)}) collective-permute-start(bf16[2048,256]{1,0:T(8,128)(2,1)} %broadcast_select_fusion.5), channel_id=1, source_target_pairs={{0,8},{24,16},{1,9},{25,17},{2,10},{26,18},{3,11},{27,19},{4,12},{... | collective-permute-start | bytes 3145736 | tf_op jit(solution)/shard_map/ppermute | solution.py:56
  253.4 64.3 %collective-permute-start.11 = (bf16[3072,256]{1,0:T(8,128)(2,1)}, bf16[3072,256]{1,0:T(8,128)(2,1)}, u32[]{:S(2)}, u32[]{:S(2)}) collective-permute-start(bf16[3072,256]{1,0:T(8,128)(2,1)} %collective-permute-done.9.middle), channel_id=1, source_target_pairs={{8,0},{16,24},{9,1},{17,25},{10,2},{18,26},{11,3},{19,27},{12,4},{... | collective-permute-start | bytes 4718600 | tf_op jit(solution)/shard_map/ppermute | solution.py:56
  274.3 24.7 %collective-permute-start.13 = (bf16[2048,256]{1,0:T(8,128)(2,1)S(1)}, bf16[2048,256]{1,0:T(8,128)(2,1)S(1)}, u32[]{:S(2)}, u32[]{:S(2)}) collective-permute-start(bf16[2048,256]{1,0:T(8,128)(2,1)S(1)} %broadcast_select_fusion.4), channel_id=1, source_target_pairs={{0,8},{24,16},{1,9},{25,17},{2,10},{26,18},{3,11},{27,19},{4,12},{... | collective-permute-start | bytes 3145736 | tf_op jit(solution)/shard_map/ppermute | solution.py:56
  300.5 47.4 %collective-permute-start.15 = (bf16[2048,256]{1,0:T(8,128)(2,1)}, bf16[2048,256]{1,0:T(8,128)(2,1)}, u32[]{:S(2)}, u32[]{:S(2)}) collective-permute-start(bf16[2048,256]{1,0:T(8,128)(2,1)} %add_convert_fusion.4), channel_id=1, source_target_pairs={{8,16},{16,8},{9,17},{17,9},{10,18},{18,10},{11,19},{19,11},{12,20... | collective-permute-start | bytes 3145736 | tf_op jit(solution)/shard_map/ppermute | solution.py:56
  304.9 34.5 %collective-permute-start.18 = (bf16[1024,256]{1,0:T(8,128)(2,1)}, bf16[1024,256]{1,0:T(8,128)(2,1)}, u32[]{:S(2)}, u32[]{:S(2)}) collective-permute-start(bf16[1024,256]{1,0:T(8,128)(2,1)} %select_convert_fusion.1), channel_id=1, source_target_pairs={{0,8},{8,0},{16,24},{24,16},{1,9},{9,1},{17,25},{25,17},{2,10},{10... | collective-permute-start | bytes 1572872 | tf_op jit(solution)/shard_map/ppermute | solution.py:56
  337.2 29.7 %collective-permute-start.20 = (bf16[512,256]{1,0:T(8,128)(2,1)}, bf16[512,256]{1,0:T(8,128)(2,1)}, u32[]{:S(2)}, u32[]{:S(2)}) collective-permute-start(bf16[512,256]{1,0:T(8,128)(2,1)} %get-tuple-element.131), channel_id=1, source_target_pairs={{0,8},{8,0},{16,24},{24,16},{1,9},{9,1},{17,25},{25,17},{2,10},{10... | collective-permute-start | bytes 786440 | tf_op jit(solution)/shard_map/ppermute | solution.py:56
  394.4 20.2 %collective-permute-start.23 = (bf16[256,1536]{1,0:T(8,128)(2,1)S(1)}, bf16[256,1536]{1,0:T(8,128)(2,1)S(1)}, u32[]{:S(2)}, u32[]{:S(2)}) collective-permute-start(bf16[256,1536]{1,0:T(8,128)(2,1)S(1)} %pad_maximum_fusion.1), channel_id=1, source_target_pairs={{0,2},{1,3},{2,0},{3,1},{4,6},{5,7},{6,4},{7,5},{8,10},{9,11},{10,... | collective-permute-start | bytes 2359304 | tf_op jit(solution)/shard_map/ppermute | solution.py:103
  396.5 19.7 %collective-permute-start.24 = (bf16[256,1536]{1,0:T(8,128)(2,1)S(1)}, bf16[256,1536]{1,0:T(8,128)(2,1)S(1)}, u32[]{:S(2)}, u32[]{:S(2)}) collective-permute-start(bf16[256,1536]{1,0:T(8,128)(2,1)S(1)} %concatenate.73), channel_id=1, source_target_pairs={{0,4},{1,5},{2,6},{3,7},{4,0},{5,1},{6,2},{7,3},{8,12},{9,13},{10,... | collective-permute-start | bytes 2359304 | tf_op jit(solution)/shard_map/ppermute | solution.py:103
  416.4 20.5 %collective-permute-start.30 = (bf16[256,1536]{1,0:T(8,128)(2,1)S(1)}, bf16[256,1536]{1,0:T(8,128)(2,1)S(1)}, u32[]{:S(2)}, u32[]{:S(2)}) collective-permute-start(bf16[256,1536]{1,0:T(8,128)(2,1)S(1)} %pad_maximum_fusion.2), channel_id=1, source_target_pairs={{0,2},{1,3},{2,0},{3,1},{4,6},{5,7},{6,4},{7,5},{8,10},{9,11},{10,... | collective-permute-start | bytes 2359304 | tf_op jit(solution)/shard_map/ppermute | solution.py:103
  416.8 20.5 %collective-permute-start.31 = (bf16[256,1536]{1,0:T(8,128)(2,1)S(1)}, bf16[256,1536]{1,0:T(8,128)(2,1)S(1)}, u32[]{:S(2)}, u32[]{:S(2)}) collective-permute-start(bf16[256,1536]{1,0:T(8,128)(2,1)S(1)} %concatenate.74), channel_id=1, source_target_pairs={{0,4},{1,5},{2,6},{3,7},{4,0},{5,1},{6,2},{7,3},{8,12},{9,13},{10,... | collective-permute-start | bytes 2359304 | tf_op jit(solution)/shard_map/ppermute | solution.py:103
  418.5 27.2 %collective-permute-start.28 = (bf16[256,768]{1,0:T(8,128)(2,1)S(1)}, bf16[256,768]{1,0:T(8,128)(2,1)S(1)}, u32[]{:S(2)}, u32[]{:S(2)}) collective-permute-start(bf16[256,768]{1,0:T(8,128)(2,1)S(1)} %get-tuple-element.110), channel_id=1, source_target_pairs={{0,4},{1,5},{2,6},{3,7},{4,0},{5,1},{6,2},{7,3},{8,12},{9,13},{10,... | collective-permute-start | bytes 1179656 | tf_op jit(solution)/shard_map/ppermute | solution.py:103
  418.8 26.9 %collective-permute-start.29 = (bf16[256,768]{1,0:T(8,128)(2,1)S(1)}, bf16[256,768]{1,0:T(8,128)(2,1)S(1)}, u32[]{:S(2)}, u32[]{:S(2)}) collective-permute-start(bf16[256,768]{1,0:T(8,128)(2,1)S(1)} %get-tuple-element.111), channel_id=1, source_target_pairs={{0,2},{1,3},{2,0},{3,1},{4,6},{5,7},{6,4},{7,5},{8,10},{9,11},{10,... | collective-permute-start | bytes 1179656 | tf_op jit(solution)/shard_map/ppermute | solution.py:103
  (45 other events, 521.6 us)
Sparse Core Ops, SparseCore 0:
  9.9 57.0 all-gather.3
  141.3 71.3 all-gather.5
  217.4 72.8 reduce-scatter.1

commit v6 on v3

--- a/solution.py
+++ b/solution.py
@@ -1,3 +1,5 @@
+import functools
+
 import jax
 import jax.numpy as jnp
 from jax import lax
@@ -154,8 +156,8 @@
 STEPS = 2
 
 
-def part_kernel(place, left, near, middle, out, first, second, basis, *rest):
-    first_out, second_out, back, total, normalized = rest[-5:]
+def part_kernel(place, left, near, middle, out, first, second, basis, *rest, results):
+    first_out, second_out, *backs, total, normalized = rest[-4 - results :]
     step = pl.program_id(0)
 
     @pl.when(step == 0)
@@ -185,16 +187,18 @@
     def _():
         first_out[...], second_out[...], normalized[...] = moments(total[...], first[...], second[...])
 
-    @pl.when(step >= 2 * STEPS)
-    def _():
-        back[...] = jnp.dot(basis[...], normalized[...], preferred_element_type=F32).astype(BF16)
-
-
-def part(number, place, left_rotated, near, middle, out, first_moment, second_moment, left_cols, before):
+    for number, back in enumerate(backs):
+
+        @pl.when(step == 2 * STEPS + number)
+        def _(back=back):
+            back[...] = jnp.dot(basis[...], normalized[...], preferred_element_type=F32).astype(BF16)
+
+
+def part(number, place, results, left_rotated, near, middle, out, first_moment, second_moment, left_cols, before):
     height, width = first_moment.shape
     size = near.shape[1]
     deep = near.shape[0] // STEPS
-    tall = left_cols.shape[0] // 2
+    tall = left_cols.shape[0] // results
     near_step = lambda s: jnp.minimum(s, STEPS - 1)
     far_step = lambda s: jnp.clip(s - STEPS, 0, STEPS - 1)
     last_step = lambda s: jnp.maximum(s - 2 * STEPS, 0)
@@ -204,11 +208,11 @@
 
     moment = pl.BlockSpec((height, size), lambda s, place: (0, number))
     before = list(before)
-    return pl.pallas_call(
-        part_kernel,
+    first_next, second_next, *backs = pl.pallas_call(
+        functools.partial(part_kernel, results=results),
         grid_spec=pltpu.PrefetchScalarGridSpec(
             num_scalar_prefetch=1,
-            grid=(2 * STEPS + 2,),
+            grid=(2 * STEPS + results,),
             in_specs=[
                 pl.BlockSpec((4 // STEPS, height, width), left_block),
                 pl.BlockSpec((deep, size), lambda s, place: (near_step(s), 0)),
@@ -216,21 +220,19 @@
                 pl.BlockSpec((deep, size), lambda s, place: (far_step(s) * (1 - place[2]), 0)),
                 moment,
                 moment,
-                pl.BlockSpec((tall, height), lambda s, place: (last_step(s), 0)),
+                pl.BlockSpec((tall, height), lambda s, place: (place[3 + last_step(s)], 0)),
             ]
             + [pl.BlockSpec(memory_space=pl.ANY)] * len(before),
-            out_specs=[moment, moment, pl.BlockSpec((tall, size), lambda s, place: (last_step(s), 0))],
+            out_specs=[moment, moment] + [pl.BlockSpec((tall, size), lambda s, place: (0, 0))] * results,
             scratch_shapes=[pltpu.VMEM((height, size), F32), pltpu.VMEM((height, size), BF16)],
         ),
-        out_shape=[
-            jax.ShapeDtypeStruct((height, width), F32),
-            jax.ShapeDtypeStruct((height, width), F32),
-            jax.ShapeDtypeStruct((left_cols.shape[0], size), BF16),
-        ],
+        out_shape=[jax.ShapeDtypeStruct((height, width), F32)] * 2
+        + [jax.ShapeDtypeStruct((tall, size), BF16)] * results,
         input_output_aliases={8: 0, 9: 1} if before else {},
         compiler_params=pltpu.CompilerParams(vmem_limit_bytes=VMEM),
         cost_estimate=QUICK,
     )(place, left_rotated, near, middle, out, first_moment, second_moment, left_cols, *before)
+    return (first_next, second_next), backs
 
 
 def body_on_line(gradient, left_stat, left_basis, right_basis, first_moment, second_moment):
@@ -271,29 +273,29 @@
     out1 = send(middle1, OUTWARD)
     middle2 = send(near2, MIDDLE)
 
-    steps = jnp.where(line.lower, jnp.array([0, STEPS]), jnp.array([STEPS, 0]))
-    place = jnp.concatenate([steps, line.inner[None]]).astype(jnp.int32)
+    halves_first = jnp.where(line.lower, jnp.array([0, STEPS]), jnp.array([STEPS, 0]))
+    far_near = jnp.where(line.lower, jnp.array([1, 0]), jnp.array([0, 1]))
+    place = jnp.concatenate([halves_first, line.inner[None]]).astype(jnp.int32)
+    to_halves = jnp.concatenate([place, far_near]).astype(jnp.int32)
+    to_blocks = jnp.concatenate([place, line.i ^ jnp.array([2, 1, 3, 0])]).astype(jnp.int32)
 
     def next_part(number, near, middle, out, before):
-        *before, back = part(
-            number, place, left_rotated, near, middle, out, first_moment, second_moment, left_cols, before
+        order, results = (to_blocks, 4) if number == 2 else (to_halves, 2)
+        return part(
+            number, order, results, left_rotated, near, middle, out, first_moment, second_moment, left_cols, before
         )
-        return before, back
-
-    moments0, back0 = next_part(0, near0, middle0, after(out0, near2), ())
-    stay0, far0 = halves(line.lower, back0)
+
+    moments0, (far0, stay0) = next_part(0, near0, middle0, after(out0, near2), ())
     got0 = send(far0, INWARD)
     out2 = send(after(middle2, out1, far0), OUTWARD)
-    moments1, back1 = next_part(1, near1, middle1, after(out1, far0), moments0)
-    stay1, far1 = halves(line.lower, after(back1, got0))
+    moments1, (far1, stay1) = next_part(1, near1, middle1, after(out1, far0), moments0)
     got1 = send(far1, INWARD)
     through0 = send(add(far0, after(got0, far1)), MIDDLE)
-    right0 = line.whole(near0, middle0, after(out0, far1))
-    right1 = line.whole(near1, middle1, after(out1, far1))
     mine0, other0 = halves(line.even, stay0.astype(F32) + through0.astype(F32))
     other0 = other0.astype(BF16)
+    got1, out2 = together([got1, out2])
     through1 = add(far1, got1)
-    moments2, back2 = next_part(2, near2, middle2, after(out2, other0, through1, right0, right1), moments1)
+    moments2, blocks2 = next_part(2, near2, middle2, after(out2, other0, through1), moments1)
     other0 = send(other0, PAIRS)
     turned0 = (mine0 + other0.astype(F32)).astype(BF16)
     through1 = send(through1, MIDDLE)
@@ -301,17 +303,19 @@
     turned1 = (mine1 + send(other1.astype(BF16), PAIRS).astype(F32)).astype(BF16)
     first_next, second_next = moments2
 
-    relay = send(line.block(back2, 2), RELAY_BACK)
-    pair = send(line.block(back2, 1), PAIRS)
+    to_relay, to_pair, to_mirror, own = blocks2
+    relay = send(to_relay, RELAY_BACK)
+    pair = send(to_pair, PAIRS)
     relay = after(relay, through1, other0)
-    mirror = send(add(line.block(back2, 3), jnp.where(line.inner, relay, 0)), MIRROR)
-    right2 = line.whole(near2, middle2, after(out2, relay))
-    left_next = 0.95 * left_stat + 0.05 * after(product, relay).astype(F32)
-    mirror, pair = together([mirror, pair], right2)
-    turned2 = line.block(back2, 0).astype(F32) + jnp.where(line.inner, 0, relay).astype(F32)
+    mirror = send(add(to_mirror, jnp.where(line.inner, relay, 0)), MIRROR)
+    out0, out1, out2, product = together([out0, out1, out2, product], turned1)
+    right = [line.whole(near0, middle0, out0), line.whole(near1, middle1, out1), line.whole(near2, middle2, out2)]
+    left_next = 0.95 * left_stat + 0.05 * product.astype(F32)
+    mirror, pair = together([mirror, pair], *right)
+    turned2 = own.astype(F32) + jnp.where(line.inner, 0, relay).astype(F32)
     turned2 = (turned2 + pair.astype(F32) + mirror.astype(F32)).astype(BF16)
 
-    right = together([right0, right1, right2], left_next)
+    right = together(right, left_next)
     direction = scatter_columns([turned0, turned1, turned2], right, "col")
     return (left_next, first_next, second_next, direction)
 

time: 463 us -> 471 us (1.017)
  waiting for transfers between devices: 224 us -> 253 us
  starting transfers between devices: 70.6 us -> 57.7 us
  other arithmetic: 38.7 us -> 30.7 us
    ppermute x21, waiting for transfers between devices: 182 us -> 210 us  [send(): return lax.ppermute(x, self.axis, pairs)]
    ppermute x21, starting transfers between devices: 58.6 us -> 46.6 us  [send(): return lax.ppermute(x, self.axis, pairs)]
  transfers between devices with their start and end apart: 34 -> 34, of which waited for: 18 -> 17; matrix products, arithmetic and copies ran while one was open for 14% -> 11% of each run, Pallas kernels for 14% -> 14%
where the time goes in v6:
time: 471 us; the launch traced here: 463 us
  waiting for transfers between devices  253 us (54%)
  Pallas kernels  72 us (15%)
  starting transfers between devices  57.7 us (12%)
  other arithmetic  30.7 us (7%)
  matrix products  24.6 us (5%)
  between operations  14.7 us (3%)
  local copies, waits for them, and re-layouts  10.6 us (2%)
    ppermute x21, waiting for transfers between devices, send(): return lax.ppermute(x, self.axis, pairs)  210 us
    pallas_call x3, Pallas kernels, part(): pl.pallas_call(functools.partial(part_kernel, results=results), grid_spec...  55.8 us
    ppermute x21, starting transfers between devices, send(): return lax.ppermute(x, self.axis, pairs)  46.6 us
    ppermute x10, waiting for transfers between devices, swap(): return lax.ppermute(x, axis, [(j, j ^ bit) for j in range(8)])  42.2 us
    pallas_call x4, Pallas kernels, products(): pl.pallas_call(products_kernel, grid_spec=pltpu.PrefetchScalarGridSpec(nu...  16.1 us
    dot_general x4, matrix products, contract_first(): lax.dot_general(first, second, (((0,), (0,)), ((), ())), preferred_elemen...  15.6 us
    ppermute x10, starting transfers between devices, swap(): return lax.ppermute(x, axis, [(j, j ^ bit) for j in range(8)])  11 us
  transfers between devices with their start and end apart: 34, of which 17 were waited for; matrix products, arithmetic and copies ran while one was open for 11% of the time, Pallas kernels for 14%

profile of v6, /device:TPU:0, one launch (start us, length us, event | category | flops | bytes accessed | tf_op | source)
XLA Modules:
  0.0 462.8 jit_solution(13893478973984219249)
XLA Ops:
  8.0 5.1 %collective-permute-start.1 = (bf16[1024,768]{1,0:T(8,128)(2,1)}, bf16[1024,768]{1,0:T(8,128)(2,1)S(1)}, u32[]{:S(2)}, u32[]{:S(2)}) collective-permute-start(bf16[1024,768]{1,0:T(8,128)(2,1)} %param.12), channel_id=1, source_target_pairs={{0,24},{8,16},{16,8},{24,0},{1,25},{9,17},{17,9},{25,1},{2,26},{10... | collective-permute-start | bytes 4718600 | tf_op jit(solution)/shard_map/ppermute | solution.py:58
  16.2 32.4 %collective-permute-done.1 = bf16[1024,768]{1,0:T(8,128)(2,1)S(1)} collective-permute-done((bf16[1024,768]{1,0:T(8,128)(2,1)}, bf16[1024,768]{1,0:T(8,128)(2,1)S(1)}, u32[]{:S(2)}, u32[]{:S(2)}) %collective-permute-start.1) | collective-permute-done | bytes 1572896 | tf_op jit(solution)/shard_map/ppermute | solution.py:58
  50.0 31.6 %collective-permute-done = bf16[1024,768]{1,0:T(8,128)(2,1)} collective-permute-done((bf16[1024,768]{1,0:T(8,128)(2,1)}, bf16[1024,768]{1,0:T(8,128)(2,1)}, u32[]{:S(2)}, u32[]{:S(2)}) %collective-permute-start) | collective-permute-done | bytes 1572896 | tf_op jit(solution)/shard_map/ppermute | solution.py:58
  83.6 4.1 fusion.4
  93.9 41.1 %collective-permute-done.2 = bf16[1536,256]{1,0:T(8,128)(2,1)S(1)} collective-permute-done((bf16[1536,256]{1,0:T(8,128)(2,1)S(1)}, bf16[1536,256]{1,0:T(8,128)(2,1)S(1)}, u32[]{:S(2)}, u32[]{:S(2)}) %collective-permute-start.2) | collective-permute-done | bytes 786464 | tf_op jit(solution)/shard_map/ppermute | solution.py:58
  135.4 5.7 %add_convert_fusion.2 = bf16[1024,768]{1,0:T(8,128)(2,1)} fusion(f32[1024,768]{1,0:T(8,128)S(1)} %copy-done.27, bf16[1024,768]{1,0:T(8,128)(2,1)} %collective-permute-done.5, bf16[4096,1024]{1,0:T(8,128)(2,1)} %all-gather.4.cloned.1.call-done.basis, s32[]{:T(128)S(6)} %select_n.130), kind=kOutput, calls=%fused_computation.6 | convolution fusion | flops 1612185600 | bytes 8388612 | tf_op jit(solution)/shard_map/dot_general | solution.py:29
  144.1 15.8 %collective-permute-done.4 = bf16[1536,256]{1,0:T(8,128)(2,1)S(1)} collective-permute-done((bf16[1536,256]{1,0:T(8,128)(2,1)S(1)}, bf16[1536,256]{1,0:T(8,128)(2,1)S(1)}, u32[]{:S(2)}, u32[]{:S(2)}) %collective-permute-start.4) | collective-permute-done | bytes 786464 | tf_op jit(solution)/shard_map/ppermute | solution.py:58
  161.8 17.5 %collective-permute-done.6 = bf16[1536,256]{1,0:T(8,128)(2,1)S(1)} collective-permute-done((bf16[1536,256]{1,0:T(8,128)(2,1)S(1)}, bf16[1536,256]{1,0:T(8,128)(2,1)S(1)}, u32[]{:S(2)}, u32[]{:S(2)}) %collective-permute-start.6) | collective-permute-done | bytes 786464 | tf_op jit(solution)/shard_map/ppermute | solution.py:58
  187.5 9.1 %convolution_convert_fusion = bf16[4096,1024]{1,0:T(8,128)(2,1)} fusion(bf16[4096,768]{1,0:T(8,128)(2,1)S(1)} %constant_dynamic-update-slice_fusion, bf16[1024,768]{1,0:T(8,128)(2,1)S(1)} %copy-done.10), kind=kOutput, calls=%fused_computation | convolution fusion | flops 6446645248 | bytes 16252928 | tf_op jit(solution)/shard_map/dot_general | solution.py:25
  196.6 20.4 %collective-permute-done.7.out = bf16[3072,256]{1,0:T(8,128)(2,1)} collective-permute-done((bf16[3072,256]{1,0:T(8,128)(2,1)}, bf16[3072,256]{1,0:T(8,128)(2,1)}, u32[]{:S(2)}, u32[]{:S(2)}) %collective-permute-start.7) | collective-permute-done | bytes 1572896 | tf_op jit(solution)/shard_map/ppermute | solution.py:58
  221.9 19.7 %shard_map.147 = (f32[1024,768]{1,0:T(8,128)}, f32[1024,768]{1,0:T(8,128)}, bf16[2048,256]{1,0:T(8,128)(2,1)}, bf16[2048,256]{1,0:T(8,128)(2,1)}) custom-call(s32[5]{0:T(128)} %pad_add_fusion.place, bf16[8,1024,768]{2,1,0:T(8,128)(2,1)} %bitcast.8, bf16[3072,256]{1,0:T(8,128)(2,1)} %copy-done.1, bf16[3072,256]{1,0:T(8,128)(2,1)} %collective-permute-done.3.middle, ...), custom_call_target="tpu_custom_call" | custom-call | flops 1048576 | bytes 65536 | tf_op jit(solution)/shard_map/pallas_call | solution.py:211
  241.6 9.4 %collective-permute-start.15 = (bf16[2048,256]{1,0:T(8,128)(2,1)}, bf16[2048,256]{1,0:T(8,128)(2,1)}, u32[]{:S(2)}, u32[]{:S(2)}) collective-permute-start(bf16[2048,256]{1,0:T(8,128)(2,1)} %get-tuple-element.84), channel_id=1, source_target_pairs={{0,8},{24,16},{1,9},{25,17},{2,10},{26,18},{3,11},{27,19},{4,12},{... | collective-permute-start | bytes 3145736 | tf_op jit(solution)/shard_map/ppermute | solution.py:58
  256.5 17.9 %shard_map.148 = (f32[1024,768]{1,0:T(8,128)}, f32[1024,768]{1,0:T(8,128)}, bf16[2048,256]{1,0:T(8,128)(2,1)}, bf16[2048,256]{1,0:T(8,128)(2,1)}) custom-call(s32[5]{0:T(128)} %pad_add_fusion.place, bf16[8,1024,768]{2,1,0:T(8,128)(2,1)} %bitcast.9, bf16[3072,256]{1,0:T(8,128)(2,1)} %maximum_select_fusion.4.near, ...), custom_call_target="tpu_custom_call", output_to_operand_aliasing={{0}: (8, {}), {1}: (9, {})} | custom-call | flops 1048576 | bytes 65536 | tf_op jit(solution)/shard_map/pallas_call | solution.py:211
  274.4 6.8 %collective-permute-start.10 = (bf16[2048,256]{1,0:T(8,128)(2,1)}, bf16[2048,256]{1,0:T(8,128)(2,1)S(1)}, u32[]{:S(2)}, u32[]{:S(2)}) collective-permute-start(bf16[2048,256]{1,0:T(8,128)(2,1)} %get-tuple-element.88), channel_id=1, source_target_pairs={{0,8},{24,16},{1,9},{25,17},{2,10},{26,18},{3,11},{27,19},{4,12},{... | collective-permute-start | bytes 3145736 | tf_op jit(solution)/shard_map/ppermute | solution.py:58
  284.1 15.5 %collective-permute-done.10 = bf16[2048,256]{1,0:T(8,128)(2,1)S(1)} collective-permute-done((bf16[2048,256]{1,0:T(8,128)(2,1)}, bf16[2048,256]{1,0:T(8,128)(2,1)S(1)}, u32[]{:S(2)}, u32[]{:S(2)}) %collective-permute-start.10) | collective-permute-done | bytes 1048608 | tf_op jit(solution)/shard_map/ppermute | solution.py:58
  307.5 18.2 %shard_map.149 = (f32[1024,768]{1,0:T(8,128)}, f32[1024,768]{1,0:T(8,128)}, bf16[1024,256]{1,0:T(8,128)(2,1)}, bf16[1024,256]{1,0:T(8,128)(2,1)}, bf16[1024,256]{1,0:T(8,128)(2,1)}, /*index=5*/bf16[1024,256]{1,0:T(8,128)(2,1)}) custom-call(s32[7]{0:T(128)} %pad_add_fusion.1.place, ...), custom_call_target="tpu_custom_call", output_to_operand_aliasing={{0}: (8, {}), {1}: (9, {})} | custom-call | flops 1048576 | bytes 65536 | tf_op jit(solution)/shard_map/pallas_call | solution.py:211
  328.6 10.2 %collective-permute-done.18 = bf16[1024,256]{1,0:T(8,128)(2,1)S(1)} collective-permute-done((bf16[1024,256]{1,0:T(8,128)(2,1)}, bf16[1024,256]{1,0:T(8,128)(2,1)S(1)}, u32[]{:S(2)}, u32[]{:S(2)}) %collective-permute-start.18) | collective-permute-done | bytes 524320 | tf_op jit(solution)/shard_map/ppermute | solution.py:58
  347.3 21.2 %collective-permute-done.14 = bf16[1024,256]{1,0:T(8,128)(2,1)S(1)} collective-permute-done((bf16[1024,256]{1,0:T(8,128)(2,1)S(1)}, bf16[1024,256]{1,0:T(8,128)(2,1)S(1)}, u32[]{:S(2)}, u32[]{:S(2)}) %collective-permute-start.14) | collective-permute-done | bytes 524320 | tf_op jit(solution)/shard_map/ppermute | solution.py:58
  381.4 4.0 shard_map.150
  392.3 4.0 shard_map.152
  405.5 11.2 %collective-permute-done.22 = bf16[256,1536]{1,0:T(8,128)(2,1)S(1)} collective-permute-done((bf16[256,1536]{1,0:T(8,128)(2,1)S(1)}, bf16[256,1536]{1,0:T(8,128)(2,1)S(1)}, u32[]{:S(2)}, u32[]{:S(2)}) %collective-permute-start.22) | collective-permute-done | bytes 786464 | tf_op jit(solution)/shard_map/ppermute | solution.py:104
  422.5 16.4 %collective-permute-done.27 = bf16[256,1536]{1,0:T(8,128)(2,1)S(1)} collective-permute-done((bf16[256,1536]{1,0:T(8,128)(2,1)S(1)}, bf16[256,1536]{1,0:T(8,128)(2,1)S(1)}, u32[]{:S(2)}, u32[]{:S(2)}) %collective-permute-start.27) | collective-permute-done | bytes 786464 | tf_op jit(solution)/shard_map/ppermute | solution.py:104
  442.7 5.0 %collective-permute-done.25 = bf16[256,768]{1,0:T(8,128)(2,1)S(1)} collective-permute-done((bf16[256,768]{1,0:T(8,128)(2,1)S(1)}, bf16[256,768]{1,0:T(8,128)(2,1)S(1)}, u32[]{:S(2)}, u32[]{:S(2)}) %collective-permute-start.25) | collective-permute-done | bytes 393248 | tf_op jit(solution)/shard_map/ppermute | solution.py:104
  448.0 6.3 %collective-permute-done.29 = bf16[256,768]{1,0:T(8,128)(2,1)S(1)} collective-permute-done((bf16[256,768]{1,0:T(8,128)(2,1)S(1)}, bf16[256,768]{1,0:T(8,128)(2,1)S(1)}, u32[]{:S(2)}, u32[]{:S(2)}) %collective-permute-start.29) | collective-permute-done | bytes 393248 | tf_op jit(solution)/shard_map/ppermute | solution.py:104
  (160 shorter events, 99.6 us)
Async XLA Ops:
  7.2 76.4 %all-gather.4.cloned.1.call-start = ((), (), s32[]{:S(2)}) async-start(), calls=%async_computation.1 | async-start | bytes 9437184 | tf_op jit(solution)/shard_map/all_gather | solution.py:243
  7.9 214.0 %all-gather.6.cloned.1.call-start = ((), (), s32[]{:S(2)}) async-start(), calls=%async_computation.3 | async-start | bytes 14155776 | tf_op jit(solution)/shard_map/all_gather | solution.py:260
  8.0 40.6 %collective-permute-start.1 = (bf16[1024,768]{1,0:T(8,128)(2,1)}, bf16[1024,768]{1,0:T(8,128)(2,1)S(1)}, u32[]{:S(2)}, u32[]{:S(2)}) collective-permute-start(bf16[1024,768]{1,0:T(8,128)(2,1)} %param.12), channel_id=1, source_target_pairs={{0,24},{8,16},{16,8},{24,0},{1,25},{9,17},{17,9},{25,1},{2,26},{10... | collective-permute-start | bytes 4718600 | tf_op jit(solution)/shard_map/ppermute | solution.py:58
  13.1 68.5 %collective-permute-start = (bf16[1024,768]{1,0:T(8,128)(2,1)}, bf16[1024,768]{1,0:T(8,128)(2,1)}, u32[]{:S(2)}, u32[]{:S(2)}) collective-permute-start(bf16[1024,768]{1,0:T(8,128)(2,1)} %param.12), channel_id=1, source_target_pairs={{0,8},{8,0},{16,24},{24,16},{1,9},{9,1},{17,25},{25,17},{2,10},{10... | collective-permute-start | bytes 4718600 | tf_op jit(solution)/shard_map/ppermute | solution.py:58
  81.6 53.8 %collective-permute-start.5 = (bf16[1024,768]{1,0:T(8,128)(2,1)}, bf16[1024,768]{1,0:T(8,128)(2,1)}, u32[]{:S(2)}, u32[]{:S(2)}) collective-permute-start(bf16[1024,768]{1,0:T(8,128)(2,1)} %broadcast_select_fusion.3), channel_id=1, source_target_pairs={{0,16},{8,0},{16,24},{24,8},{1,17},{9,1},{17,25},{25,9},{2,18},{10... | collective-permute-start | bytes 4718600 | tf_op jit(solution)/shard_map/ppermute | solution.py:58
  93.8 41.2 %collective-permute-start.2 = (bf16[1536,256]{1,0:T(8,128)(2,1)S(1)}, bf16[1536,256]{1,0:T(8,128)(2,1)S(1)}, u32[]{:S(2)}, u32[]{:S(2)}) collective-permute-start(bf16[1536,256]{1,0:T(8,128)(2,1)S(1)} %copy-done.15), channel_id=1, source_target_pairs={{0,8},{8,0},{16,24},{24,16},{1,9},{9,1},{17,25},{25,17},{2,10},{10... | collective-permute-start | bytes 2359304 | tf_op jit(solution)/shard_map/ppermute | solution.py:58
  141.2 227.4 %reduce-scatter.2.cloned.1.call-start = ((), (), s32[]{:S(2)}) async-start(), calls=%async_computation.2 | async-start | bytes 9437184 | tf_op jit(solution)/shard_map/reduce_scatter | solution.py:270
  142.3 38.6 %collective-permute-start.3 = (bf16[3072,256]{1,0:T(8,128)(2,1)S(1)}, bf16[3072,256]{1,0:T(8,128)(2,1)}, u32[]{:S(2)}, u32[]{:S(2)}) collective-permute-start(bf16[3072,256]{1,0:T(8,128)(2,1)S(1)} %maximum_select_fusion.3.near), channel_id=1, source_target_pairs={{8,16},{16,8},{9,17},{17,9},{10,18},{18,10},{11,19},{19,11},{12,20... | collective-permute-start | bytes 4718600 | tf_op jit(solution)/shard_map/ppermute | solution.py:58
  180.9 36.1 %collective-permute-start.7 = (bf16[3072,256]{1,0:T(8,128)(2,1)}, bf16[3072,256]{1,0:T(8,128)(2,1)}, u32[]{:S(2)}, u32[]{:S(2)}) collective-permute-start(bf16[3072,256]{1,0:T(8,128)(2,1)} %collective-permute-done.3.middle), channel_id=1, source_target_pairs={{8,0},{16,24},{9,1},{17,25},{10,2},{18,26},{11,3},{19,27},{12,4},{... | collective-permute-start | bytes 4718600 | tf_op jit(solution)/shard_map/ppermute | solution.py:58
  182.3 34.6 %collective-permute-start.8 = (bf16[3072,256]{1,0:T(8,128)(2,1)}, bf16[3072,256]{1,0:T(8,128)(2,1)S(1)}, u32[]{:S(2)}, u32[]{:S(2)}) collective-permute-start(bf16[3072,256]{1,0:T(8,128)(2,1)} %maximum_select_fusion.4.near), channel_id=1, source_target_pairs={{8,16},{16,8},{9,17},{17,9},{10,18},{18,10},{11,19},{19,11},{12,20... | collective-permute-start | bytes 4718600 | tf_op jit(solution)/shard_map/ppermute | solution.py:58
  218.1 36.9 %collective-permute-start.9 = (bf16[3072,256]{1,0:T(8,128)(2,1)S(1)}, bf16[3072,256]{1,0:T(8,128)(2,1)}, u32[]{:S(2)}, u32[]{:S(2)}) collective-permute-start(bf16[3072,256]{1,0:T(8,128)(2,1)S(1)} %collective-permute-done.8.middle), channel_id=1, source_target_pairs={{8,0},{16,24},{9,1},{17,25},{10,2},{18,26},{11,3},{19,27},{12,4},{... | collective-permute-start | bytes 4718600 | tf_op jit(solution)/shard_map/ppermute | solution.py:58
  219.4 35.6 %collective-permute-start.11 = (bf16[3072,256]{1,0:T(8,128)(2,1)S(1)}, bf16[3072,256]{1,0:T(8,128)(2,1)}, u32[]{:S(2)}, u32[]{:S(2)}) collective-permute-start(bf16[3072,256]{1,0:T(8,128)(2,1)S(1)} %copy-done.3), channel_id=1, source_target_pairs={{8,16},{16,8},{9,17},{17,9},{10,18},{18,10},{11,19},{19,11},{12,20... | collective-permute-start | bytes 4718600 | tf_op jit(solution)/shard_map/ppermute | solution.py:58
  241.6 39.6 %collective-permute-start.15 = (bf16[2048,256]{1,0:T(8,128)(2,1)}, bf16[2048,256]{1,0:T(8,128)(2,1)}, u32[]{:S(2)}, u32[]{:S(2)}) collective-permute-start(bf16[2048,256]{1,0:T(8,128)(2,1)} %get-tuple-element.84), channel_id=1, source_target_pairs={{0,8},{24,16},{1,9},{25,17},{2,10},{26,18},{3,11},{27,19},{4,12},{... | collective-permute-start | bytes 3145736 | tf_op jit(solution)/shard_map/ppermute | solution.py:58
  255.0 44.5 %collective-permute-start.12 = (bf16[3072,256]{1,0:T(8,128)(2,1)}, bf16[3072,256]{1,0:T(8,128)(2,1)S(1)}, u32[]{:S(2)}, u32[]{:S(2)}) collective-permute-start(bf16[3072,256]{1,0:T(8,128)(2,1)} %collective-permute-done.11.middle), channel_id=1, source_target_pairs={{8,0},{16,24},{9,1},{17,25},{10,2},{18,26},{11,3},{19,27},{12,4},{... | collective-permute-start | bytes 4718600 | tf_op jit(solution)/shard_map/ppermute | solution.py:58
  274.4 25.1 %collective-permute-start.10 = (bf16[2048,256]{1,0:T(8,128)(2,1)}, bf16[2048,256]{1,0:T(8,128)(2,1)S(1)}, u32[]{:S(2)}, u32[]{:S(2)}) collective-permute-start(bf16[2048,256]{1,0:T(8,128)(2,1)} %get-tuple-element.88), channel_id=1, source_target_pairs={{0,8},{24,16},{1,9},{25,17},{2,10},{26,18},{3,11},{27,19},{4,12},{... | collective-permute-start | bytes 3145736 | tf_op jit(solution)/shard_map/ppermute | solution.py:58
  301.0 37.7 %collective-permute-start.13 = (bf16[2048,256]{1,0:T(8,128)(2,1)}, bf16[2048,256]{1,0:T(8,128)(2,1)}, u32[]{:S(2)}, u32[]{:S(2)}) collective-permute-start(bf16[2048,256]{1,0:T(8,128)(2,1)} %add_convert_fusion.4), channel_id=1, source_target_pairs={{8,16},{16,8},{9,17},{17,9},{10,18},{18,10},{11,19},{19,11},{12,20... | collective-permute-start | bytes 3145736 | tf_op jit(solution)/shard_map/ppermute | solution.py:58
  303.9 24.7 %collective-permute-start.17 = (bf16[1024,256]{1,0:T(8,128)(2,1)}, bf16[1024,256]{1,0:T(8,128)(2,1)}, u32[]{:S(2)}, u32[]{:S(2)}) collective-permute-start(bf16[1024,256]{1,0:T(8,128)(2,1)} %select_convert_fusion), channel_id=1, source_target_pairs={{0,8},{8,0},{16,24},{24,16},{1,9},{9,1},{17,25},{25,17},{2,10},{10... | collective-permute-start | bytes 1572872 | tf_op jit(solution)/shard_map/ppermute | solution.py:58
  326.1 51.8 %collective-permute-start.20 = (bf16[1024,256]{1,0:T(8,128)(2,1)}, bf16[1024,256]{1,0:T(8,128)(2,1)}, u32[]{:S(2)}, u32[]{:S(2)}) collective-permute-start(bf16[1024,256]{1,0:T(8,128)(2,1)} %get-tuple-element.106), channel_id=1, source_target_pairs={{0,8},{8,0},{16,24},{24,16},{1,9},{9,1},{17,25},{25,17},{2,10},{10... | collective-permute-start | bytes 1572872 | tf_op jit(solution)/shard_map/ppermute | solution.py:58
  340.6 27.8 %collective-permute-start.14 = (bf16[1024,256]{1,0:T(8,128)(2,1)S(1)}, bf16[1024,256]{1,0:T(8,128)(2,1)S(1)}, u32[]{:S(2)}, u32[]{:S(2)}) collective-permute-start(bf16[1024,256]{1,0:T(8,128)(2,1)S(1)} %select_convert_fusion.1), channel_id=1, source_target_pairs={{0,8},{8,0},{16,24},{24,16},{1,9},{9,1},{17,25},{25,17},{2,10},{10... | collective-permute-start | bytes 1572872 | tf_op jit(solution)/shard_map/ppermute | solution.py:58
  344.1 33.8 %collective-permute-start.19 = (bf16[1024,256]{1,0:T(8,128)(2,1)}, bf16[1024,256]{1,0:T(8,128)(2,1)}, u32[]{:S(2)}, u32[]{:S(2)}) collective-permute-start(bf16[1024,256]{1,0:T(8,128)(2,1)} %add_convert_fusion.6), channel_id=1, source_target_pairs={{0,24},{8,16},{16,8},{24,0},{1,25},{9,17},{17,9},{25,1},{2,26},{10... | collective-permute-start | bytes 1572872 | tf_op jit(solution)/shard_map/ppermute | solution.py:58
  418.3 20.5 %collective-permute-start.27 = (bf16[256,1536]{1,0:T(8,128)(2,1)S(1)}, bf16[256,1536]{1,0:T(8,128)(2,1)S(1)}, u32[]{:S(2)}, u32[]{:S(2)}) collective-permute-start(bf16[256,1536]{1,0:T(8,128)(2,1)S(1)} %pad_maximum_fusion.2), channel_id=1, source_target_pairs={{0,2},{1,3},{2,0},{3,1},{4,6},{5,7},{6,4},{7,5},{8,10},{9,11},{10,... | collective-permute-start | bytes 2359304 | tf_op jit(solution)/shard_map/ppermute | solution.py:104
  418.8 20.5 %collective-permute-start.28 = (bf16[256,1536]{1,0:T(8,128)(2,1)S(1)}, bf16[256,1536]{1,0:T(8,128)(2,1)S(1)}, u32[]{:S(2)}, u32[]{:S(2)}) collective-permute-start(bf16[256,1536]{1,0:T(8,128)(2,1)S(1)} %concatenate.81), channel_id=1, source_target_pairs={{0,4},{1,5},{2,6},{3,7},{4,0},{5,1},{6,2},{7,3},{8,12},{9,13},{10,... | collective-permute-start | bytes 2359304 | tf_op jit(solution)/shard_map/ppermute | solution.py:104
  420.5 27.2 %collective-permute-start.25 = (bf16[256,768]{1,0:T(8,128)(2,1)S(1)}, bf16[256,768]{1,0:T(8,128)(2,1)S(1)}, u32[]{:S(2)}, u32[]{:S(2)}) collective-permute-start(bf16[256,768]{1,0:T(8,128)(2,1)S(1)} %get-tuple-element.128), channel_id=1, source_target_pairs={{0,4},{1,5},{2,6},{3,7},{4,0},{5,1},{6,2},{7,3},{8,12},{9,13},{10,... | collective-permute-start | bytes 1179656 | tf_op jit(solution)/shard_map/ppermute | solution.py:104
  420.8 26.9 %collective-permute-start.26 = (bf16[256,768]{1,0:T(8,128)(2,1)S(1)}, bf16[256,768]{1,0:T(8,128)(2,1)S(1)}, u32[]{:S(2)}, u32[]{:S(2)}) collective-permute-start(bf16[256,768]{1,0:T(8,128)(2,1)S(1)} %get-tuple-element.129), channel_id=1, source_target_pairs={{0,2},{1,3},{2,0},{3,1},{4,6},{5,7},{6,4},{7,5},{8,10},{9,11},{10,... | collective-permute-start | bytes 1179656 | tf_op jit(solution)/shard_map/ppermute | solution.py:104
  (38 other events, 534.7 us)
Sparse Core Ops, SparseCore 0:
  9.9 57.0 all-gather.3
  141.3 71.3 all-gather.5
  217.1 73.7 reduce-scatter.1

commit v7 on v6

--- a/solution.py
+++ b/solution.py
@@ -280,40 +280,43 @@
     to_blocks = jnp.concatenate([place, line.i ^ jnp.array([2, 1, 3, 0])]).astype(jnp.int32)
 
     def next_part(number, near, middle, out, before):
-        order, results = (to_blocks, 4) if number == 2 else (to_halves, 2)
+        order, results = (to_blocks, 4) if number else (to_halves, 2)
         return part(
             number, order, results, left_rotated, near, middle, out, first_moment, second_moment, left_cols, before
         )
 
+    def first_step(blocks):
+        return send(blocks[0], RELAY_BACK), send(blocks[1], PAIRS)
+
+    def to_mirror(blocks, relay):
+        return add(blocks[2], jnp.where(line.inner, relay, 0))
+
+    def summed(blocks, relay, pair, mirror):
+        total = blocks[3].astype(F32) + jnp.where(line.inner, 0, relay).astype(F32)
+        return (total + pair.astype(F32) + mirror.astype(F32)).astype(BF16)
+
     moments0, (far0, stay0) = next_part(0, near0, middle0, after(out0, near2), ())
     got0 = send(far0, INWARD)
     out2 = send(after(middle2, out1, far0), OUTWARD)
-    moments1, (far1, stay1) = next_part(1, near1, middle1, after(out1, far0), moments0)
-    got1 = send(far1, INWARD)
-    through0 = send(add(far0, after(got0, far1)), MIDDLE)
-    mine0, other0 = halves(line.even, stay0.astype(F32) + through0.astype(F32))
+    moments1, blocks1 = next_part(1, near1, middle1, after(out1, far0), moments0)
+    relay1, pair1 = first_step(blocks1)
+    through0 = send(add(far0, after(got0, blocks1[0])), MIDDLE)
+    relay1, out2 = together([relay1, out2])
+    mirror1 = to_mirror(blocks1, relay1)
+    moments2, blocks2 = next_part(2, near2, middle2, after(out2, mirror1), moments1)
+    mirror1 = send(mirror1, MIRROR)
+    relay2, pair2 = first_step(blocks2)
+    turned1 = summed(blocks1, relay1, pair1, mirror1)
+    mine0, other0 = halves(line.even, stay0.astype(F32) + after(through0, blocks2[0]).astype(F32))
     other0 = other0.astype(BF16)
-    got1, out2 = together([got1, out2])
-    through1 = add(far1, got1)
-    moments2, blocks2 = next_part(2, near2, middle2, after(out2, other0, through1), moments1)
-    other0 = send(other0, PAIRS)
-    turned0 = (mine0 + other0.astype(F32)).astype(BF16)
-    through1 = send(through1, MIDDLE)
-    mine1, other1 = halves(line.even, stay1.astype(F32) + through1.astype(F32))
-    turned1 = (mine1 + send(other1.astype(BF16), PAIRS).astype(F32)).astype(BF16)
+    turned0 = (mine0 + send(other0, PAIRS).astype(F32)).astype(BF16)
     first_next, second_next = moments2
 
-    to_relay, to_pair, to_mirror, own = blocks2
-    relay = send(to_relay, RELAY_BACK)
-    pair = send(to_pair, PAIRS)
-    relay = after(relay, through1, other0)
-    mirror = send(add(to_mirror, jnp.where(line.inner, relay, 0)), MIRROR)
-    out0, out1, out2, product = together([out0, out1, out2, product], turned1)
+    out0, out1, out2, product = together([out0, out1, out2, product], other0)
     right = [line.whole(near0, middle0, out0), line.whole(near1, middle1, out1), line.whole(near2, middle2, out2)]
+    mirror2 = send(to_mirror(blocks2, after(relay2, turned1, *right)), MIRROR)
     left_next = 0.95 * left_stat + 0.05 * product.astype(F32)
-    mirror, pair = together([mirror, pair], *right)
-    turned2 = own.astype(F32) + jnp.where(line.inner, 0, relay).astype(F32)
-    turned2 = (turned2 + pair.astype(F32) + mirror.astype(F32)).astype(BF16)
+    turned2 = summed(blocks2, relay2, pair2, mirror2)
 
     right = together(right, left_next)
     direction = scatter_columns([turned0, turned1, turned2], right, "col")

time: 471 us -> 475 us (level)
  waiting for transfers between devices: 253 us -> 262 us
  starting transfers between devices: 57.7 us -> 51.5 us
    ppermute x21, waiting for transfers between devices: 210 us -> 219 us  [send(): return lax.ppermute(x, self.axis, pairs)]
    ppermute x21, starting transfers between devices: 46.6 us -> 40.2 us  [send(): return lax.ppermute(x, self.axis, pairs)]
  transfers between devices with their start and end apart: 34 -> 34, of which waited for: 17 -> 18; matrix products, arithmetic and copies ran while one was open for 11% -> 11% of each run, Pallas kernels for 14% -> 14%
where the time goes in v7:
time: 475 us; the launch traced here: 467 us
  waiting for transfers between devices  262 us (55%)
  Pallas kernels  72.1 us (15%)
  starting transfers between devices  51.5 us (11%)
  other arithmetic  30.8 us (6%)
  matrix products  24.6 us (5%)
  between operations  14.7 us (3%)
  local copies, waits for them, and re-layouts  11.3 us (2%)
    ppermute x21, waiting for transfers between devices, send(): return lax.ppermute(x, self.axis, pairs)  219 us
    pallas_call x3, Pallas kernels, part(): pl.pallas_call(functools.partial(part_kernel, results=results), grid_spec...  56 us
    ppermute x10, waiting for transfers between devices, swap(): return lax.ppermute(x, axis, [(j, j ^ bit) for j in range(8)])  41.9 us
    ppermute x21, starting transfers between devices, send(): return lax.ppermute(x, self.axis, pairs)  40.2 us
    pallas_call x4, Pallas kernels, products(): pl.pallas_call(products_kernel, grid_spec=pltpu.PrefetchScalarGridSpec(nu...  16.1 us
    dot_general x4, matrix products, contract_first(): lax.dot_general(first, second, (((0,), (0,)), ((), ())), preferred_elemen...  15.6 us
    ppermute x10, starting transfers between devices, swap(): return lax.ppermute(x, axis, [(j, j ^ bit) for j in range(8)])  11.1 us
  transfers between devices with their start and end apart: 34, of which 18 were waited for; matrix products, arithmetic and copies ran while one was open for 11% of the time, Pallas kernels for 14%

profile of v7, /device:TPU:0, one launch (start us, length us, event | category | flops | bytes accessed | tf_op | source)
XLA Modules:
  0.0 466.7 jit_solution(18345353860486966577)
XLA Ops:
  8.0 5.1 %collective-permute-start.1 = (bf16[1024,768]{1,0:T(8,128)(2,1)}, bf16[1024,768]{1,0:T(8,128)(2,1)S(1)}, u32[]{:S(2)}, u32[]{:S(2)}) collective-permute-start(bf16[1024,768]{1,0:T(8,128)(2,1)} %param.12), channel_id=1, source_target_pairs={{0,24},{8,16},{16,8},{24,0},{1,25},{9,17},{17,9},{25,1},{2,26},{10... | collective-permute-start | bytes 4718600 | tf_op jit(solution)/shard_map/ppermute | solution.py:58
  16.2 32.4 %collective-permute-done.1 = bf16[1024,768]{1,0:T(8,128)(2,1)S(1)} collective-permute-done((bf16[1024,768]{1,0:T(8,128)(2,1)}, bf16[1024,768]{1,0:T(8,128)(2,1)S(1)}, u32[]{:S(2)}, u32[]{:S(2)}) %collective-permute-start.1) | collective-permute-done | bytes 1572896 | tf_op jit(solution)/shard_map/ppermute | solution.py:58
  50.0 31.6 %collective-permute-done = bf16[1024,768]{1,0:T(8,128)(2,1)} collective-permute-done((bf16[1024,768]{1,0:T(8,128)(2,1)}, bf16[1024,768]{1,0:T(8,128)(2,1)}, u32[]{:S(2)}, u32[]{:S(2)}) %collective-permute-start) | collective-permute-done | bytes 1572896 | tf_op jit(solution)/shard_map/ppermute | solution.py:58
  83.6 4.1 fusion.4
  93.9 41.1 %collective-permute-done.2 = bf16[1536,256]{1,0:T(8,128)(2,1)S(1)} collective-permute-done((bf16[1536,256]{1,0:T(8,128)(2,1)S(1)}, bf16[1536,256]{1,0:T(8,128)(2,1)S(1)}, u32[]{:S(2)}, u32[]{:S(2)}) %collective-permute-start.2) | collective-permute-done | bytes 786464 | tf_op jit(solution)/shard_map/ppermute | solution.py:58
  136.8 5.7 %add_convert_fusion.2 = bf16[1024,768]{1,0:T(8,128)(2,1)} fusion(f32[1024,768]{1,0:T(8,128)S(1)} %copy-done.30, bf16[1024,768]{1,0:T(8,128)(2,1)} %collective-permute-done.5, bf16[4096,1024]{1,0:T(8,128)(2,1)} %all-gather.4.cloned.1.call-done.basis, s32[]{:T(128)S(6)} %select_n.130), kind=kOutput, calls=%fused_computation.6 | convolution fusion | flops 1612185600 | bytes 8388612 | tf_op jit(solution)/shard_map/dot_general | solution.py:29
  145.5 15.8 %collective-permute-done.4 = bf16[1536,256]{1,0:T(8,128)(2,1)S(1)} collective-permute-done((bf16[1536,256]{1,0:T(8,128)(2,1)S(1)}, bf16[1536,256]{1,0:T(8,128)(2,1)S(1)}, u32[]{:S(2)}, u32[]{:S(2)}) %collective-permute-start.4) | collective-permute-done | bytes 786464 | tf_op jit(solution)/shard_map/ppermute | solution.py:58
  163.6 17.7 %collective-permute-done.6 = bf16[1536,256]{1,0:T(8,128)(2,1)S(1)} collective-permute-done((bf16[1536,256]{1,0:T(8,128)(2,1)}, bf16[1536,256]{1,0:T(8,128)(2,1)S(1)}, u32[]{:S(2)}, u32[]{:S(2)}) %collective-permute-start.6) | collective-permute-done | bytes 786464 | tf_op jit(solution)/shard_map/ppermute | solution.py:58
  191.8 9.1 %convolution_convert_fusion = bf16[4096,1024]{1,0:T(8,128)(2,1)} fusion(bf16[4096,768]{1,0:T(8,128)(2,1)S(1)} %constant_dynamic-update-slice_fusion, bf16[1024,768]{1,0:T(8,128)(2,1)S(1)} %copy-done.14), kind=kOutput, calls=%fused_computation | convolution fusion | flops 6446645248 | bytes 16252928 | tf_op jit(solution)/shard_map/dot_general | solution.py:25
  200.9 19.6 %collective-permute-done.7.out = bf16[3072,256]{1,0:T(8,128)(2,1)} collective-permute-done((bf16[3072,256]{1,0:T(8,128)(2,1)}, bf16[3072,256]{1,0:T(8,128)(2,1)}, u32[]{:S(2)}, u32[]{:S(2)}) %collective-permute-start.7) | collective-permute-done | bytes 1572896 | tf_op jit(solution)/shard_map/ppermute | solution.py:58
  224.2 19.5 %shard_map.147 = (f32[1024,768]{1,0:T(8,128)}, f32[1024,768]{1,0:T(8,128)}, bf16[2048,256]{1,0:T(8,128)(2,1)}, bf16[2048,256]{1,0:T(8,128)(2,1)}) custom-call(s32[5]{0:T(128)} %pad_add_fusion.1.place, bf16[8,1024,768]{2,1,0:T(8,128)(2,1)} %bitcast.8, bf16[3072,256]{1,0:T(8,128)(2,1)} %copy-done.1, bf16[3072,256]{1,0:T(8,128)(2,1)} %collective-permute-done.3.middle, ...), custom_call_target="tpu_custom_call" | custom-call | flops 1048576 | bytes 65536 | tf_op jit(solution)/shard_map/pallas_call | solution.py:211
  243.7 8.4 %collective-permute-start.13 = (bf16[2048,256]{1,0:T(8,128)(2,1)}, bf16[2048,256]{1,0:T(8,128)(2,1)}, u32[]{:S(2)}, u32[]{:S(2)}) collective-permute-start(bf16[2048,256]{1,0:T(8,128)(2,1)} %get-tuple-element.85), channel_id=1, source_target_pairs={{0,8},{24,16},{1,9},{25,17},{2,10},{26,18},{3,11},{27,19},{4,12},{... | collective-permute-start | bytes 3145736 | tf_op jit(solution)/shard_map/ppermute | solution.py:58
  252.0 5.4 %collective-permute-done.9.out = bf16[3072,256]{1,0:T(8,128)(2,1)S(1)} collective-permute-done((bf16[3072,256]{1,0:T(8,128)(2,1)}, bf16[3072,256]{1,0:T(8,128)(2,1)S(1)}, u32[]{:S(2)}, u32[]{:S(2)}) %collective-permute-start.9) | collective-permute-done | bytes 1572896 | tf_op jit(solution)/shard_map/ppermute | solution.py:58
  259.6 18.4 %shard_map.148 = (f32[1024,768]{1,0:T(8,128)}, f32[1024,768]{1,0:T(8,128)}, bf16[1024,256]{1,0:T(8,128)(2,1)}, bf16[1024,256]{1,0:T(8,128)(2,1)}, bf16[1024,256]{1,0:T(8,128)(2,1)}, /*index=5*/bf16[1024,256]{1,0:T(8,128)(2,1)}) custom-call(s32[7]{0:T(128)} %pad_add_fusion.place, ...), custom_call_target="tpu_custom_call", output_to_operand_aliasing={{0}: (8, {}), {1}: (9, {})} | custom-call | flops 1048576 | bytes 65536 | tf_op jit(solution)/shard_map/pallas_call | solution.py:211
  282.8 4.6 collective-permute-start.10
  287.5 40.2 %collective-permute-done.10 = bf16[1024,256]{1,0:T(8,128)(2,1)S(1)} collective-permute-done((bf16[1024,256]{1,0:T(8,128)(2,1)S(1)}, bf16[1024,256]{1,0:T(8,128)(2,1)S(1)}, u32[]{:S(2)}, u32[]{:S(2)}) %collective-permute-start.10) | collective-permute-done | bytes 524320 | tf_op jit(solution)/shard_map/ppermute | solution.py:58
  329.4 18.1 %shard_map.149 = (f32[1024,768]{1,0:T(8,128)}, f32[1024,768]{1,0:T(8,128)}, bf16[1024,256]{1,0:T(8,128)(2,1)}, bf16[1024,256]{1,0:T(8,128)(2,1)}, bf16[1024,256]{1,0:T(8,128)(2,1)}, /*index=5*/bf16[1024,256]{1,0:T(8,128)(2,1)}) custom-call(s32[7]{0:T(128)} %pad_add_fusion.place, ...), custom_call_target="tpu_custom_call", output_to_operand_aliasing={{0}: (8, {}), {1}: (9, {})} | custom-call | flops 1048576 | bytes 65536 | tf_op jit(solution)/shard_map/pallas_call | solution.py:211
  363.1 6.8 %collective-permute-done.18 = bf16[1024,256]{1,0:T(8,128)(2,1)S(1)} collective-permute-done((bf16[1024,256]{1,0:T(8,128)(2,1)}, bf16[1024,256]{1,0:T(8,128)(2,1)S(1)}, u32[]{:S(2)}, u32[]{:S(2)}) %collective-permute-start.18) | collective-permute-done | bytes 524320 | tf_op jit(solution)/shard_map/ppermute | solution.py:58
  374.3 4.2 collective-permute-done.15
  379.7 4.3 collective-permute-done.20
  409.5 11.1 %collective-permute-done.22 = bf16[256,1536]{1,0:T(8,128)(2,1)S(1)} collective-permute-done((bf16[256,1536]{1,0:T(8,128)(2,1)S(1)}, bf16[256,1536]{1,0:T(8,128)(2,1)S(1)}, u32[]{:S(2)}, u32[]{:S(2)}) %collective-permute-start.22) | collective-permute-done | bytes 786464 | tf_op jit(solution)/shard_map/ppermute | solution.py:104
  426.3 16.4 %collective-permute-done.27 = bf16[256,1536]{1,0:T(8,128)(2,1)S(1)} collective-permute-done((bf16[256,1536]{1,0:T(8,128)(2,1)S(1)}, bf16[256,1536]{1,0:T(8,128)(2,1)S(1)}, u32[]{:S(2)}, u32[]{:S(2)}) %collective-permute-start.27) | collective-permute-done | bytes 786464 | tf_op jit(solution)/shard_map/ppermute | solution.py:104
  446.8 4.9 %collective-permute-done.25 = bf16[256,768]{1,0:T(8,128)(2,1)S(1)} collective-permute-done((bf16[256,768]{1,0:T(8,128)(2,1)S(1)}, bf16[256,768]{1,0:T(8,128)(2,1)S(1)}, u32[]{:S(2)}, u32[]{:S(2)}) %collective-permute-start.25) | collective-permute-done | bytes 393248 | tf_op jit(solution)/shard_map/ppermute | solution.py:104
  452.0 6.1 %collective-permute-done.29 = bf16[256,768]{1,0:T(8,128)(2,1)S(1)} collective-permute-done((bf16[256,768]{1,0:T(8,128)(2,1)S(1)}, bf16[256,768]{1,0:T(8,128)(2,1)S(1)}, u32[]{:S(2)}, u32[]{:S(2)}) %collective-permute-start.29) | collective-permute-done | bytes 393248 | tf_op jit(solution)/shard_map/ppermute | solution.py:104
  (164 shorter events, 101.4 us)
Async XLA Ops:
  7.2 76.4 %all-gather.4.cloned.1.call-start = ((), (), s32[]{:S(2)}) async-start(), calls=%async_computation.1 | async-start | bytes 9437184 | tf_op jit(solution)/shard_map/all_gather | solution.py:243
  7.9 216.3 %all-gather.6.cloned.1.call-start = ((), (), s32[]{:S(2)}) async-start(), calls=%async_computation.3 | async-start | bytes 14155776 | tf_op jit(solution)/shard_map/all_gather | solution.py:260
  8.0 40.6 %collective-permute-start.1 = (bf16[1024,768]{1,0:T(8,128)(2,1)}, bf16[1024,768]{1,0:T(8,128)(2,1)S(1)}, u32[]{:S(2)}, u32[]{:S(2)}) collective-permute-start(bf16[1024,768]{1,0:T(8,128)(2,1)} %param.12), channel_id=1, source_target_pairs={{0,24},{8,16},{16,8},{24,0},{1,25},{9,17},{17,9},{25,1},{2,26},{10... | collective-permute-start | bytes 4718600 | tf_op jit(solution)/shard_map/ppermute | solution.py:58
  13.1 68.5 %collective-permute-start = (bf16[1024,768]{1,0:T(8,128)(2,1)}, bf16[1024,768]{1,0:T(8,128)(2,1)}, u32[]{:S(2)}, u32[]{:S(2)}) collective-permute-start(bf16[1024,768]{1,0:T(8,128)(2,1)} %param.12), channel_id=1, source_target_pairs={{0,8},{8,0},{16,24},{24,16},{1,9},{9,1},{17,25},{25,17},{2,10},{10... | collective-permute-start | bytes 4718600 | tf_op jit(solution)/shard_map/ppermute | solution.py:58
  81.6 55.2 %collective-permute-start.5 = (bf16[1024,768]{1,0:T(8,128)(2,1)}, bf16[1024,768]{1,0:T(8,128)(2,1)}, u32[]{:S(2)}, u32[]{:S(2)}) collective-permute-start(bf16[1024,768]{1,0:T(8,128)(2,1)} %broadcast_select_fusion.3), channel_id=1, source_target_pairs={{0,16},{8,0},{16,24},{24,8},{1,17},{9,1},{17,25},{25,9},{2,18},{10... | collective-permute-start | bytes 4718600 | tf_op jit(solution)/shard_map/ppermute | solution.py:58
  93.8 41.2 %collective-permute-start.2 = (bf16[1536,256]{1,0:T(8,128)(2,1)S(1)}, bf16[1536,256]{1,0:T(8,128)(2,1)S(1)}, u32[]{:S(2)}, u32[]{:S(2)}) collective-permute-start(bf16[1536,256]{1,0:T(8,128)(2,1)S(1)} %copy-done.18), channel_id=1, source_target_pairs={{0,8},{8,0},{16,24},{24,16},{1,9},{9,1},{17,25},{25,17},{2,10},{10... | collective-permute-start | bytes 2359304 | tf_op jit(solution)/shard_map/ppermute | solution.py:58
  142.6 212.1 %reduce-scatter.2.cloned.1.call-start = ((), (), s32[]{:S(2)}) async-start(), calls=%async_computation.2 | async-start | bytes 9437184 | tf_op jit(solution)/shard_map/reduce_scatter | solution.py:270
  143.7 40.6 %collective-permute-start.3 = (bf16[3072,256]{1,0:T(8,128)(2,1)S(1)}, bf16[3072,256]{1,0:T(8,128)(2,1)}, u32[]{:S(2)}, u32[]{:S(2)}) collective-permute-start(bf16[3072,256]{1,0:T(8,128)(2,1)S(1)} %maximum_select_fusion.3.near), channel_id=1, source_target_pairs={{8,16},{16,8},{9,17},{17,9},{10,18},{18,10},{11,19},{19,11},{12,20... | collective-permute-start | bytes 4718600 | tf_op jit(solution)/shard_map/ppermute | solution.py:58
  184.3 36.2 %collective-permute-start.7 = (bf16[3072,256]{1,0:T(8,128)(2,1)}, bf16[3072,256]{1,0:T(8,128)(2,1)}, u32[]{:S(2)}, u32[]{:S(2)}) collective-permute-start(bf16[3072,256]{1,0:T(8,128)(2,1)} %collective-permute-done.3.middle), channel_id=1, source_target_pairs={{8,0},{16,24},{9,1},{17,25},{10,2},{18,26},{11,3},{19,27},{12,4},{... | collective-permute-start | bytes 4718600 | tf_op jit(solution)/shard_map/ppermute | solution.py:58
  185.7 34.8 %collective-permute-start.8 = (bf16[3072,256]{1,0:T(8,128)(2,1)S(1)}, bf16[3072,256]{1,0:T(8,128)(2,1)}, u32[]{:S(2)}, u32[]{:S(2)}) collective-permute-start(bf16[3072,256]{1,0:T(8,128)(2,1)S(1)} %maximum_select_fusion.4.near), channel_id=1, source_target_pairs={{8,16},{16,8},{9,17},{17,9},{10,18},{18,10},{11,19},{19,11},{12,20... | collective-permute-start | bytes 4718600 | tf_op jit(solution)/shard_map/ppermute | solution.py:58
  220.5 37.0 %collective-permute-start.9 = (bf16[3072,256]{1,0:T(8,128)(2,1)}, bf16[3072,256]{1,0:T(8,128)(2,1)S(1)}, u32[]{:S(2)}, u32[]{:S(2)}) collective-permute-start(bf16[3072,256]{1,0:T(8,128)(2,1)} %collective-permute-done.8.middle), channel_id=1, source_target_pairs={{8,0},{16,24},{9,1},{17,25},{10,2},{18,26},{11,3},{19,27},{12,4},{... | collective-permute-start | bytes 4718600 | tf_op jit(solution)/shard_map/ppermute | solution.py:58
  221.8 35.7 %collective-permute-start.11 = (bf16[3072,256]{1,0:T(8,128)(2,1)S(1)}, bf16[3072,256]{1,0:T(8,128)(2,1)}, u32[]{:S(2)}, u32[]{:S(2)}) collective-permute-start(bf16[3072,256]{1,0:T(8,128)(2,1)S(1)} %copy-done.5), channel_id=1, source_target_pairs={{8,16},{16,8},{9,17},{17,9},{10,18},{18,10},{11,19},{19,11},{12,20... | collective-permute-start | bytes 4718600 | tf_op jit(solution)/shard_map/ppermute | solution.py:58
  243.7 34.3 %collective-permute-start.13 = (bf16[2048,256]{1,0:T(8,128)(2,1)}, bf16[2048,256]{1,0:T(8,128)(2,1)}, u32[]{:S(2)}, u32[]{:S(2)}) collective-permute-start(bf16[2048,256]{1,0:T(8,128)(2,1)} %get-tuple-element.85), channel_id=1, source_target_pairs={{0,8},{24,16},{1,9},{25,17},{2,10},{26,18},{3,11},{27,19},{4,12},{... | collective-permute-start | bytes 3145736 | tf_op jit(solution)/shard_map/ppermute | solution.py:58
  257.5 70.2 %collective-permute-start.12 = (bf16[3072,256]{1,0:T(8,128)(2,1)}, bf16[3072,256]{1,0:T(8,128)(2,1)S(1)}, u32[]{:S(2)}, u32[]{:S(2)}) collective-permute-start(bf16[3072,256]{1,0:T(8,128)(2,1)} %collective-permute-done.11.middle), channel_id=1, source_target_pairs={{8,0},{16,24},{9,1},{17,25},{10,2},{18,26},{11,3},{19,27},{12,4},{... | collective-permute-start | bytes 4718600 | tf_op jit(solution)/shard_map/ppermute | solution.py:58
  281.2 68.5 %collective-permute-start.14 = (bf16[2048,256]{1,0:T(8,128)(2,1)}, bf16[2048,256]{1,0:T(8,128)(2,1)}, u32[]{:S(2)}, u32[]{:S(2)}) collective-permute-start(bf16[2048,256]{1,0:T(8,128)(2,1)} %add_convert_fusion.3), channel_id=1, source_target_pairs={{8,16},{16,8},{9,17},{17,9},{10,18},{18,10},{11,19},{19,11},{12,20... | collective-permute-start | bytes 3145736 | tf_op jit(solution)/shard_map/ppermute | solution.py:58
  282.8 44.8 %collective-permute-start.10 = (bf16[1024,256]{1,0:T(8,128)(2,1)S(1)}, bf16[1024,256]{1,0:T(8,128)(2,1)S(1)}, u32[]{:S(2)}, u32[]{:S(2)}) collective-permute-start(bf16[1024,256]{1,0:T(8,128)(2,1)S(1)} %copy-done.25), channel_id=1, source_target_pairs={{0,8},{8,24},{16,0},{24,16},{1,9},{9,25},{17,1},{25,17},{2,10},{10... | collective-permute-start | bytes 1572872 | tf_op jit(solution)/shard_map/ppermute | solution.py:58
  287.4 73.0 %collective-permute-start.16 = (bf16[1024,256]{1,0:T(8,128)(2,1)}, bf16[1024,256]{1,0:T(8,128)(2,1)}, u32[]{:S(2)}, u32[]{:S(2)}) collective-permute-start(bf16[1024,256]{1,0:T(8,128)(2,1)} %get-tuple-element.106), channel_id=1, source_target_pairs={{0,8},{8,0},{16,24},{24,16},{1,9},{9,1},{17,25},{25,17},{2,10},{10... | collective-permute-start | bytes 1572872 | tf_op jit(solution)/shard_map/ppermute | solution.py:58
  327.9 32.6 %collective-permute-start.17 = (bf16[1024,256]{1,0:T(8,128)(2,1)S(1)}, bf16[1024,256]{1,0:T(8,128)(2,1)}, u32[]{:S(2)}, u32[]{:S(2)}) collective-permute-start(bf16[1024,256]{1,0:T(8,128)(2,1)S(1)} %add_convert_fusion.8), channel_id=1, source_target_pairs={{0,24},{8,16},{16,8},{24,0},{1,25},{9,17},{17,9},{25,1},{2,26},{10... | collective-permute-start | bytes 1572872 | tf_op jit(solution)/shard_map/ppermute | solution.py:58
  347.5 32.3 %collective-permute-start.19 = (bf16[1024,256]{1,0:T(8,128)(2,1)}, bf16[1024,256]{1,0:T(8,128)(2,1)}, u32[]{:S(2)}, u32[]{:S(2)}) collective-permute-start(bf16[1024,256]{1,0:T(8,128)(2,1)} %get-tuple-element.108), channel_id=1, source_target_pairs={{0,8},{8,0},{16,24},{24,16},{1,9},{9,1},{17,25},{25,17},{2,10},{10... | collective-permute-start | bytes 1572872 | tf_op jit(solution)/shard_map/ppermute | solution.py:58
  347.5 22.5 %collective-permute-start.18 = (bf16[1024,256]{1,0:T(8,128)(2,1)}, bf16[1024,256]{1,0:T(8,128)(2,1)S(1)}, u32[]{:S(2)}, u32[]{:S(2)}) collective-permute-start(bf16[1024,256]{1,0:T(8,128)(2,1)} %get-tuple-element.100), channel_id=1, source_target_pairs={{0,8},{8,24},{16,0},{24,16},{1,9},{9,25},{17,1},{25,17},{2,10},{10... | collective-permute-start | bytes 1572872 | tf_op jit(solution)/shard_map/ppermute | solution.py:58
  353.7 24.7 %collective-permute-start.15 = (bf16[1024,256]{1,0:T(8,128)(2,1)}, bf16[1024,256]{1,0:T(8,128)(2,1)}, u32[]{:S(2)}, u32[]{:S(2)}) collective-permute-start(bf16[1024,256]{1,0:T(8,128)(2,1)} %select_convert_fusion), channel_id=1, source_target_pairs={{0,8},{8,0},{16,24},{24,16},{1,9},{9,1},{17,25},{25,17},{2,10},{10... | collective-permute-start | bytes 1572872 | tf_op jit(solution)/shard_map/ppermute | solution.py:58
  422.2 20.5 %collective-permute-start.27 = (bf16[256,1536]{1,0:T(8,128)(2,1)S(1)}, bf16[256,1536]{1,0:T(8,128)(2,1)S(1)}, u32[]{:S(2)}, u32[]{:S(2)}) collective-permute-start(bf16[256,1536]{1,0:T(8,128)(2,1)S(1)} %pad_maximum_fusion.2), channel_id=1, source_target_pairs={{0,2},{1,3},{2,0},{3,1},{4,6},{5,7},{6,4},{7,5},{8,10},{9,11},{10,... | collective-permute-start | bytes 2359304 | tf_op jit(solution)/shard_map/ppermute | solution.py:104
  424.4 27.3 %collective-permute-start.25 = (bf16[256,768]{1,0:T(8,128)(2,1)S(1)}, bf16[256,768]{1,0:T(8,128)(2,1)S(1)}, u32[]{:S(2)}, u32[]{:S(2)}) collective-permute-start(bf16[256,768]{1,0:T(8,128)(2,1)S(1)} %get-tuple-element.130), channel_id=1, source_target_pairs={{0,4},{1,5},{2,6},{3,7},{4,0},{5,1},{6,2},{7,3},{8,12},{9,13},{10,... | collective-permute-start | bytes 1179656 | tf_op jit(solution)/shard_map/ppermute | solution.py:104
  424.8 26.9 %collective-permute-start.26 = (bf16[256,768]{1,0:T(8,128)(2,1)S(1)}, bf16[256,768]{1,0:T(8,128)(2,1)S(1)}, u32[]{:S(2)}, u32[]{:S(2)}) collective-permute-start(bf16[256,768]{1,0:T(8,128)(2,1)S(1)} %get-tuple-element.131), channel_id=1, source_target_pairs={{0,2},{1,3},{2,0},{3,1},{4,6},{5,7},{6,4},{7,5},{8,10},{9,11},{10,... | collective-permute-start | bytes 1179656 | tf_op jit(solution)/shard_map/ppermute | solution.py:104
  (41 other events, 562.3 us)
Sparse Core Ops, SparseCore 0:
  9.9 57.0 all-gather.3
  142.7 71.3 all-gather.5
  220.6 73.5 reduce-scatter.1

commit v8 on v6

--- a/solution.py
+++ b/solution.py
@@ -291,10 +291,10 @@
     moments1, (far1, stay1) = next_part(1, near1, middle1, after(out1, far0), moments0)
     got1 = send(far1, INWARD)
     through0 = send(add(far0, after(got0, far1)), MIDDLE)
-    mine0, other0 = halves(line.even, stay0.astype(F32) + through0.astype(F32))
-    other0 = other0.astype(BF16)
     got1, out2 = together([got1, out2])
     through1 = add(far1, got1)
+    mine0, other0 = halves(line.even, stay0.astype(F32) + after(through0, through1).astype(F32))
+    other0 = other0.astype(BF16)
     moments2, blocks2 = next_part(2, near2, middle2, after(out2, other0, through1), moments1)
     other0 = send(other0, PAIRS)
     turned0 = (mine0 + other0.astype(F32)).astype(BF16)
@@ -308,7 +308,7 @@
     pair = send(to_pair, PAIRS)
     relay = after(relay, through1, other0)
     mirror = send(add(to_mirror, jnp.where(line.inner, relay, 0)), MIRROR)
-    out0, out1, out2, product = together([out0, out1, out2, product], turned1)
+    out0, out1, out2, product = together([out0, out1, out2, product], turned0)
     right = [line.whole(near0, middle0, out0), line.whole(near1, middle1, out1), line.whole(near2, middle2, out2)]
     left_next = 0.95 * left_stat + 0.05 * product.astype(F32)
     mirror, pair = together([mirror, pair], *right)

time: 471 us -> 463 us (0.983)
  waiting for transfers between devices: 253 us -> 242 us
    ppermute x21, waiting for transfers between devices: 210 us -> 198 us  [send(): return lax.ppermute(x, self.axis, pairs)]
  transfers between devices with their start and end apart: 34 -> 34, of which waited for: 17 -> 19; matrix products, arithmetic and copies ran while one was open for 11% -> 12% of each run, Pallas kernels for 14% -> 14%
where the time goes in v8:
time: 463 us; the launch traced here: 455 us
  waiting for transfers between devices  242 us (52%)
  Pallas kernels  71.6 us (15%)
  starting transfers between devices  58.5 us (13%)
  other arithmetic  33.1 us (7%)
  matrix products  24.6 us (5%)
  between operations  14.7 us (3%)
  local copies, waits for them, and re-layouts  10.3 us (2%)
    ppermute x21, waiting for transfers between devices, send(): return lax.ppermute(x, self.axis, pairs)  198 us
    pallas_call x3, Pallas kernels, part(): pl.pallas_call(functools.partial(part_kernel, results=results), grid_spec...  55.5 us
    ppermute x21, starting transfers between devices, send(): return lax.ppermute(x, self.axis, pairs)  47.8 us
    ppermute x10, waiting for transfers between devices, swap(): return lax.ppermute(x, axis, [(j, j ^ bit) for j in range(8)])  42.7 us
    pallas_call x4, Pallas kernels, products(): pl.pallas_call(products_kernel, grid_spec=pltpu.PrefetchScalarGridSpec(nu...  16.1 us
    dot_general x4, matrix products, contract_first(): lax.dot_general(first, second, (((0,), (0,)), ((), ())), preferred_elemen...  15.6 us
    ppermute x10, starting transfers between devices, swap(): return lax.ppermute(x, axis, [(j, j ^ bit) for j in range(8)])  10.7 us
  transfers between devices with their start and end apart: 34, of which 19 were waited for; matrix products, arithmetic and copies ran while one was open for 12% of the time, Pallas kernels for 14%

profile of v8, /device:TPU:0, one launch (start us, length us, event | category | flops | bytes accessed | tf_op | source)
XLA Modules:
  0.0 454.6 jit_solution(6399798838807503592)
XLA Ops:
  8.0 5.1 %collective-permute-start.1 = (bf16[1024,768]{1,0:T(8,128)(2,1)}, bf16[1024,768]{1,0:T(8,128)(2,1)S(1)}, u32[]{:S(2)}, u32[]{:S(2)}) collective-permute-start(bf16[1024,768]{1,0:T(8,128)(2,1)} %param.12), channel_id=1, source_target_pairs={{0,24},{8,16},{16,8},{24,0},{1,25},{9,17},{17,9},{25,1},{2,26},{10... | collective-permute-start | bytes 4718600 | tf_op jit(solution)/shard_map/ppermute | solution.py:58
  16.2 32.4 %collective-permute-done.1 = bf16[1024,768]{1,0:T(8,128)(2,1)S(1)} collective-permute-done((bf16[1024,768]{1,0:T(8,128)(2,1)}, bf16[1024,768]{1,0:T(8,128)(2,1)S(1)}, u32[]{:S(2)}, u32[]{:S(2)}) %collective-permute-start.1) | collective-permute-done | bytes 1572896 | tf_op jit(solution)/shard_map/ppermute | solution.py:58
  50.0 31.5 %collective-permute-done = bf16[1024,768]{1,0:T(8,128)(2,1)} collective-permute-done((bf16[1024,768]{1,0:T(8,128)(2,1)}, bf16[1024,768]{1,0:T(8,128)(2,1)}, u32[]{:S(2)}, u32[]{:S(2)}) %collective-permute-start) | collective-permute-done | bytes 1572896 | tf_op jit(solution)/shard_map/ppermute | solution.py:58
  83.6 4.1 fusion.4
  93.9 41.1 %collective-permute-done.2 = bf16[1536,256]{1,0:T(8,128)(2,1)S(1)} collective-permute-done((bf16[1536,256]{1,0:T(8,128)(2,1)S(1)}, bf16[1536,256]{1,0:T(8,128)(2,1)S(1)}, u32[]{:S(2)}, u32[]{:S(2)}) %collective-permute-start.2) | collective-permute-done | bytes 786464 | tf_op jit(solution)/shard_map/ppermute | solution.py:58
  136.8 5.7 %add_convert_fusion.2 = bf16[1024,768]{1,0:T(8,128)(2,1)} fusion(f32[1024,768]{1,0:T(8,128)S(1)} %copy-done.27, bf16[1024,768]{1,0:T(8,128)(2,1)} %collective-permute-done.5, bf16[4096,1024]{1,0:T(8,128)(2,1)} %all-gather.4.cloned.1.call-done.basis, s32[]{:T(128)S(6)} %select_n.130), kind=kOutput, calls=%fused_computation.6 | convolution fusion | flops 1612185600 | bytes 8388612 | tf_op jit(solution)/shard_map/dot_general | solution.py:29
  145.5 15.8 %collective-permute-done.4 = bf16[1536,256]{1,0:T(8,128)(2,1)S(1)} collective-permute-done((bf16[1536,256]{1,0:T(8,128)(2,1)S(1)}, bf16[1536,256]{1,0:T(8,128)(2,1)S(1)}, u32[]{:S(2)}, u32[]{:S(2)}) %collective-permute-start.4) | collective-permute-done | bytes 786464 | tf_op jit(solution)/shard_map/ppermute | solution.py:58
  163.2 17.5 %collective-permute-done.6 = bf16[1536,256]{1,0:T(8,128)(2,1)S(1)} collective-permute-done((bf16[1536,256]{1,0:T(8,128)(2,1)S(1)}, bf16[1536,256]{1,0:T(8,128)(2,1)S(1)}, u32[]{:S(2)}, u32[]{:S(2)}) %collective-permute-start.6) | collective-permute-done | bytes 786464 | tf_op jit(solution)/shard_map/ppermute | solution.py:58
  188.8 9.1 %convolution_convert_fusion = bf16[4096,1024]{1,0:T(8,128)(2,1)} fusion(bf16[4096,768]{1,0:T(8,128)(2,1)S(1)} %constant_dynamic-update-slice_fusion, bf16[1024,768]{1,0:T(8,128)(2,1)S(1)} %copy-done.10), kind=kOutput, calls=%fused_computation | convolution fusion | flops 6446645248 | bytes 16252928 | tf_op jit(solution)/shard_map/dot_general | solution.py:25
  197.9 20.4 %collective-permute-done.7.out = bf16[3072,256]{1,0:T(8,128)(2,1)} collective-permute-done((bf16[3072,256]{1,0:T(8,128)(2,1)}, bf16[3072,256]{1,0:T(8,128)(2,1)}, u32[]{:S(2)}, u32[]{:S(2)}) %collective-permute-start.7) | collective-permute-done | bytes 1572896 | tf_op jit(solution)/shard_map/ppermute | solution.py:58
  223.2 19.7 %shard_map.147 = (f32[1024,768]{1,0:T(8,128)}, f32[1024,768]{1,0:T(8,128)}, bf16[2048,256]{1,0:T(8,128)(2,1)}, bf16[2048,256]{1,0:T(8,128)(2,1)}) custom-call(s32[5]{0:T(128)} %pad_add_fusion.place, bf16[8,1024,768]{2,1,0:T(8,128)(2,1)} %bitcast.8, bf16[3072,256]{1,0:T(8,128)(2,1)} %copy-done.1, bf16[3072,256]{1,0:T(8,128)(2,1)} %collective-permute-done.3.middle, ...), custom_call_target="tpu_custom_call" | custom-call | flops 1048576 | bytes 65536 | tf_op jit(solution)/shard_map/pallas_call | solution.py:211
  242.9 9.5 %collective-permute-start.13 = (bf16[2048,256]{1,0:T(8,128)(2,1)}, bf16[2048,256]{1,0:T(8,128)(2,1)}, u32[]{:S(2)}, u32[]{:S(2)}) collective-permute-start(bf16[2048,256]{1,0:T(8,128)(2,1)} %get-tuple-element.85), channel_id=1, source_target_pairs={{0,8},{24,16},{1,9},{25,17},{2,10},{26,18},{3,11},{27,19},{4,12},{... | collective-permute-start | bytes 3145736 | tf_op jit(solution)/shard_map/ppermute | solution.py:58
  257.8 17.7 %shard_map.148 = (f32[1024,768]{1,0:T(8,128)}, f32[1024,768]{1,0:T(8,128)}, bf16[2048,256]{1,0:T(8,128)(2,1)}, bf16[2048,256]{1,0:T(8,128)(2,1)}) custom-call(s32[5]{0:T(128)} %pad_add_fusion.place, bf16[8,1024,768]{2,1,0:T(8,128)(2,1)} %bitcast.9, bf16[3072,256]{1,0:T(8,128)(2,1)} %maximum_select_fusion.4.near, ...), custom_call_target="tpu_custom_call", output_to_operand_aliasing={{0}: (8, {}), {1}: (9, {})} | custom-call | flops 1048576 | bytes 65536 | tf_op jit(solution)/shard_map/pallas_call | solution.py:211
  275.6 7.8 %collective-permute-start.10 = (bf16[2048,256]{1,0:T(8,128)(2,1)}, bf16[2048,256]{1,0:T(8,128)(2,1)}, u32[]{:S(2)}, u32[]{:S(2)}) collective-permute-start(bf16[2048,256]{1,0:T(8,128)(2,1)} %get-tuple-element.89), channel_id=1, source_target_pairs={{0,8},{24,16},{1,9},{25,17},{2,10},{26,18},{3,11},{27,19},{4,12},{... | collective-permute-start | bytes 3145736 | tf_op jit(solution)/shard_map/ppermute | solution.py:58
  287.9 12.8 %collective-permute-done.10 = bf16[2048,256]{1,0:T(8,128)(2,1)} collective-permute-done((bf16[2048,256]{1,0:T(8,128)(2,1)}, bf16[2048,256]{1,0:T(8,128)(2,1)}, u32[]{:S(2)}, u32[]{:S(2)}) %collective-permute-start.10) | collective-permute-done | bytes 1048608 | tf_op jit(solution)/shard_map/ppermute | solution.py:58
  311.3 18.1 %shard_map.149 = (f32[1024,768]{1,0:T(8,128)}, f32[1024,768]{1,0:T(8,128)}, bf16[1024,256]{1,0:T(8,128)(2,1)}, bf16[1024,256]{1,0:T(8,128)(2,1)}, bf16[1024,256]{1,0:T(8,128)(2,1)}, /*index=5*/bf16[1024,256]{1,0:T(8,128)(2,1)}) custom-call(s32[7]{0:T(128)} %pad_add_fusion.1.place, ...), custom_call_target="tpu_custom_call", output_to_operand_aliasing={{0}: (8, {}), {1}: (9, {})} | custom-call | flops 1048576 | bytes 65536 | tf_op jit(solution)/shard_map/pallas_call | solution.py:211
  350.6 10.5 %collective-permute-done.20 = bf16[1024,256]{1,0:T(8,128)(2,1)} collective-permute-done((bf16[1024,256]{1,0:T(8,128)(2,1)}, bf16[1024,256]{1,0:T(8,128)(2,1)}, u32[]{:S(2)}, u32[]{:S(2)}) %collective-permute-start.20) | collective-permute-done | bytes 524320 | tf_op jit(solution)/shard_map/ppermute | solution.py:58
  361.1 6.1 %collective-permute-done.19 = bf16[1024,256]{1,0:T(8,128)(2,1)S(1)} collective-permute-done((bf16[1024,256]{1,0:T(8,128)(2,1)S(1)}, bf16[1024,256]{1,0:T(8,128)(2,1)S(1)}, u32[]{:S(2)}, u32[]{:S(2)}) %collective-permute-start.19) | collective-permute-done | bytes 524320 | tf_op jit(solution)/shard_map/ppermute | solution.py:58
  368.5 4.2 collective-permute-done.17
  373.0 4.0 shard_map.150
  397.0 11.4 %collective-permute-done.22 = bf16[256,1536]{1,0:T(8,128)(2,1)S(1)} collective-permute-done((bf16[256,1536]{1,0:T(8,128)(2,1)S(1)}, bf16[256,1536]{1,0:T(8,128)(2,1)S(1)}, u32[]{:S(2)}, u32[]{:S(2)}) %collective-permute-start.22) | collective-permute-done | bytes 786464 | tf_op jit(solution)/shard_map/ppermute | solution.py:104
  414.2 16.4 %collective-permute-done.27 = bf16[256,1536]{1,0:T(8,128)(2,1)S(1)} collective-permute-done((bf16[256,1536]{1,0:T(8,128)(2,1)S(1)}, bf16[256,1536]{1,0:T(8,128)(2,1)S(1)}, u32[]{:S(2)}, u32[]{:S(2)}) %collective-permute-start.27) | collective-permute-done | bytes 786464 | tf_op jit(solution)/shard_map/ppermute | solution.py:104
  434.3 5.2 %collective-permute-done.25 = bf16[256,768]{1,0:T(8,128)(2,1)S(1)} collective-permute-done((bf16[256,768]{1,0:T(8,128)(2,1)S(1)}, bf16[256,768]{1,0:T(8,128)(2,1)S(1)}, u32[]{:S(2)}, u32[]{:S(2)}) %collective-permute-start.25) | collective-permute-done | bytes 393248 | tf_op jit(solution)/shard_map/ppermute | solution.py:104
  439.8 6.3 %collective-permute-done.29 = bf16[256,768]{1,0:T(8,128)(2,1)S(1)} collective-permute-done((bf16[256,768]{1,0:T(8,128)(2,1)S(1)}, bf16[256,768]{1,0:T(8,128)(2,1)S(1)}, u32[]{:S(2)}, u32[]{:S(2)}) %collective-permute-start.29) | collective-permute-done | bytes 393248 | tf_op jit(solution)/shard_map/ppermute | solution.py:104
  (160 shorter events, 107.5 us)
Async XLA Ops:
  7.2 76.4 %all-gather.4.cloned.1.call-start = ((), (), s32[]{:S(2)}) async-start(), calls=%async_computation.1 | async-start | bytes 9437184 | tf_op jit(solution)/shard_map/all_gather | solution.py:243
  7.9 215.3 %all-gather.6.cloned.1.call-start = ((), (), s32[]{:S(2)}) async-start(), calls=%async_computation.3 | async-start | bytes 14155776 | tf_op jit(solution)/shard_map/all_gather | solution.py:260
  8.0 40.6 %collective-permute-start.1 = (bf16[1024,768]{1,0:T(8,128)(2,1)}, bf16[1024,768]{1,0:T(8,128)(2,1)S(1)}, u32[]{:S(2)}, u32[]{:S(2)}) collective-permute-start(bf16[1024,768]{1,0:T(8,128)(2,1)} %param.12), channel_id=1, source_target_pairs={{0,24},{8,16},{16,8},{24,0},{1,25},{9,17},{17,9},{25,1},{2,26},{10... | collective-permute-start | bytes 4718600 | tf_op jit(solution)/shard_map/ppermute | solution.py:58
  13.1 68.5 %collective-permute-start = (bf16[1024,768]{1,0:T(8,128)(2,1)}, bf16[1024,768]{1,0:T(8,128)(2,1)}, u32[]{:S(2)}, u32[]{:S(2)}) collective-permute-start(bf16[1024,768]{1,0:T(8,128)(2,1)} %param.12), channel_id=1, source_target_pairs={{0,8},{8,0},{16,24},{24,16},{1,9},{9,1},{17,25},{25,17},{2,10},{10... | collective-permute-start | bytes 4718600 | tf_op jit(solution)/shard_map/ppermute | solution.py:58
  81.6 55.2 %collective-permute-start.5 = (bf16[1024,768]{1,0:T(8,128)(2,1)}, bf16[1024,768]{1,0:T(8,128)(2,1)}, u32[]{:S(2)}, u32[]{:S(2)}) collective-permute-start(bf16[1024,768]{1,0:T(8,128)(2,1)} %broadcast_select_fusion.3), channel_id=1, source_target_pairs={{0,16},{8,0},{16,24},{24,8},{1,17},{9,1},{17,25},{25,9},{2,18},{10... | collective-permute-start | bytes 4718600 | tf_op jit(solution)/shard_map/ppermute | solution.py:58
  93.8 41.2 %collective-permute-start.2 = (bf16[1536,256]{1,0:T(8,128)(2,1)S(1)}, bf16[1536,256]{1,0:T(8,128)(2,1)S(1)}, u32[]{:S(2)}, u32[]{:S(2)}) collective-permute-start(bf16[1536,256]{1,0:T(8,128)(2,1)S(1)} %copy-done.15), channel_id=1, source_target_pairs={{0,8},{8,0},{16,24},{24,16},{1,9},{9,1},{17,25},{25,17},{2,10},{10... | collective-permute-start | bytes 2359304 | tf_op jit(solution)/shard_map/ppermute | solution.py:58
  142.6 189.7 %reduce-scatter.2.cloned.1.call-start = ((), (), s32[]{:S(2)}) async-start(), calls=%async_computation.2 | async-start | bytes 9437184 | tf_op jit(solution)/shard_map/reduce_scatter | solution.py:270
  143.7 38.5 %collective-permute-start.3 = (bf16[3072,256]{1,0:T(8,128)(2,1)S(1)}, bf16[3072,256]{1,0:T(8,128)(2,1)}, u32[]{:S(2)}, u32[]{:S(2)}) collective-permute-start(bf16[3072,256]{1,0:T(8,128)(2,1)S(1)} %maximum_select_fusion.3.near), channel_id=1, source_target_pairs={{8,16},{16,8},{9,17},{17,9},{10,18},{18,10},{11,19},{19,11},{12,20... | collective-permute-start | bytes 4718600 | tf_op jit(solution)/shard_map/ppermute | solution.py:58
  182.2 36.1 %collective-permute-start.7 = (bf16[3072,256]{1,0:T(8,128)(2,1)}, bf16[3072,256]{1,0:T(8,128)(2,1)}, u32[]{:S(2)}, u32[]{:S(2)}) collective-permute-start(bf16[3072,256]{1,0:T(8,128)(2,1)} %collective-permute-done.3.middle), channel_id=1, source_target_pairs={{8,0},{16,24},{9,1},{17,25},{10,2},{18,26},{11,3},{19,27},{12,4},{... | collective-permute-start | bytes 4718600 | tf_op jit(solution)/shard_map/ppermute | solution.py:58
  183.7 34.6 %collective-permute-start.8 = (bf16[3072,256]{1,0:T(8,128)(2,1)}, bf16[3072,256]{1,0:T(8,128)(2,1)S(1)}, u32[]{:S(2)}, u32[]{:S(2)}) collective-permute-start(bf16[3072,256]{1,0:T(8,128)(2,1)} %maximum_select_fusion.4.near), channel_id=1, source_target_pairs={{8,16},{16,8},{9,17},{17,9},{10,18},{18,10},{11,19},{19,11},{12,20... | collective-permute-start | bytes 4718600 | tf_op jit(solution)/shard_map/ppermute | solution.py:58
  219.4 36.9 %collective-permute-start.9 = (bf16[3072,256]{1,0:T(8,128)(2,1)S(1)}, bf16[3072,256]{1,0:T(8,128)(2,1)}, u32[]{:S(2)}, u32[]{:S(2)}) collective-permute-start(bf16[3072,256]{1,0:T(8,128)(2,1)S(1)} %collective-permute-done.8.middle), channel_id=1, source_target_pairs={{8,0},{16,24},{9,1},{17,25},{10,2},{18,26},{11,3},{19,27},{12,4},{... | collective-permute-start | bytes 4718600 | tf_op jit(solution)/shard_map/ppermute | solution.py:58
  220.7 35.6 %collective-permute-start.11 = (bf16[3072,256]{1,0:T(8,128)(2,1)S(1)}, bf16[3072,256]{1,0:T(8,128)(2,1)}, u32[]{:S(2)}, u32[]{:S(2)}) collective-permute-start(bf16[3072,256]{1,0:T(8,128)(2,1)S(1)} %copy-done.3), channel_id=1, source_target_pairs={{8,16},{16,8},{9,17},{17,9},{10,18},{18,10},{11,19},{19,11},{12,20... | collective-permute-start | bytes 4718600 | tf_op jit(solution)/shard_map/ppermute | solution.py:58
  242.9 40.5 %collective-permute-start.13 = (bf16[2048,256]{1,0:T(8,128)(2,1)}, bf16[2048,256]{1,0:T(8,128)(2,1)}, u32[]{:S(2)}, u32[]{:S(2)}) collective-permute-start(bf16[2048,256]{1,0:T(8,128)(2,1)} %get-tuple-element.85), channel_id=1, source_target_pairs={{0,8},{24,16},{1,9},{25,17},{2,10},{26,18},{3,11},{27,19},{4,12},{... | collective-permute-start | bytes 3145736 | tf_op jit(solution)/shard_map/ppermute | solution.py:58
  256.3 44.4 %collective-permute-start.12 = (bf16[3072,256]{1,0:T(8,128)(2,1)}, bf16[3072,256]{1,0:T(8,128)(2,1)S(1)}, u32[]{:S(2)}, u32[]{:S(2)}) collective-permute-start(bf16[3072,256]{1,0:T(8,128)(2,1)} %collective-permute-done.11.middle), channel_id=1, source_target_pairs={{8,0},{16,24},{9,1},{17,25},{10,2},{18,26},{11,3},{19,27},{12,4},{... | collective-permute-start | bytes 4718600 | tf_op jit(solution)/shard_map/ppermute | solution.py:58
  275.6 25.2 %collective-permute-start.10 = (bf16[2048,256]{1,0:T(8,128)(2,1)}, bf16[2048,256]{1,0:T(8,128)(2,1)}, u32[]{:S(2)}, u32[]{:S(2)}) collective-permute-start(bf16[2048,256]{1,0:T(8,128)(2,1)} %get-tuple-element.89), channel_id=1, source_target_pairs={{0,8},{24,16},{1,9},{25,17},{2,10},{26,18},{3,11},{27,19},{4,12},{... | collective-permute-start | bytes 3145736 | tf_op jit(solution)/shard_map/ppermute | solution.py:58
  305.4 26.6 %collective-permute-start.15 = (bf16[1024,256]{1,0:T(8,128)(2,1)S(1)}, bf16[1024,256]{1,0:T(8,128)(2,1)S(1)}, u32[]{:S(2)}, u32[]{:S(2)}) collective-permute-start(bf16[1024,256]{1,0:T(8,128)(2,1)S(1)} %select_convert_fusion.1), channel_id=1, source_target_pairs={{0,8},{8,0},{16,24},{24,16},{1,9},{9,1},{17,25},{25,17},{2,10},{10... | collective-permute-start | bytes 1572872 | tf_op jit(solution)/shard_map/ppermute | solution.py:58
  309.6 33.9 %collective-permute-start.16 = (bf16[2048,256]{1,0:T(8,128)(2,1)}, bf16[2048,256]{1,0:T(8,128)(2,1)}, u32[]{:S(2)}, u32[]{:S(2)}) collective-permute-start(bf16[2048,256]{1,0:T(8,128)(2,1)} %add_convert_fusion.3), channel_id=1, source_target_pairs={{8,16},{16,8},{9,17},{17,9},{10,18},{18,10},{11,19},{19,11},{12,20... | collective-permute-start | bytes 3145736 | tf_op jit(solution)/shard_map/ppermute | solution.py:58
  330.8 30.3 %collective-permute-start.20 = (bf16[1024,256]{1,0:T(8,128)(2,1)}, bf16[1024,256]{1,0:T(8,128)(2,1)}, u32[]{:S(2)}, u32[]{:S(2)}) collective-permute-start(bf16[1024,256]{1,0:T(8,128)(2,1)} %get-tuple-element.108), channel_id=1, source_target_pairs={{0,8},{8,0},{16,24},{24,16},{1,9},{9,1},{17,25},{25,17},{2,10},{10... | collective-permute-start | bytes 1572872 | tf_op jit(solution)/shard_map/ppermute | solution.py:58
  343.7 23.5 %collective-permute-start.19 = (bf16[1024,256]{1,0:T(8,128)(2,1)S(1)}, bf16[1024,256]{1,0:T(8,128)(2,1)S(1)}, u32[]{:S(2)}, u32[]{:S(2)}) collective-permute-start(bf16[1024,256]{1,0:T(8,128)(2,1)S(1)} %add_convert_fusion.6), channel_id=1, source_target_pairs={{0,24},{8,16},{16,8},{24,0},{1,25},{9,17},{17,9},{25,1},{2,26},{10... | collective-permute-start | bytes 1572872 | tf_op jit(solution)/shard_map/ppermute | solution.py:58
  348.8 24.0 %collective-permute-start.17 = (bf16[1024,256]{1,0:T(8,128)(2,1)S(1)}, bf16[1024,256]{1,0:T(8,128)(2,1)S(1)}, u32[]{:S(2)}, u32[]{:S(2)}) collective-permute-start(bf16[1024,256]{1,0:T(8,128)(2,1)S(1)} %select_convert_fusion), channel_id=1, source_target_pairs={{0,8},{8,0},{16,24},{24,16},{1,9},{9,1},{17,25},{25,17},{2,10},{10... | collective-permute-start | bytes 1572872 | tf_op jit(solution)/shard_map/ppermute | solution.py:58
  410.1 20.5 %collective-permute-start.27 = (bf16[256,1536]{1,0:T(8,128)(2,1)S(1)}, bf16[256,1536]{1,0:T(8,128)(2,1)S(1)}, u32[]{:S(2)}, u32[]{:S(2)}) collective-permute-start(bf16[256,1536]{1,0:T(8,128)(2,1)S(1)} %pad_maximum_fusion.2), channel_id=1, source_target_pairs={{0,2},{1,3},{2,0},{3,1},{4,6},{5,7},{6,4},{7,5},{8,10},{9,11},{10,... | collective-permute-start | bytes 2359304 | tf_op jit(solution)/shard_map/ppermute | solution.py:104
  410.5 20.5 %collective-permute-start.28 = (bf16[256,1536]{1,0:T(8,128)(2,1)S(1)}, bf16[256,1536]{1,0:T(8,128)(2,1)S(1)}, u32[]{:S(2)}, u32[]{:S(2)}) collective-permute-start(bf16[256,1536]{1,0:T(8,128)(2,1)S(1)} %concatenate.81), channel_id=1, source_target_pairs={{0,4},{1,5},{2,6},{3,7},{4,0},{5,1},{6,2},{7,3},{8,12},{9,13},{10,... | collective-permute-start | bytes 2359304 | tf_op jit(solution)/shard_map/ppermute | solution.py:104
  412.1 27.3 %collective-permute-start.25 = (bf16[256,768]{1,0:T(8,128)(2,1)S(1)}, bf16[256,768]{1,0:T(8,128)(2,1)S(1)}, u32[]{:S(2)}, u32[]{:S(2)}) collective-permute-start(bf16[256,768]{1,0:T(8,128)(2,1)S(1)} %get-tuple-element.130), channel_id=1, source_target_pairs={{0,4},{1,5},{2,6},{3,7},{4,0},{5,1},{6,2},{7,3},{8,12},{9,13},{10,... | collective-permute-start | bytes 1179656 | tf_op jit(solution)/shard_map/ppermute | solution.py:104
  412.5 26.9 %collective-permute-start.26 = (bf16[256,768]{1,0:T(8,128)(2,1)S(1)}, bf16[256,768]{1,0:T(8,128)(2,1)S(1)}, u32[]{:S(2)}, u32[]{:S(2)}) collective-permute-start(bf16[256,768]{1,0:T(8,128)(2,1)S(1)} %get-tuple-element.131), channel_id=1, source_target_pairs={{0,2},{1,3},{2,0},{3,1},{4,6},{5,7},{6,4},{7,5},{8,10},{9,11},{10,... | collective-permute-start | bytes 1179656 | tf_op jit(solution)/shard_map/ppermute | solution.py:104
  (38 other events, 498.3 us)
Sparse Core Ops, SparseCore 0:
  9.9 57.0 all-gather.3
  142.7 71.3 all-gather.5
  218.5 73.7 reduce-scatter.1

commit v9 on v8

--- a/solution.py
+++ b/solution.py
@@ -82,14 +82,15 @@
 
 
 def products(rows, half, right, order, start):
-    height, depth = rows[0].shape[0] // 2, rows[0].shape[1]
+    height, depth = rows[-1].shape
     width = right[0].shape[0] // 8
     return pl.pallas_call(
         products_kernel,
         grid_spec=pltpu.PrefetchScalarGridSpec(
             num_scalar_prefetch=1,
             grid=(4,),
-            in_specs=[pl.BlockSpec((height, depth), lambda b, order: (half, 0))] * len(rows)
+            in_specs=[pl.BlockSpec((height, depth), lambda b, order: (half, 0))] * (len(rows) - 1)
+            + [pl.BlockSpec((height, depth), lambda b, order: (0, 0))]
             + [pl.BlockSpec((width, depth), lambda b, order: (order[start + b], 0))] * len(right),
             out_specs=pl.BlockSpec((height, width), lambda b, order: (0, b)),
         ),
@@ -99,13 +100,13 @@
     )(order, *rows, *right)
 
 
-def scatter_columns(rows, right, axis):
+def scatter_columns(rows, rows_low, rows_high, right, axis):
     def swap(x, bit):
         return lax.ppermute(x, axis, [(j, j ^ bit) for j in range(8)])
 
     order = lax.axis_index(axis) ^ jnp.array([0, 2, 4, 6, 1, 3, 5, 7], jnp.int32)
     width = right[0].shape[0] // 8
-    height = rows[0].shape[0] // 2
+    height = rows_low.shape[0]
     low, high = slice(0, height // 2), slice(height // 2, height)
 
     def pair_sum(half, rows):
@@ -129,14 +130,13 @@
         total = lambda a, b, c: a.astype(F32) + b[:, :width].astype(F32) + c.astype(F32)
         return [total(block(x, 0, low), by_x, then_y), total(block(x, 0, high), by_y, then_x)]
 
-    sum0 = pair_sum(0, rows)
+    sum0 = pair_sum(0, rows + [rows_low])
     by_x0, by_y0 = together(first_sends(sum0))
     by_x0, by_y0 = swap(by_x0, 2), swap(by_y0, 4)
-    sum1 = pair_sum(1, together(rows, sum0))
-    then_y0, then_x0, by_x1, by_y1 = together(
-        second_sends(sum0, *together([by_x0, by_y0], sum1)) + first_sends(sum1)
-    )
+    then_y0, then_x0 = together(second_sends(sum0, by_x0, by_y0))
+    sum1 = pair_sum(1, rows + [rows_high(then_y0)])
     then_y0, then_x0 = swap(then_y0, 4), swap(then_x0, 2)
+    by_x1, by_y1 = together(first_sends(sum1), then_y0, then_x0)
     by_x1, by_y1 = swap(by_x1, 2), swap(by_y1, 4)
     then_y1, then_x1 = together(second_sends(sum1, by_x1, by_y1))
     then_y1, then_x1 = swap(then_y1, 4), swap(then_x1, 2)
@@ -303,20 +303,33 @@
     turned1 = (mine1 + send(other1.astype(BF16), PAIRS).astype(F32)).astype(BF16)
     first_next, second_next = moments2
 
-    to_relay, to_pair, to_mirror, own = blocks2
-    relay = send(to_relay, RELAY_BACK)
-    pair = send(to_pair, PAIRS)
-    relay = after(relay, through1, other0)
-    mirror = send(add(to_mirror, jnp.where(line.inner, relay, 0)), MIRROR)
+    half = height // 2
+    low, high = [x[:half] for x in blocks2], [x[half:] for x in blocks2]
+
+    def summed(blocks, relay, pair, mirror):
+        total = blocks[3].astype(F32) + jnp.where(line.inner, 0, relay).astype(F32)
+        return (total + pair.astype(F32) + mirror.astype(F32)).astype(BF16)
+
+    relay_low = send(low[0], RELAY_BACK)
+    pair_low = send(low[1], PAIRS)
+    relay_low = after(relay_low, through1, other0)
+    to_mirror = add(low[2], jnp.where(line.inner, relay_low, 0))
+    mirror_low = send(to_mirror, MIRROR)
+    to_relay, to_pair = together(high[:2], relay_low)
+    relay_high = send(to_relay, RELAY_BACK)
+    pair_high = send(to_pair, PAIRS)
     out0, out1, out2, product = together([out0, out1, out2, product], turned0)
     right = [line.whole(near0, middle0, out0), line.whole(near1, middle1, out1), line.whole(near2, middle2, out2)]
     left_next = 0.95 * left_stat + 0.05 * product.astype(F32)
-    mirror, pair = together([mirror, pair], *right)
-    turned2 = own.astype(F32) + jnp.where(line.inner, 0, relay).astype(F32)
-    turned2 = (turned2 + pair.astype(F32) + mirror.astype(F32)).astype(BF16)
+    relay_high = after(relay_high, to_mirror)
+    mirror_high = send(add(high[2], jnp.where(line.inner, relay_high, 0)), MIRROR)
+    turned_low = summed(low, relay_low, pair_low, after(mirror_low, *right))
+
+    def turned_high(earlier):
+        return summed(high, relay_high, pair_high, after(mirror_high, earlier))
 
     right = together(right, left_next)
-    direction = scatter_columns([turned0, turned1, turned2], right, "col")
+    direction = scatter_columns([turned0, turned1], turned_low, turned_high, right, "col")
     return (left_next, first_next, second_next, direction)
 
 

time: 463 us -> 456 us (0.985)
  waiting for transfers between devices: 242 us -> 231 us
    ppermute x21 -> x24, waiting for transfers between devices: 198 us -> 192 us  [send(): return lax.ppermute(x, self.axis, pairs)]
    ppermute x21 -> x24, starting transfers between devices: 47.8 us -> 51.4 us  [send(): return lax.ppermute(x, self.axis, pairs)]
  transfers between devices with their start and end apart: 34 -> 37, of which waited for: 19 -> 21; matrix products, arithmetic and copies ran while one was open for 12% -> 13% of each run, Pallas kernels for 14% -> 14%
where the time goes in v9:
time: 456 us; the launch traced here: 448 us
  waiting for transfers between devices  231 us (51%)
  Pallas kernels  71.5 us (16%)
  starting transfers between devices  61.7 us (14%)
  other arithmetic  31.8 us (7%)
  matrix products  24.6 us (5%)
  between operations  14.7 us (3%)
  local copies, waits for them, and re-layouts  12.2 us (3%)
    ppermute x24, waiting for transfers between devices, send(): return lax.ppermute(x, self.axis, pairs)  192 us
    pallas_call x3, Pallas kernels, part(): pl.pallas_call(functools.partial(part_kernel, results=results), grid_spec...  55.4 us
    ppermute x24, starting transfers between devices, send(): return lax.ppermute(x, self.axis, pairs)  51.4 us
    ppermute x10, waiting for transfers between devices, swap(): return lax.ppermute(x, axis, [(j, j ^ bit) for j in range(8)])  38.4 us
    pallas_call x4, Pallas kernels, products(): pl.pallas_call(products_kernel, grid_spec=pltpu.PrefetchScalarGridSpec(nu...  16.1 us
    dot_general x4, matrix products, contract_first(): lax.dot_general(first, second, (((0,), (0,)), ((), ())), preferred_elemen...  15.6 us
    ppermute x10, starting transfers between devices, swap(): return lax.ppermute(x, axis, [(j, j ^ bit) for j in range(8)])  10.3 us
  transfers between devices with their start and end apart: 37, of which 21 were waited for; matrix products, arithmetic and copies ran while one was open for 13% of the time, Pallas kernels for 14%

profile of v9, /device:TPU:0, one launch (start us, length us, event | category | flops | bytes accessed | tf_op | source)
XLA Modules:
  0.0 447.9 jit_solution(13567519429985320845)
XLA Ops:
  8.0 5.1 %collective-permute-start.1 = (bf16[1024,768]{1,0:T(8,128)(2,1)}, bf16[1024,768]{1,0:T(8,128)(2,1)S(1)}, u32[]{:S(2)}, u32[]{:S(2)}) collective-permute-start(bf16[1024,768]{1,0:T(8,128)(2,1)} %param.12), channel_id=1, source_target_pairs={{0,24},{8,16},{16,8},{24,0},{1,25},{9,17},{17,9},{25,1},{2,26},{10... | collective-permute-start | bytes 4718600 | tf_op jit(solution)/shard_map/ppermute | solution.py:58
  16.2 32.4 %collective-permute-done.1 = bf16[1024,768]{1,0:T(8,128)(2,1)S(1)} collective-permute-done((bf16[1024,768]{1,0:T(8,128)(2,1)}, bf16[1024,768]{1,0:T(8,128)(2,1)S(1)}, u32[]{:S(2)}, u32[]{:S(2)}) %collective-permute-start.1) | collective-permute-done | bytes 1572896 | tf_op jit(solution)/shard_map/ppermute | solution.py:58
  50.0 31.5 %collective-permute-done = bf16[1024,768]{1,0:T(8,128)(2,1)} collective-permute-done((bf16[1024,768]{1,0:T(8,128)(2,1)}, bf16[1024,768]{1,0:T(8,128)(2,1)}, u32[]{:S(2)}, u32[]{:S(2)}) %collective-permute-start) | collective-permute-done | bytes 1572896 | tf_op jit(solution)/shard_map/ppermute | solution.py:58
  83.6 4.1 fusion.4
  93.9 41.1 %collective-permute-done.2 = bf16[1536,256]{1,0:T(8,128)(2,1)S(1)} collective-permute-done((bf16[1536,256]{1,0:T(8,128)(2,1)S(1)}, bf16[1536,256]{1,0:T(8,128)(2,1)S(1)}, u32[]{:S(2)}, u32[]{:S(2)}) %collective-permute-start.2) | collective-permute-done | bytes 786464 | tf_op jit(solution)/shard_map/ppermute | solution.py:58
  136.8 5.7 %add_convert_fusion.2 = bf16[1024,768]{1,0:T(8,128)(2,1)} fusion(f32[1024,768]{1,0:T(8,128)S(1)} %copy-done.26, bf16[1024,768]{1,0:T(8,128)(2,1)} %collective-permute-done.5, bf16[4096,1024]{1,0:T(8,128)(2,1)} %all-gather.4.cloned.1.call-done.basis, s32[]{:T(128)S(6)} %select_n.138), kind=kOutput, calls=%fused_computation.6 | convolution fusion | flops 1612185600 | bytes 8388612 | tf_op jit(solution)/shard_map/dot_general | solution.py:29
  145.5 15.8 %collective-permute-done.4 = bf16[1536,256]{1,0:T(8,128)(2,1)S(1)} collective-permute-done((bf16[1536,256]{1,0:T(8,128)(2,1)S(1)}, bf16[1536,256]{1,0:T(8,128)(2,1)S(1)}, u32[]{:S(2)}, u32[]{:S(2)}) %collective-permute-start.4) | collective-permute-done | bytes 786464 | tf_op jit(solution)/shard_map/ppermute | solution.py:58
  163.2 17.5 %collective-permute-done.6 = bf16[1536,256]{1,0:T(8,128)(2,1)S(1)} collective-permute-done((bf16[1536,256]{1,0:T(8,128)(2,1)S(1)}, bf16[1536,256]{1,0:T(8,128)(2,1)S(1)}, u32[]{:S(2)}, u32[]{:S(2)}) %collective-permute-start.6) | collective-permute-done | bytes 786464 | tf_op jit(solution)/shard_map/ppermute | solution.py:58
  189.7 9.1 %convolution_convert_fusion = bf16[4096,1024]{1,0:T(8,128)(2,1)} fusion(bf16[4096,768]{1,0:T(8,128)(2,1)S(1)} %constant_dynamic-update-slice_fusion, bf16[1024,768]{1,0:T(8,128)(2,1)S(1)} %copy-done.8), kind=kOutput, calls=%fused_computation | convolution fusion | flops 6446645248 | bytes 16252928 | tf_op jit(solution)/shard_map/dot_general | solution.py:25
  198.8 19.5 %collective-permute-done.7.out = bf16[3072,256]{1,0:T(8,128)(2,1)} collective-permute-done((bf16[3072,256]{1,0:T(8,128)(2,1)}, bf16[3072,256]{1,0:T(8,128)(2,1)}, u32[]{:S(2)}, u32[]{:S(2)}) %collective-permute-start.7) | collective-permute-done | bytes 1572896 | tf_op jit(solution)/shard_map/ppermute | solution.py:58
  222.1 19.4 %shard_map.147 = (f32[1024,768]{1,0:T(8,128)}, f32[1024,768]{1,0:T(8,128)}, bf16[2048,256]{1,0:T(8,128)(2,1)}, bf16[2048,256]{1,0:T(8,128)(2,1)}) custom-call(s32[5]{0:T(128)} %pad_add_fusion.place, bf16[8,1024,768]{2,1,0:T(8,128)(2,1)} %bitcast.8, bf16[3072,256]{1,0:T(8,128)(2,1)} %copy-done.1, bf16[3072,256]{1,0:T(8,128)(2,1)} %collective-permute-done.3.middle, ...), custom_call_target="tpu_custom_call" | custom-call | flops 1048576 | bytes 65536 | tf_op jit(solution)/shard_map/pallas_call | solution.py:211
  241.5 10.0 %collective-permute-start.13 = (bf16[2048,256]{1,0:T(8,128)(2,1)}, bf16[2048,256]{1,0:T(8,128)(2,1)}, u32[]{:S(2)}, u32[]{:S(2)}) collective-permute-start(bf16[2048,256]{1,0:T(8,128)(2,1)} %get-tuple-element.83), channel_id=1, source_target_pairs={{0,8},{24,16},{1,9},{25,17},{2,10},{26,18},{3,11},{27,19},{4,12},{... | collective-permute-start | bytes 3145736 | tf_op jit(solution)/shard_map/ppermute | solution.py:58
  251.5 4.1 collective-permute-done.9.out
  257.1 17.8 %shard_map.148 = (f32[1024,768]{1,0:T(8,128)}, f32[1024,768]{1,0:T(8,128)}, bf16[2048,256]{1,0:T(8,128)(2,1)}, bf16[2048,256]{1,0:T(8,128)(2,1)}) custom-call(s32[5]{0:T(128)} %pad_add_fusion.place, bf16[8,1024,768]{2,1,0:T(8,128)(2,1)} %bitcast.9, bf16[3072,256]{1,0:T(8,128)(2,1)} %maximum_select_fusion.4.near, ...), custom_call_target="tpu_custom_call", output_to_operand_aliasing={{0}: (8, {}), {1}: (9, {})} | custom-call | flops 1048576 | bytes 65536 | tf_op jit(solution)/shard_map/pallas_call | solution.py:211
  274.9 7.4 %collective-permute-start.10 = (bf16[2048,256]{1,0:T(8,128)(2,1)}, bf16[2048,256]{1,0:T(8,128)(2,1)}, u32[]{:S(2)}, u32[]{:S(2)}) collective-permute-start(bf16[2048,256]{1,0:T(8,128)(2,1)} %get-tuple-element.87), channel_id=1, source_target_pairs={{0,8},{24,16},{1,9},{25,17},{2,10},{26,18},{3,11},{27,19},{4,12},{... | collective-permute-start | bytes 3145736 | tf_op jit(solution)/shard_map/ppermute | solution.py:58
  286.8 13.0 %collective-permute-done.10 = bf16[2048,256]{1,0:T(8,128)(2,1)} collective-permute-done((bf16[2048,256]{1,0:T(8,128)(2,1)}, bf16[2048,256]{1,0:T(8,128)(2,1)}, u32[]{:S(2)}, u32[]{:S(2)}) %collective-permute-start.10) | collective-permute-done | bytes 1048608 | tf_op jit(solution)/shard_map/ppermute | solution.py:58
  310.3 18.1 %shard_map.149 = (f32[1024,768]{1,0:T(8,128)}, f32[1024,768]{1,0:T(8,128)}, bf16[1024,256]{1,0:T(8,128)(2,1)}, bf16[1024,256]{1,0:T(8,128)(2,1)}, bf16[1024,256]{1,0:T(8,128)(2,1)}, /*index=5*/bf16[1024,256]{1,0:T(8,128)(2,1)}) custom-call(s32[7]{0:T(128)} %pad_add_fusion.1.place, ...), custom_call_target="tpu_custom_call", output_to_operand_aliasing={{0}: (8, {}), {1}: (9, {})} | custom-call | flops 1048576 | bytes 65536 | tf_op jit(solution)/shard_map/pallas_call | solution.py:211
  353.3 5.3 %collective-permute-done.17 = bf16[1024,256]{1,0:T(8,128)(2,1)S(1)} collective-permute-done((bf16[1024,256]{1,0:T(8,128)(2,1)S(1)}, bf16[1024,256]{1,0:T(8,128)(2,1)S(1)}, u32[]{:S(2)}, u32[]{:S(2)}) %collective-permute-start.17) | collective-permute-done | bytes 524320 | tf_op jit(solution)/shard_map/ppermute | solution.py:58
  376.3 6.7 %collective-permute-done.26 = bf16[512,256]{1,0:T(8,128)(2,1)S(1)} collective-permute-done((bf16[512,256]{1,0:T(8,128)(2,1)S(1)}, bf16[512,256]{1,0:T(8,128)(2,1)S(1)}, u32[]{:S(2)}, u32[]{:S(2)}) %collective-permute-start.26) | collective-permute-done | bytes 262176 | tf_op jit(solution)/shard_map/ppermute | solution.py:58
  384.6 5.4 %collective-permute-done.22 = bf16[256,1536]{1,0:T(8,128)(2,1)S(1)} collective-permute-done((bf16[256,1536]{1,0:T(8,128)(2,1)S(1)}, bf16[256,1536]{1,0:T(8,128)(2,1)S(1)}, u32[]{:S(2)}, u32[]{:S(2)}) %collective-permute-start.22) | collective-permute-done | bytes 786464 | tf_op jit(solution)/shard_map/ppermute | solution.py:105
  393.4 4.0 shard_map.152
  404.6 5.0 %collective-permute-done.25 = bf16[256,768]{1,0:T(8,128)(2,1)S(1)} collective-permute-done((bf16[256,768]{1,0:T(8,128)(2,1)S(1)}, bf16[256,768]{1,0:T(8,128)(2,1)S(1)}, u32[]{:S(2)}, u32[]{:S(2)}) %collective-permute-start.25) | collective-permute-done | bytes 393248 | tf_op jit(solution)/shard_map/ppermute | solution.py:105
  411.7 16.8 %collective-permute-done.30 = bf16[256,1536]{1,0:T(8,128)(2,1)S(1)} collective-permute-done((bf16[256,1536]{1,0:T(8,128)(2,1)S(1)}, bf16[256,1536]{1,0:T(8,128)(2,1)S(1)}, u32[]{:S(2)}, u32[]{:S(2)}) %collective-permute-start.30) | collective-permute-done | bytes 786464 | tf_op jit(solution)/shard_map/ppermute | solution.py:105
  432.0 6.3 %collective-permute-done.32 = bf16[256,768]{1,0:T(8,128)(2,1)S(1)} collective-permute-done((bf16[256,768]{1,0:T(8,128)(2,1)S(1)}, bf16[256,768]{1,0:T(8,128)(2,1)S(1)}, u32[]{:S(2)}, u32[]{:S(2)}) %collective-permute-start.32) | collective-permute-done | bytes 393248 | tf_op jit(solution)/shard_map/ppermute | solution.py:105
  (168 shorter events, 111.9 us)
Async XLA Ops:
  7.2 76.4 %all-gather.4.cloned.1.call-start = ((), (), s32[]{:S(2)}) async-start(), calls=%async_computation.1 | async-start | bytes 9437184 | tf_op jit(solution)/shard_map/all_gather | solution.py:243
  7.9 214.2 %all-gather.6.cloned.1.call-start = ((), (), s32[]{:S(2)}) async-start(), calls=%async_computation.3 | async-start | bytes 14155776 | tf_op jit(solution)/shard_map/all_gather | solution.py:260
  8.0 40.6 %collective-permute-start.1 = (bf16[1024,768]{1,0:T(8,128)(2,1)}, bf16[1024,768]{1,0:T(8,128)(2,1)S(1)}, u32[]{:S(2)}, u32[]{:S(2)}) collective-permute-start(bf16[1024,768]{1,0:T(8,128)(2,1)} %param.12), channel_id=1, source_target_pairs={{0,24},{8,16},{16,8},{24,0},{1,25},{9,17},{17,9},{25,1},{2,26},{10... | collective-permute-start | bytes 4718600 | tf_op jit(solution)/shard_map/ppermute | solution.py:58
  13.1 68.5 %collective-permute-start = (bf16[1024,768]{1,0:T(8,128)(2,1)}, bf16[1024,768]{1,0:T(8,128)(2,1)}, u32[]{:S(2)}, u32[]{:S(2)}) collective-permute-start(bf16[1024,768]{1,0:T(8,128)(2,1)} %param.12), channel_id=1, source_target_pairs={{0,8},{8,0},{16,24},{24,16},{1,9},{9,1},{17,25},{25,17},{2,10},{10... | collective-permute-start | bytes 4718600 | tf_op jit(solution)/shard_map/ppermute | solution.py:58
  81.6 55.2 %collective-permute-start.5 = (bf16[1024,768]{1,0:T(8,128)(2,1)}, bf16[1024,768]{1,0:T(8,128)(2,1)}, u32[]{:S(2)}, u32[]{:S(2)}) collective-permute-start(bf16[1024,768]{1,0:T(8,128)(2,1)} %broadcast_select_fusion.3), channel_id=1, source_target_pairs={{0,16},{8,0},{16,24},{24,8},{1,17},{9,1},{17,25},{25,9},{2,18},{10... | collective-permute-start | bytes 4718600 | tf_op jit(solution)/shard_map/ppermute | solution.py:58
  93.8 41.2 %collective-permute-start.2 = (bf16[1536,256]{1,0:T(8,128)(2,1)S(1)}, bf16[1536,256]{1,0:T(8,128)(2,1)S(1)}, u32[]{:S(2)}, u32[]{:S(2)}) collective-permute-start(bf16[1536,256]{1,0:T(8,128)(2,1)S(1)} %copy-done.13), channel_id=1, source_target_pairs={{0,8},{8,0},{16,24},{24,16},{1,9},{9,1},{17,25},{25,17},{2,10},{10... | collective-permute-start | bytes 2359304 | tf_op jit(solution)/shard_map/ppermute | solution.py:58
  142.6 192.2 %reduce-scatter.2.cloned.1.call-start = ((), (), s32[]{:S(2)}) async-start(), calls=%async_computation.2 | async-start | bytes 9437184 | tf_op jit(solution)/shard_map/reduce_scatter | solution.py:270
  142.7 18.7 %collective-permute-start.4 = (bf16[1536,256]{1,0:T(8,128)(2,1)S(1)}, bf16[1536,256]{1,0:T(8,128)(2,1)S(1)}, u32[]{:S(2)}, u32[]{:S(2)}) collective-permute-start(bf16[1536,256]{1,0:T(8,128)(2,1)S(1)} %copy-done.12), channel_id=1, source_target_pairs={{0,8},{8,0},{16,24},{24,16},{1,9},{9,1},{17,25},{25,17},{2,10},{10... | collective-permute-start | bytes 2359304 | tf_op jit(solution)/shard_map/ppermute | solution.py:58
  143.8 38.5 %collective-permute-start.3 = (bf16[3072,256]{1,0:T(8,128)(2,1)S(1)}, bf16[3072,256]{1,0:T(8,128)(2,1)}, u32[]{:S(2)}, u32[]{:S(2)}) collective-permute-start(bf16[3072,256]{1,0:T(8,128)(2,1)S(1)} %maximum_select_fusion.3.near), channel_id=1, source_target_pairs={{8,16},{16,8},{9,17},{17,9},{10,18},{18,10},{11,19},{19,11},{12,20... | collective-permute-start | bytes 4718600 | tf_op jit(solution)/shard_map/ppermute | solution.py:58
  182.3 36.1 %collective-permute-start.7 = (bf16[3072,256]{1,0:T(8,128)(2,1)}, bf16[3072,256]{1,0:T(8,128)(2,1)}, u32[]{:S(2)}, u32[]{:S(2)}) collective-permute-start(bf16[3072,256]{1,0:T(8,128)(2,1)} %collective-permute-done.3.middle), channel_id=1, source_target_pairs={{8,0},{16,24},{9,1},{17,25},{10,2},{18,26},{11,3},{19,27},{12,4},{... | collective-permute-start | bytes 4718600 | tf_op jit(solution)/shard_map/ppermute | solution.py:58
  183.7 34.6 %collective-permute-start.8 = (bf16[3072,256]{1,0:T(8,128)(2,1)}, bf16[3072,256]{1,0:T(8,128)(2,1)}, u32[]{:S(2)}, u32[]{:S(2)}) collective-permute-start(bf16[3072,256]{1,0:T(8,128)(2,1)} %maximum_select_fusion.4.near), channel_id=1, source_target_pairs={{8,16},{16,8},{9,17},{17,9},{10,18},{18,10},{11,19},{19,11},{12,20... | collective-permute-start | bytes 4718600 | tf_op jit(solution)/shard_map/ppermute | solution.py:58
  218.4 37.2 %collective-permute-start.9 = (bf16[3072,256]{1,0:T(8,128)(2,1)}, bf16[3072,256]{1,0:T(8,128)(2,1)}, u32[]{:S(2)}, u32[]{:S(2)}) collective-permute-start(bf16[3072,256]{1,0:T(8,128)(2,1)} %collective-permute-done.8.middle), channel_id=1, source_target_pairs={{8,0},{16,24},{9,1},{17,25},{10,2},{18,26},{11,3},{19,27},{12,4},{... | collective-permute-start | bytes 4718600 | tf_op jit(solution)/shard_map/ppermute | solution.py:58
  219.7 35.9 %collective-permute-start.11 = (bf16[3072,256]{1,0:T(8,128)(2,1)S(1)}, bf16[3072,256]{1,0:T(8,128)(2,1)}, u32[]{:S(2)}, u32[]{:S(2)}) collective-permute-start(bf16[3072,256]{1,0:T(8,128)(2,1)S(1)} %copy-done.3), channel_id=1, source_target_pairs={{8,16},{16,8},{9,17},{17,9},{10,18},{18,10},{11,19},{19,11},{12,20... | collective-permute-start | bytes 4718600 | tf_op jit(solution)/shard_map/ppermute | solution.py:58
  241.5 40.8 %collective-permute-start.13 = (bf16[2048,256]{1,0:T(8,128)(2,1)}, bf16[2048,256]{1,0:T(8,128)(2,1)}, u32[]{:S(2)}, u32[]{:S(2)}) collective-permute-start(bf16[2048,256]{1,0:T(8,128)(2,1)} %get-tuple-element.83), channel_id=1, source_target_pairs={{0,8},{24,16},{1,9},{25,17},{2,10},{26,18},{3,11},{27,19},{4,12},{... | collective-permute-start | bytes 3145736 | tf_op jit(solution)/shard_map/ppermute | solution.py:58
  255.6 44.3 %collective-permute-start.12 = (bf16[3072,256]{1,0:T(8,128)(2,1)}, bf16[3072,256]{1,0:T(8,128)(2,1)S(1)}, u32[]{:S(2)}, u32[]{:S(2)}) collective-permute-start(bf16[3072,256]{1,0:T(8,128)(2,1)} %collective-permute-done.11.middle), channel_id=1, source_target_pairs={{8,0},{16,24},{9,1},{17,25},{10,2},{18,26},{11,3},{19,27},{12,4},{... | collective-permute-start | bytes 4718600 | tf_op jit(solution)/shard_map/ppermute | solution.py:58
  274.9 24.9 %collective-permute-start.10 = (bf16[2048,256]{1,0:T(8,128)(2,1)}, bf16[2048,256]{1,0:T(8,128)(2,1)}, u32[]{:S(2)}, u32[]{:S(2)}) collective-permute-start(bf16[2048,256]{1,0:T(8,128)(2,1)} %get-tuple-element.87), channel_id=1, source_target_pairs={{0,8},{24,16},{1,9},{25,17},{2,10},{26,18},{3,11},{27,19},{4,12},{... | collective-permute-start | bytes 3145736 | tf_op jit(solution)/shard_map/ppermute | solution.py:58
  304.5 30.0 %collective-permute-start.15 = (bf16[1024,256]{1,0:T(8,128)(2,1)S(1)}, bf16[1024,256]{1,0:T(8,128)(2,1)S(1)}, u32[]{:S(2)}, u32[]{:S(2)}) collective-permute-start(bf16[1024,256]{1,0:T(8,128)(2,1)S(1)} %select_convert_fusion.1), channel_id=1, source_target_pairs={{0,8},{8,0},{16,24},{24,16},{1,9},{9,1},{17,25},{25,17},{2,10},{10... | collective-permute-start | bytes 1572872 | tf_op jit(solution)/shard_map/ppermute | solution.py:58
  308.7 34.5 %collective-permute-start.16 = (bf16[2048,256]{1,0:T(8,128)(2,1)}, bf16[2048,256]{1,0:T(8,128)(2,1)}, u32[]{:S(2)}, u32[]{:S(2)}) collective-permute-start(bf16[2048,256]{1,0:T(8,128)(2,1)} %add_convert_fusion.3), channel_id=1, source_target_pairs={{8,16},{16,8},{9,17},{17,9},{10,18},{18,10},{11,19},{19,11},{12,20... | collective-permute-start | bytes 3145736 | tf_op jit(solution)/shard_map/ppermute | solution.py:58
  333.3 19.8 %collective-permute-start.19 = (bf16[512,256]{1,0:T(8,128)(2,1)}, bf16[512,256]{1,0:T(8,128)(2,1)S(1)}, u32[]{:S(2)}, u32[]{:S(2)}) collective-permute-start(bf16[512,256]{1,0:T(8,128)(2,1)} %get-tuple-element.147), channel_id=1, source_target_pairs={{0,8},{8,0},{16,24},{24,16},{1,9},{9,1},{17,25},{25,17},{2,10},{10... | collective-permute-start | bytes 786440 | tf_op jit(solution)/shard_map/ppermute | solution.py:58
  370.1 20.0 %collective-permute-start.22 = (bf16[256,1536]{1,0:T(8,128)(2,1)S(1)}, bf16[256,1536]{1,0:T(8,128)(2,1)S(1)}, u32[]{:S(2)}, u32[]{:S(2)}) collective-permute-start(bf16[256,1536]{1,0:T(8,128)(2,1)S(1)} %pad_maximum_fusion.1), channel_id=1, source_target_pairs={{0,2},{1,3},{2,0},{3,1},{4,6},{5,7},{6,4},{7,5},{8,10},{9,11},{10,... | collective-permute-start | bytes 2359304 | tf_op jit(solution)/shard_map/ppermute | solution.py:105
  372.2 19.5 %collective-permute-start.23 = (bf16[256,1536]{1,0:T(8,128)(2,1)S(1)}, bf16[256,1536]{1,0:T(8,128)(2,1)S(1)}, u32[]{:S(2)}, u32[]{:S(2)}) collective-permute-start(bf16[256,1536]{1,0:T(8,128)(2,1)S(1)} %concatenate.80), channel_id=1, source_target_pairs={{0,4},{1,5},{2,6},{3,7},{4,0},{5,1},{6,2},{7,3},{8,12},{9,13},{10,... | collective-permute-start | bytes 2359304 | tf_op jit(solution)/shard_map/ppermute | solution.py:105
  374.1 19.1 %collective-permute-start.27 = (bf16[512,256]{1,0:T(8,128)(2,1)S(1)}, bf16[512,256]{1,0:T(8,128)(2,1)S(1)}, u32[]{:S(2)}, u32[]{:S(2)}) collective-permute-start(bf16[512,256]{1,0:T(8,128)(2,1)S(1)} %get-tuple-element.123), channel_id=1, source_target_pairs={{0,8},{8,0},{16,24},{24,16},{1,9},{9,1},{17,25},{25,17},{2,10},{10... | collective-permute-start | bytes 786440 | tf_op jit(solution)/shard_map/ppermute | solution.py:58
  409.6 18.8 %collective-permute-start.30 = (bf16[256,1536]{1,0:T(8,128)(2,1)S(1)}, bf16[256,1536]{1,0:T(8,128)(2,1)S(1)}, u32[]{:S(2)}, u32[]{:S(2)}) collective-permute-start(bf16[256,1536]{1,0:T(8,128)(2,1)S(1)} %pad_maximum_fusion.2), channel_id=1, source_target_pairs={{0,2},{1,3},{2,0},{3,1},{4,6},{5,7},{6,4},{7,5},{8,10},{9,11},{10,... | collective-permute-start | bytes 2359304 | tf_op jit(solution)/shard_map/ppermute | solution.py:105
  410.1 18.7 %collective-permute-start.31 = (bf16[256,1536]{1,0:T(8,128)(2,1)S(1)}, bf16[256,1536]{1,0:T(8,128)(2,1)S(1)}, u32[]{:S(2)}, u32[]{:S(2)}) collective-permute-start(bf16[256,1536]{1,0:T(8,128)(2,1)S(1)} %concatenate.81), channel_id=1, source_target_pairs={{0,4},{1,5},{2,6},{3,7},{4,0},{5,1},{6,2},{7,3},{8,12},{9,13},{10,... | collective-permute-start | bytes 2359304 | tf_op jit(solution)/shard_map/ppermute | solution.py:105
  (40 other events, 477.7 us)
Sparse Core Ops, SparseCore 0:
  9.9 57.0 all-gather.3
  142.7 71.3 all-gather.5
  218.5 73.8 reduce-scatter.1

commit v10 on v9

--- a/solution.py
+++ b/solution.py
@@ -300,7 +300,8 @@
     turned0 = (mine0 + other0.astype(F32)).astype(BF16)
     through1 = send(through1, MIDDLE)
     mine1, other1 = halves(line.even, stay1.astype(F32) + through1.astype(F32))
-    turned1 = (mine1 + send(other1.astype(BF16), PAIRS).astype(F32)).astype(BF16)
+    other1 = other1.astype(BF16)
+    turned1 = (mine1 + send(other1, PAIRS).astype(F32)).astype(BF16)
     first_next, second_next = moments2
 
     half = height // 2
@@ -318,7 +319,7 @@
     to_relay, to_pair = together(high[:2], relay_low)
     relay_high = send(to_relay, RELAY_BACK)
     pair_high = send(to_pair, PAIRS)
-    out0, out1, out2, product = together([out0, out1, out2, product], turned0)
+    out0, out1, out2, product = together([out0, out1, out2, product], turned0, to_mirror, other1)
     right = [line.whole(near0, middle0, out0), line.whole(near1, middle1, out1), line.whole(near2, middle2, out2)]
     left_next = 0.95 * left_stat + 0.05 * product.astype(F32)
     relay_high = after(relay_high, to_mirror)

time: 456 us -> 462 us (1.013)
  transfers between devices with their start and end apart: 37 -> 37, of which waited for: 21 -> 20; matrix products, arithmetic and copies ran while one was open for 13% -> 13% of each run, Pallas kernels for 14% -> 14%
where the time goes in v10:
time: 462 us; the launch traced here: 453 us
  waiting for transfers between devices  231 us (50%)
  Pallas kernels  71.5 us (15%)
  starting transfers between devices  62 us (13%)
  other arithmetic  35.6 us (8%)
  matrix products  24.6 us (5%)
  between operations  14.7 us (3%)
  local copies, waits for them, and re-layouts  14.3 us (3%)
    ppermute x24, waiting for transfers between devices, send(): return lax.ppermute(x, self.axis, pairs)  192 us
    pallas_call x3, Pallas kernels, part(): pl.pallas_call(functools.partial(part_kernel, results=results), grid_spec...  55.4 us
    ppermute x24, starting transfers between devices, send(): return lax.ppermute(x, self.axis, pairs)  52.1 us
    ppermute x10, waiting for transfers between devices, swap(): return lax.ppermute(x, axis, [(j, j ^ bit) for j in range(8)])  37.5 us
    pallas_call x4, Pallas kernels, products(): pl.pallas_call(products_kernel, grid_spec=pltpu.PrefetchScalarGridSpec(nu...  16.1 us
    dot_general x4, matrix products, contract_first(): lax.dot_general(first, second, (((0,), (0,)), ((), ())), preferred_elemen...  15.6 us
    convert_element_type x8, other arithmetic, add(): return (first.astype(F32) + second.astype(F32)).astype(first.dtype)  10.5 us
    ppermute x10, starting transfers between devices, swap(): return lax.ppermute(x, axis, [(j, j ^ bit) for j in range(8)])  9.78 us
  transfers between devices with their start and end apart: 37, of which 20 were waited for; matrix products, arithmetic and copies ran while one was open for 13% of the time, Pallas kernels for 14%

profile of v10, /device:TPU:0, one launch (start us, length us, event | category | flops | bytes accessed | tf_op | source)
XLA Modules:
  0.0 453.4 jit_solution(2926803106069976149)
XLA Ops:
  8.0 5.1 %collective-permute-start.1 = (bf16[1024,768]{1,0:T(8,128)(2,1)}, bf16[1024,768]{1,0:T(8,128)(2,1)S(1)}, u32[]{:S(2)}, u32[]{:S(2)}) collective-permute-start(bf16[1024,768]{1,0:T(8,128)(2,1)} %param.12), channel_id=1, source_target_pairs={{0,24},{8,16},{16,8},{24,0},{1,25},{9,17},{17,9},{25,1},{2,26},{10... | collective-permute-start | bytes 4718600 | tf_op jit(solution)/shard_map/ppermute | solution.py:58
  16.2 32.4 %collective-permute-done.1 = bf16[1024,768]{1,0:T(8,128)(2,1)S(1)} collective-permute-done((bf16[1024,768]{1,0:T(8,128)(2,1)}, bf16[1024,768]{1,0:T(8,128)(2,1)S(1)}, u32[]{:S(2)}, u32[]{:S(2)}) %collective-permute-start.1) | collective-permute-done | bytes 1572896 | tf_op jit(solution)/shard_map/ppermute | solution.py:58
  50.0 31.6 %collective-permute-done = bf16[1024,768]{1,0:T(8,128)(2,1)} collective-permute-done((bf16[1024,768]{1,0:T(8,128)(2,1)}, bf16[1024,768]{1,0:T(8,128)(2,1)}, u32[]{:S(2)}, u32[]{:S(2)}) %collective-permute-start) | collective-permute-done | bytes 1572896 | tf_op jit(solution)/shard_map/ppermute | solution.py:58
  83.6 4.1 fusion.4
  93.9 41.1 %collective-permute-done.2 = bf16[1536,256]{1,0:T(8,128)(2,1)S(1)} collective-permute-done((bf16[1536,256]{1,0:T(8,128)(2,1)S(1)}, bf16[1536,256]{1,0:T(8,128)(2,1)S(1)}, u32[]{:S(2)}, u32[]{:S(2)}) %collective-permute-start.2) | collective-permute-done | bytes 786464 | tf_op jit(solution)/shard_map/ppermute | solution.py:58
  136.8 5.7 %add_convert_fusion.2 = bf16[1024,768]{1,0:T(8,128)(2,1)} fusion(f32[1024,768]{1,0:T(8,128)S(1)} %copy-done.29, bf16[1024,768]{1,0:T(8,128)(2,1)} %collective-permute-done.5, bf16[4096,1024]{1,0:T(8,128)(2,1)} %all-gather.4.cloned.1.call-done.basis, s32[]{:T(128)S(6)} %select_n.138), kind=kOutput, calls=%fused_computation.6 | convolution fusion | flops 1612185600 | bytes 8388612 | tf_op jit(solution)/shard_map/dot_general | solution.py:29
  145.5 15.8 %collective-permute-done.4 = bf16[1536,256]{1,0:T(8,128)(2,1)S(1)} collective-permute-done((bf16[1536,256]{1,0:T(8,128)(2,1)S(1)}, bf16[1536,256]{1,0:T(8,128)(2,1)S(1)}, u32[]{:S(2)}, u32[]{:S(2)}) %collective-permute-start.4) | collective-permute-done | bytes 786464 | tf_op jit(solution)/shard_map/ppermute | solution.py:58
  163.1 17.5 %collective-permute-done.6 = bf16[1536,256]{1,0:T(8,128)(2,1)S(1)} collective-permute-done((bf16[1536,256]{1,0:T(8,128)(2,1)S(1)}, bf16[1536,256]{1,0:T(8,128)(2,1)S(1)}, u32[]{:S(2)}, u32[]{:S(2)}) %collective-permute-start.6) | collective-permute-done | bytes 786464 | tf_op jit(solution)/shard_map/ppermute | solution.py:58
  189.7 9.1 %convolution_convert_fusion = bf16[4096,1024]{1,0:T(8,128)(2,1)} fusion(bf16[4096,768]{1,0:T(8,128)(2,1)S(1)} %constant_dynamic-update-slice_fusion, bf16[1024,768]{1,0:T(8,128)(2,1)S(1)} %copy-done.10), kind=kOutput, calls=%fused_computation | convolution fusion | flops 6446645248 | bytes 16252928 | tf_op jit(solution)/shard_map/dot_general | solution.py:25
  198.7 19.6 %collective-permute-done.7.out = bf16[3072,256]{1,0:T(8,128)(2,1)} collective-permute-done((bf16[3072,256]{1,0:T(8,128)(2,1)}, bf16[3072,256]{1,0:T(8,128)(2,1)}, u32[]{:S(2)}, u32[]{:S(2)}) %collective-permute-start.7) | collective-permute-done | bytes 1572896 | tf_op jit(solution)/shard_map/ppermute | solution.py:58
  222.1 19.4 %shard_map.147 = (f32[1024,768]{1,0:T(8,128)}, f32[1024,768]{1,0:T(8,128)}, bf16[2048,256]{1,0:T(8,128)(2,1)}, bf16[2048,256]{1,0:T(8,128)(2,1)}) custom-call(s32[5]{0:T(128)} %pad_add_fusion.place, bf16[8,1024,768]{2,1,0:T(8,128)(2,1)} %bitcast.8, bf16[3072,256]{1,0:T(8,128)(2,1)} %copy-done.1, bf16[3072,256]{1,0:T(8,128)(2,1)} %collective-permute-done.3.middle, ...), custom_call_target="tpu_custom_call" | custom-call | flops 1048576 | bytes 65536 | tf_op jit(solution)/shard_map/pallas_call | solution.py:211
  241.5 10.0 %collective-permute-start.13 = (bf16[2048,256]{1,0:T(8,128)(2,1)}, bf16[2048,256]{1,0:T(8,128)(2,1)}, u32[]{:S(2)}, u32[]{:S(2)}) collective-permute-start(bf16[2048,256]{1,0:T(8,128)(2,1)} %get-tuple-element.83), channel_id=1, source_target_pairs={{0,8},{24,16},{1,9},{25,17},{2,10},{26,18},{3,11},{27,19},{4,12},{... | collective-permute-start | bytes 3145736 | tf_op jit(solution)/shard_map/ppermute | solution.py:58
  251.5 4.1 collective-permute-done.9.out
  257.1 17.8 %shard_map.148 = (f32[1024,768]{1,0:T(8,128)}, f32[1024,768]{1,0:T(8,128)}, bf16[2048,256]{1,0:T(8,128)(2,1)}, bf16[2048,256]{1,0:T(8,128)(2,1)}) custom-call(s32[5]{0:T(128)} %pad_add_fusion.place, bf16[8,1024,768]{2,1,0:T(8,128)(2,1)} %bitcast.9, bf16[3072,256]{1,0:T(8,128)(2,1)} %maximum_select_fusion.4.near, ...), custom_call_target="tpu_custom_call", output_to_operand_aliasing={{0}: (8, {}), {1}: (9, {})} | custom-call | flops 1048576 | bytes 65536 | tf_op jit(solution)/shard_map/pallas_call | solution.py:211
  274.9 7.4 %collective-permute-start.10 = (bf16[2048,256]{1,0:T(8,128)(2,1)}, bf16[2048,256]{1,0:T(8,128)(2,1)}, u32[]{:S(2)}, u32[]{:S(2)}) collective-permute-start(bf16[2048,256]{1,0:T(8,128)(2,1)} %get-tuple-element.87), channel_id=1, source_target_pairs={{0,8},{24,16},{1,9},{25,17},{2,10},{26,18},{3,11},{27,19},{4,12},{... | collective-permute-start | bytes 3145736 | tf_op jit(solution)/shard_map/ppermute | solution.py:58
  287.3 12.5 %collective-permute-done.10 = bf16[2048,256]{1,0:T(8,128)(2,1)} collective-permute-done((bf16[2048,256]{1,0:T(8,128)(2,1)}, bf16[2048,256]{1,0:T(8,128)(2,1)}, u32[]{:S(2)}, u32[]{:S(2)}) %collective-permute-start.10) | collective-permute-done | bytes 1048608 | tf_op jit(solution)/shard_map/ppermute | solution.py:58
  309.6 18.2 %shard_map.149 = (f32[1024,768]{1,0:T(8,128)}, f32[1024,768]{1,0:T(8,128)}, bf16[1024,256]{1,0:T(8,128)(2,1)}, bf16[1024,256]{1,0:T(8,128)(2,1)}, bf16[1024,256]{1,0:T(8,128)(2,1)}, /*index=5*/bf16[1024,256]{1,0:T(8,128)(2,1)}) custom-call(s32[7]{0:T(128)} %pad_add_fusion.1.place, ...), custom_call_target="tpu_custom_call", output_to_operand_aliasing={{0}: (8, {}), {1}: (9, {})} | custom-call | flops 1048576 | bytes 65536 | tf_op jit(solution)/shard_map/pallas_call | solution.py:211
  334.5 7.8 %collective-permute-done.16 = bf16[512,256]{1,0:T(8,128)(2,1)S(1)} collective-permute-done((bf16[512,256]{1,0:T(8,128)(2,1)S(1)}, bf16[512,256]{1,0:T(8,128)(2,1)S(1)}, u32[]{:S(2)}, u32[]{:S(2)}) %collective-permute-start.16) | collective-permute-done | bytes 262176 | tf_op jit(solution)/shard_map/ppermute | solution.py:58
  362.9 4.0 shard_map.150
  380.1 6.7 %collective-permute-done.26 = bf16[512,256]{1,0:T(8,128)(2,1)S(1)} collective-permute-done((bf16[512,256]{1,0:T(8,128)(2,1)S(1)}, bf16[512,256]{1,0:T(8,128)(2,1)S(1)}, u32[]{:S(2)}, u32[]{:S(2)}) %collective-permute-start.26) | collective-permute-done | bytes 262176 | tf_op jit(solution)/shard_map/ppermute | solution.py:58
  388.9 5.1 %collective-permute-done.22 = bf16[256,1536]{1,0:T(8,128)(2,1)S(1)} collective-permute-done((bf16[256,1536]{1,0:T(8,128)(2,1)S(1)}, bf16[256,1536]{1,0:T(8,128)(2,1)S(1)}, u32[]{:S(2)}, u32[]{:S(2)}) %collective-permute-start.22) | collective-permute-done | bytes 786464 | tf_op jit(solution)/shard_map/ppermute | solution.py:105
  410.4 4.7 %collective-permute-done.25 = bf16[256,768]{1,0:T(8,128)(2,1)S(1)} collective-permute-done((bf16[256,768]{1,0:T(8,128)(2,1)S(1)}, bf16[256,768]{1,0:T(8,128)(2,1)S(1)}, u32[]{:S(2)}, u32[]{:S(2)}) %collective-permute-start.25) | collective-permute-done | bytes 393248 | tf_op jit(solution)/shard_map/ppermute | solution.py:105
  417.1 16.9 %collective-permute-done.30 = bf16[256,1536]{1,0:T(8,128)(2,1)S(1)} collective-permute-done((bf16[256,1536]{1,0:T(8,128)(2,1)S(1)}, bf16[256,1536]{1,0:T(8,128)(2,1)S(1)}, u32[]{:S(2)}, u32[]{:S(2)}) %collective-permute-start.30) | collective-permute-done | bytes 786464 | tf_op jit(solution)/shard_map/ppermute | solution.py:105
  437.8 6.0 %collective-permute-done.32 = bf16[256,768]{1,0:T(8,128)(2,1)S(1)} collective-permute-done((bf16[256,768]{1,0:T(8,128)(2,1)S(1)}, bf16[256,768]{1,0:T(8,128)(2,1)S(1)}, u32[]{:S(2)}, u32[]{:S(2)}) %collective-permute-start.32) | collective-permute-done | bytes 393248 | tf_op jit(solution)/shard_map/ppermute | solution.py:105
  (174 shorter events, 116.2 us)
Async XLA Ops:
  7.2 76.4 %all-gather.4.cloned.1.call-start = ((), (), s32[]{:S(2)}) async-start(), calls=%async_computation.1 | async-start | bytes 9437184 | tf_op jit(solution)/shard_map/all_gather | solution.py:243
  7.9 214.2 %all-gather.6.cloned.1.call-start = ((), (), s32[]{:S(2)}) async-start(), calls=%async_computation.3 | async-start | bytes 14155776 | tf_op jit(solution)/shard_map/all_gather | solution.py:260
  8.0 40.6 %collective-permute-start.1 = (bf16[1024,768]{1,0:T(8,128)(2,1)}, bf16[1024,768]{1,0:T(8,128)(2,1)S(1)}, u32[]{:S(2)}, u32[]{:S(2)}) collective-permute-start(bf16[1024,768]{1,0:T(8,128)(2,1)} %param.12), channel_id=1, source_target_pairs={{0,24},{8,16},{16,8},{24,0},{1,25},{9,17},{17,9},{25,1},{2,26},{10... | collective-permute-start | bytes 4718600 | tf_op jit(solution)/shard_map/ppermute | solution.py:58
  13.1 68.5 %collective-permute-start = (bf16[1024,768]{1,0:T(8,128)(2,1)}, bf16[1024,768]{1,0:T(8,128)(2,1)}, u32[]{:S(2)}, u32[]{:S(2)}) collective-permute-start(bf16[1024,768]{1,0:T(8,128)(2,1)} %param.12), channel_id=1, source_target_pairs={{0,8},{8,0},{16,24},{24,16},{1,9},{9,1},{17,25},{25,17},{2,10},{10... | collective-permute-start | bytes 4718600 | tf_op jit(solution)/shard_map/ppermute | solution.py:58
  81.6 55.2 %collective-permute-start.5 = (bf16[1024,768]{1,0:T(8,128)(2,1)}, bf16[1024,768]{1,0:T(8,128)(2,1)}, u32[]{:S(2)}, u32[]{:S(2)}) collective-permute-start(bf16[1024,768]{1,0:T(8,128)(2,1)} %broadcast_select_fusion.3), channel_id=1, source_target_pairs={{0,16},{8,0},{16,24},{24,8},{1,17},{9,1},{17,25},{25,9},{2,18},{10... | collective-permute-start | bytes 4718600 | tf_op jit(solution)/shard_map/ppermute | solution.py:58
  93.8 41.2 %collective-permute-start.2 = (bf16[1536,256]{1,0:T(8,128)(2,1)S(1)}, bf16[1536,256]{1,0:T(8,128)(2,1)S(1)}, u32[]{:S(2)}, u32[]{:S(2)}) collective-permute-start(bf16[1536,256]{1,0:T(8,128)(2,1)S(1)} %copy-done.15), channel_id=1, source_target_pairs={{0,8},{8,0},{16,24},{24,16},{1,9},{9,1},{17,25},{25,17},{2,10},{10... | collective-permute-start | bytes 2359304 | tf_op jit(solution)/shard_map/ppermute | solution.py:58
  142.6 206.8 %reduce-scatter.2.cloned.1.call-start = ((), (), s32[]{:S(2)}) async-start(), calls=%async_computation.2 | async-start | bytes 9437184 | tf_op jit(solution)/shard_map/reduce_scatter | solution.py:270
  142.6 18.7 %collective-permute-start.4 = (bf16[1536,256]{1,0:T(8,128)(2,1)S(1)}, bf16[1536,256]{1,0:T(8,128)(2,1)S(1)}, u32[]{:S(2)}, u32[]{:S(2)}) collective-permute-start(bf16[1536,256]{1,0:T(8,128)(2,1)S(1)} %copy-done.14), channel_id=1, source_target_pairs={{0,8},{8,0},{16,24},{24,16},{1,9},{9,1},{17,25},{25,17},{2,10},{10... | collective-permute-start | bytes 2359304 | tf_op jit(solution)/shard_map/ppermute | solution.py:58
  143.7 38.5 %collective-permute-start.3 = (bf16[3072,256]{1,0:T(8,128)(2,1)S(1)}, bf16[3072,256]{1,0:T(8,128)(2,1)}, u32[]{:S(2)}, u32[]{:S(2)}) collective-permute-start(bf16[3072,256]{1,0:T(8,128)(2,1)S(1)} %maximum_select_fusion.3.near), channel_id=1, source_target_pairs={{8,16},{16,8},{9,17},{17,9},{10,18},{18,10},{11,19},{19,11},{12,20... | collective-permute-start | bytes 4718600 | tf_op jit(solution)/shard_map/ppermute | solution.py:58
  182.2 36.1 %collective-permute-start.7 = (bf16[3072,256]{1,0:T(8,128)(2,1)}, bf16[3072,256]{1,0:T(8,128)(2,1)}, u32[]{:S(2)}, u32[]{:S(2)}) collective-permute-start(bf16[3072,256]{1,0:T(8,128)(2,1)} %collective-permute-done.3.middle), channel_id=1, source_target_pairs={{8,0},{16,24},{9,1},{17,25},{10,2},{18,26},{11,3},{19,27},{12,4},{... | collective-permute-start | bytes 4718600 | tf_op jit(solution)/shard_map/ppermute | solution.py:58
  183.7 34.6 %collective-permute-start.8 = (bf16[3072,256]{1,0:T(8,128)(2,1)}, bf16[3072,256]{1,0:T(8,128)(2,1)}, u32[]{:S(2)}, u32[]{:S(2)}) collective-permute-start(bf16[3072,256]{1,0:T(8,128)(2,1)} %maximum_select_fusion.4.near), channel_id=1, source_target_pairs={{8,16},{16,8},{9,17},{17,9},{10,18},{18,10},{11,19},{19,11},{12,20... | collective-permute-start | bytes 4718600 | tf_op jit(solution)/shard_map/ppermute | solution.py:58
  218.3 37.2 %collective-permute-start.9 = (bf16[3072,256]{1,0:T(8,128)(2,1)}, bf16[3072,256]{1,0:T(8,128)(2,1)}, u32[]{:S(2)}, u32[]{:S(2)}) collective-permute-start(bf16[3072,256]{1,0:T(8,128)(2,1)} %collective-permute-done.8.middle), channel_id=1, source_target_pairs={{8,0},{16,24},{9,1},{17,25},{10,2},{18,26},{11,3},{19,27},{12,4},{... | collective-permute-start | bytes 4718600 | tf_op jit(solution)/shard_map/ppermute | solution.py:58
  219.6 35.9 %collective-permute-start.11 = (bf16[3072,256]{1,0:T(8,128)(2,1)S(1)}, bf16[3072,256]{1,0:T(8,128)(2,1)}, u32[]{:S(2)}, u32[]{:S(2)}) collective-permute-start(bf16[3072,256]{1,0:T(8,128)(2,1)S(1)} %copy-done.3), channel_id=1, source_target_pairs={{8,16},{16,8},{9,17},{17,9},{10,18},{18,10},{11,19},{19,11},{12,20... | collective-permute-start | bytes 4718600 | tf_op jit(solution)/shard_map/ppermute | solution.py:58
  241.5 40.8 %collective-permute-start.13 = (bf16[2048,256]{1,0:T(8,128)(2,1)}, bf16[2048,256]{1,0:T(8,128)(2,1)}, u32[]{:S(2)}, u32[]{:S(2)}) collective-permute-start(bf16[2048,256]{1,0:T(8,128)(2,1)} %get-tuple-element.83), channel_id=1, source_target_pairs={{0,8},{24,16},{1,9},{25,17},{2,10},{26,18},{3,11},{27,19},{4,12},{... | collective-permute-start | bytes 3145736 | tf_op jit(solution)/shard_map/ppermute | solution.py:58
  255.5 44.2 %collective-permute-start.12 = (bf16[3072,256]{1,0:T(8,128)(2,1)}, bf16[3072,256]{1,0:T(8,128)(2,1)S(1)}, u32[]{:S(2)}, u32[]{:S(2)}) collective-permute-start(bf16[3072,256]{1,0:T(8,128)(2,1)} %collective-permute-done.11.middle), channel_id=1, source_target_pairs={{8,0},{16,24},{9,1},{17,25},{10,2},{18,26},{11,3},{19,27},{12,4},{... | collective-permute-start | bytes 4718600 | tf_op jit(solution)/shard_map/ppermute | solution.py:58
  274.9 24.9 %collective-permute-start.10 = (bf16[2048,256]{1,0:T(8,128)(2,1)}, bf16[2048,256]{1,0:T(8,128)(2,1)}, u32[]{:S(2)}, u32[]{:S(2)}) collective-permute-start(bf16[2048,256]{1,0:T(8,128)(2,1)} %get-tuple-element.87), channel_id=1, source_target_pairs={{0,8},{24,16},{1,9},{25,17},{2,10},{26,18},{3,11},{27,19},{4,12},{... | collective-permute-start | bytes 3145736 | tf_op jit(solution)/shard_map/ppermute | solution.py:58
  285.1 19.4 %collective-permute-start.14 = (bf16[2048,256]{1,0:T(8,128)(2,1)}, bf16[2048,256]{1,0:T(8,128)(2,1)}, u32[]{:S(2)}, u32[]{:S(2)}) collective-permute-start(bf16[2048,256]{1,0:T(8,128)(2,1)} %add_convert_fusion.4), channel_id=1, source_target_pairs={{8,16},{16,8},{9,17},{17,9},{10,18},{18,10},{11,19},{19,11},{12,20... | collective-permute-start | bytes 3145736 | tf_op jit(solution)/shard_map/ppermute | solution.py:58
  302.8 39.5 %collective-permute-start.17 = (bf16[2048,256]{1,0:T(8,128)(2,1)}, bf16[2048,256]{1,0:T(8,128)(2,1)}, u32[]{:S(2)}, u32[]{:S(2)}) collective-permute-start(bf16[2048,256]{1,0:T(8,128)(2,1)} %add_convert_fusion.3), channel_id=1, source_target_pairs={{8,16},{16,8},{9,17},{17,9},{10,18},{18,10},{11,19},{19,11},{12,20... | collective-permute-start | bytes 3145736 | tf_op jit(solution)/shard_map/ppermute | solution.py:58
  306.0 36.3 %collective-permute-start.15 = (bf16[1024,256]{1,0:T(8,128)(2,1)S(1)}, bf16[1024,256]{1,0:T(8,128)(2,1)S(1)}, u32[]{:S(2)}, u32[]{:S(2)}) collective-permute-start(bf16[1024,256]{1,0:T(8,128)(2,1)S(1)} %select_convert_fusion.1), channel_id=1, source_target_pairs={{0,8},{8,0},{16,24},{24,16},{1,9},{9,1},{17,25},{25,17},{2,10},{10... | collective-permute-start | bytes 1572872 | tf_op jit(solution)/shard_map/ppermute | solution.py:58
  331.8 28.6 %collective-permute-start.19 = (bf16[512,256]{1,0:T(8,128)(2,1)}, bf16[512,256]{1,0:T(8,128)(2,1)}, u32[]{:S(2)}, u32[]{:S(2)}) collective-permute-start(bf16[512,256]{1,0:T(8,128)(2,1)} %get-tuple-element.147), channel_id=1, source_target_pairs={{0,8},{8,0},{16,24},{24,16},{1,9},{9,1},{17,25},{25,17},{2,10},{10... | collective-permute-start | bytes 786440 | tf_op jit(solution)/shard_map/ppermute | solution.py:58
  374.1 19.8 %collective-permute-start.22 = (bf16[256,1536]{1,0:T(8,128)(2,1)S(1)}, bf16[256,1536]{1,0:T(8,128)(2,1)S(1)}, u32[]{:S(2)}, u32[]{:S(2)}) collective-permute-start(bf16[256,1536]{1,0:T(8,128)(2,1)S(1)} %pad_maximum_fusion.1), channel_id=1, source_target_pairs={{0,2},{1,3},{2,0},{3,1},{4,6},{5,7},{6,4},{7,5},{8,10},{9,11},{10,... | collective-permute-start | bytes 2359304 | tf_op jit(solution)/shard_map/ppermute | solution.py:105
  376.1 19.3 %collective-permute-start.23 = (bf16[256,1536]{1,0:T(8,128)(2,1)S(1)}, bf16[256,1536]{1,0:T(8,128)(2,1)S(1)}, u32[]{:S(2)}, u32[]{:S(2)}) collective-permute-start(bf16[256,1536]{1,0:T(8,128)(2,1)S(1)} %concatenate.80), channel_id=1, source_target_pairs={{0,4},{1,5},{2,6},{3,7},{4,0},{5,1},{6,2},{7,3},{8,12},{9,13},{10,... | collective-permute-start | bytes 2359304 | tf_op jit(solution)/shard_map/ppermute | solution.py:105
  380.0 19.0 %collective-permute-start.27 = (bf16[512,256]{1,0:T(8,128)(2,1)S(1)}, bf16[512,256]{1,0:T(8,128)(2,1)S(1)}, u32[]{:S(2)}, u32[]{:S(2)}) collective-permute-start(bf16[512,256]{1,0:T(8,128)(2,1)S(1)} %copy-done.23), channel_id=1, source_target_pairs={{0,8},{8,0},{16,24},{24,16},{1,9},{9,1},{17,25},{25,17},{2,10},{10... | collective-permute-start | bytes 786440 | tf_op jit(solution)/shard_map/ppermute | solution.py:58
  415.1 18.9 %collective-permute-start.30 = (bf16[256,1536]{1,0:T(8,128)(2,1)S(1)}, bf16[256,1536]{1,0:T(8,128)(2,1)S(1)}, u32[]{:S(2)}, u32[]{:S(2)}) collective-permute-start(bf16[256,1536]{1,0:T(8,128)(2,1)S(1)} %pad_maximum_fusion.2), channel_id=1, source_target_pairs={{0,2},{1,3},{2,0},{3,1},{4,6},{5,7},{6,4},{7,5},{8,10},{9,11},{10,... | collective-permute-start | bytes 2359304 | tf_op jit(solution)/shard_map/ppermute | solution.py:105
  (43 other events, 526.8 us)
Sparse Core Ops, SparseCore 0:
  9.9 57.0 all-gather.3
  142.7 71.3 all-gather.5
  218.4 73.8 reduce-scatter.1

commit v11 on v9

--- a/solution.py
+++ b/solution.py
@@ -9,7 +9,7 @@
 
 BF16 = jnp.bfloat16
 F32 = jnp.float32
-VMEM = 60 * 2**20
+VMEM = 40 * 2**20
 QUICK = pl.CostEstimate(flops=2**20, bytes_accessed=2**16, transcendentals=0)
 
 PAIRS = [(0, 1), (1, 0), (2, 3), (3, 2)]

time: 456 us -> 452 us (level)
  transfers between devices with their start and end apart: 37 -> 37, of which waited for: 21 -> 22; matrix products, arithmetic and copies ran while one was open for 13% -> 12% of each run, Pallas kernels for 14% -> 13%
where the time goes in v11:
time: 452 us; the launch traced here: 443 us
  waiting for transfers between devices  233 us (52%)
  Pallas kernels  67.5 us (15%)
  starting transfers between devices  60.1 us (13%)
  other arithmetic  31.3 us (7%)
  matrix products  24.6 us (5%)
  between operations  14.7 us (3%)
  local copies, waits for them, and re-layouts  11.9 us (3%)
    ppermute x24, waiting for transfers between devices, send(): return lax.ppermute(x, self.axis, pairs)  195 us
    pallas_call x3, Pallas kernels, part(): pl.pallas_call(functools.partial(part_kernel, results=results), grid_spec...  51.3 us
    ppermute x24, starting transfers between devices, send(): return lax.ppermute(x, self.axis, pairs)  50.8 us
    ppermute x10, waiting for transfers between devices, swap(): return lax.ppermute(x, axis, [(j, j ^ bit) for j in range(8)])  37.9 us
    pallas_call x4, Pallas kernels, products(): pl.pallas_call(products_kernel, grid_spec=pltpu.PrefetchScalarGridSpec(nu...  16.1 us
    dot_general x4, matrix products, contract_first(): lax.dot_general(first, second, (((0,), (0,)), ((), ())), preferred_elemen...  15.5 us
    select_n x6, other arithmetic, joined(): jnp.where(keep_order, jnp.concatenate([first, second]), jnp.concatenate([...  11.1 us
    ppermute x10, starting transfers between devices, swap(): return lax.ppermute(x, axis, [(j, j ^ bit) for j in range(8)])  9.2 us
  transfers between devices with their start and end apart: 37, of which 22 were waited for; matrix products, arithmetic and copies ran while one was open for 12% of the time, Pallas kernels for 13%

profile of v11, /device:TPU:0, one launch (start us, length us, event | category | flops | bytes accessed | tf_op | source)
XLA Modules:
  0.0 443.5 jit_solution(7935054910940260506)
XLA Ops:
  8.0 5.1 %collective-permute-start.1 = (bf16[1024,768]{1,0:T(8,128)(2,1)}, bf16[1024,768]{1,0:T(8,128)(2,1)S(1)}, u32[]{:S(2)}, u32[]{:S(2)}) collective-permute-start(bf16[1024,768]{1,0:T(8,128)(2,1)} %param.12), channel_id=1, source_target_pairs={{0,24},{8,16},{16,8},{24,0},{1,25},{9,17},{17,9},{25,1},{2,26},{10... | collective-permute-start | bytes 4718600 | tf_op jit(solution)/shard_map/ppermute | solution.py:58
  16.2 32.4 %collective-permute-done.1 = bf16[1024,768]{1,0:T(8,128)(2,1)S(1)} collective-permute-done((bf16[1024,768]{1,0:T(8,128)(2,1)}, bf16[1024,768]{1,0:T(8,128)(2,1)S(1)}, u32[]{:S(2)}, u32[]{:S(2)}) %collective-permute-start.1) | collective-permute-done | bytes 1572896 | tf_op jit(solution)/shard_map/ppermute | solution.py:58
  50.0 31.6 %collective-permute-done = bf16[1024,768]{1,0:T(8,128)(2,1)} collective-permute-done((bf16[1024,768]{1,0:T(8,128)(2,1)}, bf16[1024,768]{1,0:T(8,128)(2,1)}, u32[]{:S(2)}, u32[]{:S(2)}) %collective-permute-start) | collective-permute-done | bytes 1572896 | tf_op jit(solution)/shard_map/ppermute | solution.py:58
  83.6 4.1 fusion.4
  93.8 41.2 %collective-permute-done.2 = bf16[1536,256]{1,0:T(8,128)(2,1)} collective-permute-done((bf16[1536,256]{1,0:T(8,128)(2,1)}, bf16[1536,256]{1,0:T(8,128)(2,1)}, u32[]{:S(2)}, u32[]{:S(2)}) %collective-permute-start.2) | collective-permute-done | bytes 786464 | tf_op jit(solution)/shard_map/ppermute | solution.py:58
  137.5 5.7 %add_convert_fusion.2 = bf16[1024,768]{1,0:T(8,128)(2,1)} fusion(f32[1024,768]{1,0:T(8,128)S(1)} %copy-done.28, bf16[1024,768]{1,0:T(8,128)(2,1)} %collective-permute-done.5, bf16[4096,1024]{1,0:T(8,128)(2,1)} %all-gather.4.cloned.1.call-done.basis, s32[]{:T(128)S(6)} %select_n.138), kind=kOutput, calls=%fused_computation.6 | convolution fusion | flops 1612185600 | bytes 8388612 | tf_op jit(solution)/shard_map/dot_general | solution.py:29
  146.2 16.0 %collective-permute-done.4 = bf16[1536,256]{1,0:T(8,128)(2,1)S(1)} collective-permute-done((bf16[1536,256]{1,0:T(8,128)(2,1)}, bf16[1536,256]{1,0:T(8,128)(2,1)S(1)}, u32[]{:S(2)}, u32[]{:S(2)}) %collective-permute-start.4) | collective-permute-done | bytes 786464 | tf_op jit(solution)/shard_map/ppermute | solution.py:58
  165.4 17.5 %collective-permute-done.6 = bf16[1536,256]{1,0:T(8,128)(2,1)S(1)} collective-permute-done((bf16[1536,256]{1,0:T(8,128)(2,1)S(1)}, bf16[1536,256]{1,0:T(8,128)(2,1)S(1)}, u32[]{:S(2)}, u32[]{:S(2)}) %collective-permute-start.6) | collective-permute-done | bytes 786464 | tf_op jit(solution)/shard_map/ppermute | solution.py:58
  191.9 9.1 %convolution_convert_fusion = bf16[4096,1024]{1,0:T(8,128)(2,1)} fusion(bf16[4096,768]{1,0:T(8,128)(2,1)S(1)} %constant_dynamic-update-slice_fusion, bf16[1024,768]{1,0:T(8,128)(2,1)S(1)} %copy-done.18), kind=kOutput, calls=%fused_computation | convolution fusion | flops 6446645248 | bytes 16252928 | tf_op jit(solution)/shard_map/dot_general | solution.py:25
  201.0 19.7 %collective-permute-done.7.out = bf16[3072,256]{1,0:T(8,128)(2,1)} collective-permute-done((bf16[3072,256]{1,0:T(8,128)(2,1)}, bf16[3072,256]{1,0:T(8,128)(2,1)}, u32[]{:S(2)}, u32[]{:S(2)}) %collective-permute-start.7) | collective-permute-done | bytes 1572896 | tf_op jit(solution)/shard_map/ppermute | solution.py:58
  227.2 18.4 %shard_map.147 = (f32[1024,768]{1,0:T(8,128)}, f32[1024,768]{1,0:T(8,128)}, bf16[2048,256]{1,0:T(8,128)(2,1)S(1)}, bf16[2048,256]{1,0:T(8,128)(2,1)S(1)}) custom-call(s32[5]{0:T(128)S(1)} %pad_add_fusion.place, bf16[8,1024,768]{2,1,0:T(8,128)(2,1)} %bitcast.8, bf16[3072,256]{1,0:T(8,128)(2,1)S(1)} %copy-done.5, ...), custom_call_target="tpu_custom_call" | custom-call | flops 1048576 | bytes 65536 | tf_op jit(solution)/shard_map/pallas_call | solution.py:211
  245.6 8.5 %collective-permute-start.13 = (bf16[2048,256]{1,0:T(8,128)(2,1)S(1)}, bf16[2048,256]{1,0:T(8,128)(2,1)S(1)}, u32[]{:S(2)}, u32[]{:S(2)}) collective-permute-start(bf16[2048,256]{1,0:T(8,128)(2,1)S(1)} %get-tuple-element.83), channel_id=1, source_target_pairs={{0,8},{24,16},{1,9},{25,17},{2,10},{26,18},{3,11},{27,19},{4,12},{... | collective-permute-start | bytes 3145736 | tf_op jit(solution)/shard_map/ppermute | solution.py:58
  259.5 16.7 %shard_map.148 = (f32[1024,768]{1,0:T(8,128)}, f32[1024,768]{1,0:T(8,128)}, bf16[2048,256]{1,0:T(8,128)(2,1)}, bf16[2048,256]{1,0:T(8,128)(2,1)S(1)}) custom-call(s32[5]{0:T(128)S(1)} %pad_add_fusion.place, bf16[8,1024,768]{2,1,0:T(8,128)(2,1)} %bitcast.9, ...), custom_call_target="tpu_custom_call", output_to_operand_aliasing={{0}: (8, {}), {1}: (9, {})} | custom-call | flops 1048576 | bytes 65536 | tf_op jit(solution)/shard_map/pallas_call | solution.py:211
  276.2 8.7 %collective-permute-start.10 = (bf16[2048,256]{1,0:T(8,128)(2,1)}, bf16[2048,256]{1,0:T(8,128)(2,1)}, u32[]{:S(2)}, u32[]{:S(2)}) collective-permute-start(bf16[2048,256]{1,0:T(8,128)(2,1)} %get-tuple-element.87), channel_id=1, source_target_pairs={{0,8},{24,16},{1,9},{25,17},{2,10},{26,18},{3,11},{27,19},{4,12},{... | collective-permute-start | bytes 3145736 | tf_op jit(solution)/shard_map/ppermute | solution.py:58
  287.8 14.5 %collective-permute-done.10 = bf16[2048,256]{1,0:T(8,128)(2,1)} collective-permute-done((bf16[2048,256]{1,0:T(8,128)(2,1)}, bf16[2048,256]{1,0:T(8,128)(2,1)}, u32[]{:S(2)}, u32[]{:S(2)}) %collective-permute-start.10) | collective-permute-done | bytes 1048608 | tf_op jit(solution)/shard_map/ppermute | solution.py:58
  311.2 16.3 %shard_map.149 = (f32[1024,768]{1,0:T(8,128)}, f32[1024,768]{1,0:T(8,128)}, bf16[1024,256]{1,0:T(8,128)(2,1)S(1)}, bf16[1024,256]{1,0:T(8,128)(2,1)S(1)}, bf16[1...) custom-call(s32[7]{0:T(128)S(1)} %pad_add_fusion.1.place, ...), custom_call_target="tpu_custom_call", output_to_operand_aliasing={{0}: (8, {}), {1}: (9, {})} | custom-call | flops 1048576 | bytes 65536 | tf_op jit(solution)/shard_map/pallas_call | solution.py:211
  344.9 4.8 %collective-permute-done.20 = bf16[512,256]{1,0:T(8,128)(2,1)S(1)} collective-permute-done((bf16[512,256]{1,0:T(8,128)(2,1)S(1)}, bf16[512,256]{1,0:T(8,128)(2,1)S(1)}, u32[]{:S(2)}, u32[]{:S(2)}) %collective-permute-start.20) | collective-permute-done | bytes 262176 | tf_op jit(solution)/shard_map/ppermute | solution.py:58
  349.9 5.4 %collective-permute-done.17 = bf16[1024,256]{1,0:T(8,128)(2,1)S(1)} collective-permute-done((bf16[1024,256]{1,0:T(8,128)(2,1)S(1)}, bf16[1024,256]{1,0:T(8,128)(2,1)S(1)}, u32[]{:S(2)}, u32[]{:S(2)}) %collective-permute-start.17) | collective-permute-done | bytes 524320 | tf_op jit(solution)/shard_map/ppermute | solution.py:58
  355.5 4.0 shard_map.150
  372.2 6.2 %collective-permute-done.26 = bf16[512,256]{1,0:T(8,128)(2,1)S(1)} collective-permute-done((bf16[512,256]{1,0:T(8,128)(2,1)S(1)}, bf16[512,256]{1,0:T(8,128)(2,1)S(1)}, u32[]{:S(2)}, u32[]{:S(2)}) %collective-permute-start.26) | collective-permute-done | bytes 262176 | tf_op jit(solution)/shard_map/ppermute | solution.py:58
  380.5 5.8 %collective-permute-done.22 = bf16[256,1536]{1,0:T(8,128)(2,1)S(1)} collective-permute-done((bf16[256,1536]{1,0:T(8,128)(2,1)S(1)}, bf16[256,1536]{1,0:T(8,128)(2,1)S(1)}, u32[]{:S(2)}, u32[]{:S(2)}) %collective-permute-start.22) | collective-permute-done | bytes 786464 | tf_op jit(solution)/shard_map/ppermute | solution.py:105
  400.5 4.7 %collective-permute-done.25 = bf16[256,768]{1,0:T(8,128)(2,1)S(1)} collective-permute-done((bf16[256,768]{1,0:T(8,128)(2,1)S(1)}, bf16[256,768]{1,0:T(8,128)(2,1)S(1)}, u32[]{:S(2)}, u32[]{:S(2)}) %collective-permute-start.25) | collective-permute-done | bytes 393248 | tf_op jit(solution)/shard_map/ppermute | solution.py:105
  407.2 16.8 %collective-permute-done.30 = bf16[256,1536]{1,0:T(8,128)(2,1)S(1)} collective-permute-done((bf16[256,1536]{1,0:T(8,128)(2,1)S(1)}, bf16[256,1536]{1,0:T(8,128)(2,1)S(1)}, u32[]{:S(2)}, u32[]{:S(2)}) %collective-permute-start.30) | collective-permute-done | bytes 786464 | tf_op jit(solution)/shard_map/ppermute | solution.py:105
  427.9 6.0 %collective-permute-done.32 = bf16[256,768]{1,0:T(8,128)(2,1)S(1)} collective-permute-done((bf16[256,768]{1,0:T(8,128)(2,1)S(1)}, bf16[256,768]{1,0:T(8,128)(2,1)S(1)}, u32[]{:S(2)}, u32[]{:S(2)}) %collective-permute-start.32) | collective-permute-done | bytes 393248 | tf_op jit(solution)/shard_map/ppermute | solution.py:105
  (172 shorter events, 109.5 us)
Async XLA Ops:
  7.2 76.4 %all-gather.4.cloned.1.call-start = ((), (), s32[]{:S(2)}) async-start(), calls=%async_computation.1 | async-start | bytes 9437184 | tf_op jit(solution)/shard_map/all_gather | solution.py:243
  7.9 216.0 %all-gather.6.cloned.1.call-start = ((), (), s32[]{:S(2)}) async-start(), calls=%async_computation.3 | async-start | bytes 14155776 | tf_op jit(solution)/shard_map/all_gather | solution.py:260
  8.0 40.6 %collective-permute-start.1 = (bf16[1024,768]{1,0:T(8,128)(2,1)}, bf16[1024,768]{1,0:T(8,128)(2,1)S(1)}, u32[]{:S(2)}, u32[]{:S(2)}) collective-permute-start(bf16[1024,768]{1,0:T(8,128)(2,1)} %param.12), channel_id=1, source_target_pairs={{0,24},{8,16},{16,8},{24,0},{1,25},{9,17},{17,9},{25,1},{2,26},{10... | collective-permute-start | bytes 4718600 | tf_op jit(solution)/shard_map/ppermute | solution.py:58
  13.1 68.5 %collective-permute-start = (bf16[1024,768]{1,0:T(8,128)(2,1)}, bf16[1024,768]{1,0:T(8,128)(2,1)}, u32[]{:S(2)}, u32[]{:S(2)}) collective-permute-start(bf16[1024,768]{1,0:T(8,128)(2,1)} %param.12), channel_id=1, source_target_pairs={{0,8},{8,0},{16,24},{24,16},{1,9},{9,1},{17,25},{25,17},{2,10},{10... | collective-permute-start | bytes 4718600 | tf_op jit(solution)/shard_map/ppermute | solution.py:58
  81.6 55.9 %collective-permute-start.5 = (bf16[1024,768]{1,0:T(8,128)(2,1)}, bf16[1024,768]{1,0:T(8,128)(2,1)}, u32[]{:S(2)}, u32[]{:S(2)}) collective-permute-start(bf16[1024,768]{1,0:T(8,128)(2,1)} %broadcast_select_fusion.3), channel_id=1, source_target_pairs={{0,16},{8,0},{16,24},{24,8},{1,17},{9,1},{17,25},{25,9},{2,18},{10... | collective-permute-start | bytes 4718600 | tf_op jit(solution)/shard_map/ppermute | solution.py:58
  93.8 41.3 %collective-permute-start.2 = (bf16[1536,256]{1,0:T(8,128)(2,1)}, bf16[1536,256]{1,0:T(8,128)(2,1)}, u32[]{:S(2)}, u32[]{:S(2)}) collective-permute-start(bf16[1536,256]{1,0:T(8,128)(2,1)} %get-tuple-element.68), channel_id=1, source_target_pairs={{0,8},{8,0},{16,24},{24,16},{1,9},{9,1},{17,25},{25,17},{2,10},{10... | collective-permute-start | bytes 2359304 | tf_op jit(solution)/shard_map/ppermute | solution.py:58
  143.2 187.4 %reduce-scatter.2.cloned.1.call-start = ((), (), s32[]{:S(2)}) async-start(), calls=%async_computation.2 | async-start | bytes 9437184 | tf_op jit(solution)/shard_map/reduce_scatter | solution.py:270
  143.3 18.9 %collective-permute-start.4 = (bf16[1536,256]{1,0:T(8,128)(2,1)}, bf16[1536,256]{1,0:T(8,128)(2,1)S(1)}, u32[]{:S(2)}, u32[]{:S(2)}) collective-permute-start(bf16[1536,256]{1,0:T(8,128)(2,1)} %get-tuple-element.70), channel_id=1, source_target_pairs={{0,8},{8,0},{16,24},{24,16},{1,9},{9,1},{17,25},{25,17},{2,10},{10... | collective-permute-start | bytes 2359304 | tf_op jit(solution)/shard_map/ppermute | solution.py:58
  144.4 40.2 %collective-permute-start.3 = (bf16[3072,256]{1,0:T(8,128)(2,1)S(1)}, bf16[3072,256]{1,0:T(8,128)(2,1)}, u32[]{:S(2)}, u32[]{:S(2)}) collective-permute-start(bf16[3072,256]{1,0:T(8,128)(2,1)S(1)} %maximum_select_fusion.3.near), channel_id=1, source_target_pairs={{8,16},{16,8},{9,17},{17,9},{10,18},{18,10},{11,19},{19,11},{12,20... | collective-permute-start | bytes 4718600 | tf_op jit(solution)/shard_map/ppermute | solution.py:58
  184.6 36.0 %collective-permute-start.7 = (bf16[3072,256]{1,0:T(8,128)(2,1)}, bf16[3072,256]{1,0:T(8,128)(2,1)}, u32[]{:S(2)}, u32[]{:S(2)}) collective-permute-start(bf16[3072,256]{1,0:T(8,128)(2,1)} %collective-permute-done.3.middle), channel_id=1, source_target_pairs={{8,0},{16,24},{9,1},{17,25},{10,2},{18,26},{11,3},{19,27},{12,4},{... | collective-permute-start | bytes 4718600 | tf_op jit(solution)/shard_map/ppermute | solution.py:58
  185.9 34.8 %collective-permute-start.8 = (bf16[3072,256]{1,0:T(8,128)(2,1)}, bf16[3072,256]{1,0:T(8,128)(2,1)}, u32[]{:S(2)}, u32[]{:S(2)}) collective-permute-start(bf16[3072,256]{1,0:T(8,128)(2,1)} %maximum_select_fusion.4.near), channel_id=1, source_target_pairs={{8,16},{16,8},{9,17},{17,9},{10,18},{18,10},{11,19},{19,11},{12,20... | collective-permute-start | bytes 4718600 | tf_op jit(solution)/shard_map/ppermute | solution.py:58
  220.6 37.3 %collective-permute-start.9 = (bf16[3072,256]{1,0:T(8,128)(2,1)}, bf16[3072,256]{1,0:T(8,128)(2,1)}, u32[]{:S(2)}, u32[]{:S(2)}) collective-permute-start(bf16[3072,256]{1,0:T(8,128)(2,1)} %collective-permute-done.8.middle), channel_id=1, source_target_pairs={{8,0},{16,24},{9,1},{17,25},{10,2},{18,26},{11,3},{19,27},{12,4},{... | collective-permute-start | bytes 4718600 | tf_op jit(solution)/shard_map/ppermute | solution.py:58
  221.9 36.0 %collective-permute-start.11 = (bf16[3072,256]{1,0:T(8,128)(2,1)}, bf16[3072,256]{1,0:T(8,128)(2,1)}, u32[]{:S(2)}, u32[]{:S(2)}) collective-permute-start(bf16[3072,256]{1,0:T(8,128)(2,1)} %maximum_select_fusion.5.near), channel_id=1, source_target_pairs={{8,16},{16,8},{9,17},{17,9},{10,18},{18,10},{11,19},{19,11},{12,20... | collective-permute-start | bytes 4718600 | tf_op jit(solution)/shard_map/ppermute | solution.py:58
  245.6 39.4 %collective-permute-start.13 = (bf16[2048,256]{1,0:T(8,128)(2,1)S(1)}, bf16[2048,256]{1,0:T(8,128)(2,1)S(1)}, u32[]{:S(2)}, u32[]{:S(2)}) collective-permute-start(bf16[2048,256]{1,0:T(8,128)(2,1)S(1)} %get-tuple-element.83), channel_id=1, source_target_pairs={{0,8},{24,16},{1,9},{25,17},{2,10},{26,18},{3,11},{27,19},{4,12},{... | collective-permute-start | bytes 3145736 | tf_op jit(solution)/shard_map/ppermute | solution.py:58
  258.0 44.4 %collective-permute-start.12 = (bf16[3072,256]{1,0:T(8,128)(2,1)}, bf16[3072,256]{1,0:T(8,128)(2,1)}, u32[]{:S(2)}, u32[]{:S(2)}) collective-permute-start(bf16[3072,256]{1,0:T(8,128)(2,1)} %collective-permute-done.11.middle), channel_id=1, source_target_pairs={{8,0},{16,24},{9,1},{17,25},{10,2},{18,26},{11,3},{19,27},{12,4},{... | collective-permute-start | bytes 4718600 | tf_op jit(solution)/shard_map/ppermute | solution.py:58
  276.2 26.1 %collective-permute-start.10 = (bf16[2048,256]{1,0:T(8,128)(2,1)}, bf16[2048,256]{1,0:T(8,128)(2,1)}, u32[]{:S(2)}, u32[]{:S(2)}) collective-permute-start(bf16[2048,256]{1,0:T(8,128)(2,1)} %get-tuple-element.87), channel_id=1, source_target_pairs={{0,8},{24,16},{1,9},{25,17},{2,10},{26,18},{3,11},{27,19},{4,12},{... | collective-permute-start | bytes 3145736 | tf_op jit(solution)/shard_map/ppermute | solution.py:58
  286.2 19.0 %collective-permute-start.14 = (bf16[2048,256]{1,0:T(8,128)(2,1)}, bf16[2048,256]{1,0:T(8,128)(2,1)}, u32[]{:S(2)}, u32[]{:S(2)}) collective-permute-start(bf16[2048,256]{1,0:T(8,128)(2,1)} %add_convert_fusion.4), channel_id=1, source_target_pairs={{8,16},{16,8},{9,17},{17,9},{10,18},{18,10},{11,19},{19,11},{12,20... | collective-permute-start | bytes 3145736 | tf_op jit(solution)/shard_map/ppermute | solution.py:58
  306.9 23.5 %collective-permute-start.15 = (bf16[1024,256]{1,0:T(8,128)(2,1)S(1)}, bf16[1024,256]{1,0:T(8,128)(2,1)S(1)}, u32[]{:S(2)}, u32[]{:S(2)}) collective-permute-start(bf16[1024,256]{1,0:T(8,128)(2,1)S(1)} %select_convert_fusion.1), channel_id=1, source_target_pairs={{0,8},{8,0},{16,24},{24,16},{1,9},{9,1},{17,25},{25,17},{2,10},{10... | collective-permute-start | bytes 1572872 | tf_op jit(solution)/shard_map/ppermute | solution.py:58
  309.5 29.8 %collective-permute-start.16 = (bf16[2048,256]{1,0:T(8,128)(2,1)}, bf16[2048,256]{1,0:T(8,128)(2,1)}, u32[]{:S(2)}, u32[]{:S(2)}) collective-permute-start(bf16[2048,256]{1,0:T(8,128)(2,1)} %add_convert_fusion.3), channel_id=1, source_target_pairs={{8,16},{16,8},{9,17},{17,9},{10,18},{18,10},{11,19},{19,11},{12,20... | collective-permute-start | bytes 3145736 | tf_op jit(solution)/shard_map/ppermute | solution.py:58
  329.2 20.5 %collective-permute-start.19 = (bf16[512,256]{1,0:T(8,128)(2,1)S(1)}, bf16[512,256]{1,0:T(8,128)(2,1)S(1)}, u32[]{:S(2)}, u32[]{:S(2)}) collective-permute-start(bf16[512,256]{1,0:T(8,128)(2,1)S(1)} %get-tuple-element.147), channel_id=1, source_target_pairs={{0,8},{8,0},{16,24},{24,16},{1,9},{9,1},{17,25},{25,17},{2,10},{10... | collective-permute-start | bytes 786440 | tf_op jit(solution)/shard_map/ppermute | solution.py:58
  366.7 19.6 %collective-permute-start.22 = (bf16[256,1536]{1,0:T(8,128)(2,1)S(1)}, bf16[256,1536]{1,0:T(8,128)(2,1)S(1)}, u32[]{:S(2)}, u32[]{:S(2)}) collective-permute-start(bf16[256,1536]{1,0:T(8,128)(2,1)S(1)} %pad_maximum_fusion.1), channel_id=1, source_target_pairs={{0,2},{1,3},{2,0},{3,1},{4,6},{5,7},{6,4},{7,5},{8,10},{9,11},{10,... | collective-permute-start | bytes 2359304 | tf_op jit(solution)/shard_map/ppermute | solution.py:105
  368.2 19.3 %collective-permute-start.23 = (bf16[256,1536]{1,0:T(8,128)(2,1)S(1)}, bf16[256,1536]{1,0:T(8,128)(2,1)S(1)}, u32[]{:S(2)}, u32[]{:S(2)}) collective-permute-start(bf16[256,1536]{1,0:T(8,128)(2,1)S(1)} %concatenate.80), channel_id=1, source_target_pairs={{0,4},{1,5},{2,6},{3,7},{4,0},{5,1},{6,2},{7,3},{8,12},{9,13},{10,... | collective-permute-start | bytes 2359304 | tf_op jit(solution)/shard_map/ppermute | solution.py:105
  369.6 19.6 %collective-permute-start.27 = (bf16[512,256]{1,0:T(8,128)(2,1)S(1)}, bf16[512,256]{1,0:T(8,128)(2,1)S(1)}, u32[]{:S(2)}, u32[]{:S(2)}) collective-permute-start(bf16[512,256]{1,0:T(8,128)(2,1)S(1)} %get-tuple-element.123), channel_id=1, source_target_pairs={{0,8},{8,0},{16,24},{24,16},{1,9},{9,1},{17,25},{25,17},{2,10},{10... | collective-permute-start | bytes 786440 | tf_op jit(solution)/shard_map/ppermute | solution.py:58
  405.2 18.9 %collective-permute-start.30 = (bf16[256,1536]{1,0:T(8,128)(2,1)S(1)}, bf16[256,1536]{1,0:T(8,128)(2,1)S(1)}, u32[]{:S(2)}, u32[]{:S(2)}) collective-permute-start(bf16[256,1536]{1,0:T(8,128)(2,1)S(1)} %pad_maximum_fusion.2), channel_id=1, source_target_pairs={{0,2},{1,3},{2,0},{3,1},{4,6},{5,7},{6,4},{7,5},{8,10},{9,11},{10,... | collective-permute-start | bytes 2359304 | tf_op jit(solution)/shard_map/ppermute | solution.py:105
  (42 other events, 529.6 us)
Sparse Core Ops, SparseCore 0:
  9.9 57.0 all-gather.3
  143.3 71.3 all-gather.5
  220.8 73.7 reduce-scatter.1
